TPU v7x, 32 devices: a whole 2x2x4 slice. The times are simulated.
32 devices in a mesh: groups: 2 (over y), rows: 4 (over z), cols: 4 (over x, core).
Axes of the slice: x: 2, y: 2, z: 4, core: 2. Of those that a mesh axis runs over, the one named last changes fastest.
Arguments:
- pair: float32 [512, 256, 128], P(('groups', 'rows'), 'cols'), parts along dimension 0, may hold values from -6 to 6
- pair_mask: int32 [512, 256], P(('groups', 'rows'), 'cols'), parts along dimension 0, may hold values 0 or 1
- in_gain: float32 [128], replicated, may hold values from 0.1 to 1.9
- in_bias: float32 [128], replicated, may hold values from -3 to 3
- proj_weight: bfloat16 [128, 512], replicated, may hold values from -0.5 to 0.5
- gate_weight: bfloat16 [128, 128], replicated, may hold values from -0.5 to 0.5
- out_gain: float32 [128], replicated, may hold values from 0.1 to 1.9
- out_bias: float32 [128], replicated, may hold values from -3 to 3
- out_weight: bfloat16 [128, 128], replicated, may hold values from -0.5 to 0.5
Outputs:
- update: float32 [512, 256, 128], P(('groups', 'rows'), 'cols'), parts along dimension 0
There are 2 independent parts, one for each index of `groups`. A program takes and returns all parts, laid end to end along the dimension named above; an argument that names none is the same for every part. Nothing has to cross between parts.
Inputs may be any that keep to these rules, and one draw needn't show every extreme that they name: `pair_mask`: 1 where a pair of residues takes part, else 0.
All inputs are finite; a program needn't handle non-finite values. No bound on the sum of `pair_mask` on one device may be relied on, other than what follows from the above.
Results may differ from a plain program's by a relative error of at most 0.0052.
Values may be sent and summed in bfloat16 or wider, within the bound.
No kernel may reach another device: no remote copies, remote signals or barrier semaphores. Data moves between devices by JAX's collectives and lax.ppermute only.
A program may use at most 64 MiB of HBM per device.

v0:
```python
import jax
import jax.numpy as jnp
from jax import lax
from jax.sharding import PartitionSpec as P


def layer_norm(values, gain, shift, axis):
    mean = jnp.mean(values, axis=axis, keepdims=True)
    centered = values - mean
    spread = jnp.mean(centered * centered, axis=axis, keepdims=True)
    return centered * lax.rsqrt(spread + 1e-05) * gain + shift


def gated_side(normed, weights, keep):
    channels = weights.shape[0]
    values = jnp.einsum("ikd,dc->cik", normed, weights, preferred_element_type=jnp.float32)
    gated = jax.nn.sigmoid(values[channels:]) * values[:channels] * keep
    return gated.astype(jnp.bfloat16)


def per_device(
    pair, pair_mask, in_gain, in_bias, proj_weight, gate_weight, out_gain, out_bias, out_weight
):
    channels = pair.shape[2]
    normed = layer_norm(pair, in_gain, in_bias, -1).astype(jnp.bfloat16)
    keep = pair_mask.astype(jnp.float32)[None]
    side_b = gated_side(normed, proj_weight[:, 2 * channels :], keep)
    moved_b = lax.all_to_all(side_b, "cols", split_axis=0, concat_axis=2, tiled=True)
    side_a = gated_side(normed, proj_weight[:, : 2 * channels], keep)
    moved_a = lax.all_to_all(side_a, "cols", split_axis=0, concat_axis=2, tiled=True)
    gating = jax.nn.sigmoid(
        jnp.einsum("ijd,do->ijo", normed, gate_weight, preferred_element_type=jnp.float32)
    )
    product = jnp.einsum(
        "cik,cjk->cij",
        moved_a,
        lax.all_gather(moved_b, "rows", axis=1, tiled=True),
        preferred_element_type=jnp.float32,
    ).astype(jnp.bfloat16)
    returned = lax.all_to_all(product, "cols", split_axis=2, concat_axis=0, tiled=True).astype(
        jnp.float32
    )
    normed_out = layer_norm(returned, out_gain[:, None, None], out_bias[:, None, None], 0).astype(
        jnp.bfloat16
    )
    update = (
        jnp.einsum("cij,co->ijo", normed_out, out_weight, preferred_element_type=jnp.float32)
        * gating
    )
    return update


def solution(mesh):
    return jax.shard_map(
        per_device,
        mesh=mesh,
        in_specs=(
            P(("groups", "rows"), "cols", None),
            P(("groups", "rows"), "cols"),
            P(),
            P(),
            P(),
            P(),
            P(),
            P(),
            P(),
        ),
        out_specs=P(("groups", "rows"), "cols", None),
        check_vma=False,
    )
```

profile of v0, /device:TPU:7, one launch (start us, length us, event | category | flops | bytes accessed | tf_op | source)
XLA Modules:
  0.0 184.5 jit_solution(18031997078388836100)
XLA Ops:
  6.6 2.3 %reduce_sum.36 = f32[64,64]{1,0:T(8,128)S(1)} reduce(f32[64,64,128]{2,1,0:T(8,128)} %param.9, f32[]{:T(128)} %constant.5.clone.1), dimensions={2}, to_apply=%region_0.0 | reduce | flops 520192 | bytes 2113540 | tf_op jit(solution)/shard_map/reduce_sum | solution.py:8
  13.1 2.2 %fusion.7 = (bf16[128,64,64]{0,2,1:T(8,128)(2,1)}, bf16[128,64,64]{0,2,1:T(8,128)(2,1)}) fusion(f32[256,64,64]{0,2,1:T(8,128)S(1)} %convolution_bitcast_fusion, f32[64,64]{1,0:T(8,128)S(1)} %convert_element_type.37, f32[256,64,64]{0,2,1:T(8,128)S(1)} %convolution_bitcast_fusion.1), kind=kLoop, calls=%fused_computation.13 | loop fusion | flops 6291456 | bytes 10502144 | tf_op jit(solution)/shard_map/convert_element_type | solution.py:18
  15.3 3.9 %copy.21 = bf16[128,64,64]{2,1,0:T(8,128)(2,1)S(1)} copy(bf16[128,64,64]{0,2,1:T(8,128)(2,1)} %get-tuple-element.5) | data formatting | bytes 2097152 | tf_op jit(solution)/shard_map/convert_element_type | solution.py:18
  19.2 2.7 %reshape.44 = bf16[4,2,65536]{2,1,0:T(2,128)(2,1)} reshape(bf16[128,64,64]{2,1,0:T(8,128)(2,1)S(1)} %copy.21) | data formatting | bytes 2097152
  21.9 17.7 %all_to_all.45 = bf16[4,2,65536]{2,1,0:T(2,128)(2,1)} all-to-all(bf16[4,2,65536]{2,1,0:T(2,128)(2,1)} %reshape.44), channel_id=1, replica_groups=mesh['groups'=2,'rows'=4,'cols'=4] {'cols'}, dimensions={0} | all-to-all | bytes 2097152 | tf_op jit(solution)/shard_map/all_to_all | solution.py:28
  39.6 3.1 %reshape.45 = bf16[128,64,64]{2,1,0:T(8,128)(2,1)S(1)} reshape(bf16[4,2,65536]{2,1,0:T(2,128)(2,1)} %all_to_all.45) | data formatting | bytes 2097152
  42.7 3.3 %copy.22 = bf16[32,64,4,64]{3,2,1,0:T(4,128)(2,1)} copy(bf16[32,64,4,64]{3,1,0,2:T(8,128)(2,1)S(1)} %bitcast.51) | data formatting | bytes 2097152 | tf_op jit(solution)/shard_map/all_to_all | solution.py:28
  45.9 4.3 %all_to_all.40 = bf16[32,64,256]{2,1,0:T(8,128)(2,1)} reshape(bf16[32,64,4,64]{3,2,1,0:T(4,128)(2,1)} %copy.22) | data formatting | bytes 2097152 | tf_op jit(solution)/shard_map/all_to_all | solution.py:28
  50.3 3.9 %copy.19 = bf16[128,64,64]{2,1,0:T(8,128)(2,1)S(1)} copy(bf16[128,64,64]{0,2,1:T(8,128)(2,1)} %get-tuple-element.6) | data formatting | bytes 2097152 | tf_op jit(solution)/shard_map/convert_element_type | solution.py:18
  54.2 2.7 %reshape.42 = bf16[4,2,65536]{2,1,0:T(2,128)(2,1)} reshape(bf16[128,64,64]{2,1,0:T(8,128)(2,1)S(1)} %copy.19) | data formatting | bytes 2097152
  56.9 18.7 %all_to_all.46 = bf16[4,2,65536]{2,1,0:T(2,128)(2,1)} all-to-all(bf16[4,2,65536]{2,1,0:T(2,128)(2,1)} %reshape.42), channel_id=1, replica_groups=mesh['groups'=2,'rows'=4,'cols'=4] {'cols'}, dimensions={0} | all-to-all | bytes 2097152 | tf_op jit(solution)/shard_map/all_to_all | solution.py:30
  75.6 3.1 %reshape.43 = bf16[128,64,64]{2,1,0:T(8,128)(2,1)S(1)} reshape(bf16[4,2,65536]{2,1,0:T(2,128)(2,1)} %all_to_all.46) | data formatting | bytes 2097152
  78.7 3.3 %copy.20 = bf16[32,64,4,64]{3,2,1,0:T(4,128)(2,1)} copy(bf16[32,64,4,64]{3,1,0,2:T(8,128)(2,1)S(1)} %bitcast.52) | data formatting | bytes 2097152 | tf_op jit(solution)/shard_map/all_to_all | solution.py:30
  82.0 3.5 %all_to_all.36 = bf16[32,64,256]{2,1,0:T(8,128)(2,1)S(1)} reshape(bf16[32,64,4,64]{3,2,1,0:T(4,128)(2,1)} %copy.20) | data formatting | bytes 2097152 | tf_op jit(solution)/shard_map/all_to_all | solution.py:30
  85.5 47.1 %all-gather.2.cloned.1.call-done = bf16[32,256,256]{2,1,0:T(8,128)(2,1)} async-done(((bf16[32,64,256]{2,1,0:T(8,128)(2,1)}), bf16[32,256,256]{2,1,0:T(8,128)(2,1)}) %all-gather.2.cloned.1.call-update) | async-done | bytes 4194320 | tf_op jit(solution)/shard_map/all_gather | solution.py:37
  132.5 4.5 %convolution_convert_fusion = bf16[32,64,256]{2,1,0:T(8,128)(2,1)} fusion(bf16[32,64,256]{2,1,0:T(8,128)(2,1)S(1)} %all_to_all.36, bf16[32,256,256]{2,1,0:T(8,128)(2,1)} %all-gather.2.cloned.1.call-done), kind=kOutput, calls=%fused_computation.30 | convolution fusion | flops 268959744 | bytes 6291456 | tf_op jit(solution)/shard_map/cik,cjk->cij/dot_general | solution.py:34
  137.1 3.9 %copy.23 = bf16[32,64,256]{1,0,2:T(8,128)(2,1)S(1)} copy(bf16[32,64,256]{2,1,0:T(8,128)(2,1)} %convolution_convert_fusion) | data formatting | bytes 2097152 | tf_op jit(solution)/shard_map/convert_element_type | solution.py:39
  141.0 2.6 %reshape.46 = bf16[4,2,65536]{2,1,0:T(2,128)(2,1)} reshape(bf16[256,32,64]{2,1,0:T(8,128)(2,1)S(1)} %bitcast.50) | data formatting | bytes 2097152
  143.6 5.1 %all-to-all-start.2 = ((bf16[4,2,65536]{2,1,0:T(2,128)(2,1)}), bf16[4,2,65536]{2,1,0:T(2,128)(2,1)}, u32[]{:S(2)}, u32[]{:S(2)}) async-start(bf16[4,2,65536]{2,1,0:T(2,128)(2,1)} %reshape.46), calls=%async_computation.2 | async-start | bytes 2097152 | tf_op jit(solution)/shard_map/all_to_all | solution.py:40
  150.4 10.8 %all-to-all-done.2 = bf16[4,2,65536]{2,1,0:T(2,128)(2,1)} async-done(((bf16[4,2,65536]{2,1,0:T(2,128)(2,1)}), bf16[4,2,65536]{2,1,0:T(2,128)(2,1)}, u32[]{:S(2)}, u32[]{:S(2)}) %all-to-all-start.2) | async-done | bytes 1048608 | tf_op jit(solution)/shard_map/all_to_all | solution.py:40
  161.2 3.1 %reshape.47 = bf16[256,32,64]{2,1,0:T(8,128)(2,1)S(1)} reshape(bf16[4,2,65536]{2,1,0:T(2,128)(2,1)} %all-to-all-done.2) | data formatting | bytes 2097152
  164.3 3.8 %copy.24 = f32[32,64,4,64]{3,1,0,2:T(8,128)} copy(bf16[32,64,4,64]{1,0,3,2:T(8,128)(2,1)S(1)} %bitcast.49) | data formatting | bytes 3145728 | tf_op jit(solution)/shard_map/convert_element_type | solution.py:40
  168.1 2.7 %bitcast_reduce_fusion = f32[64,64]{1,0:T(8,128)S(1)} fusion(f32[32,64,4,64]{3,1,0,2:T(8,128)} %copy.24), kind=kLoop, calls=%fused_computation.5 | loop fusion | flops 520192 | bytes 2113536 | tf_op jit(solution)/shard_map/reduce_sum | solution.py:8
  173.8 3.9 %divide_multiply_fusion = f32[64,64,128]{2,1,0:T(8,128)} fusion(f32[64,64,128]{2,1,0:T(8,128)S(1)} %copy-done.3, bf16[128,64,64]{2,1,0:T(8,128)(2,1)S(1)} %fusion.3, bf16[128,128]{1,0:T(8,128)(2,1)S(1)} %copy-done.10), kind=kOutput, calls=%fused_computation.27 | convolution fusion | flops 136314880 | bytes 5275648 | tf_op jit(solution)/shard_map/cij,co->ijo/dot_general | solution.py:47
  (36 shorter events, 8.9 us)
Async XLA Ops:
  6.5 142.2 %copy-start = (bf16[128,128]{1,0:T(8,128)(2,1)S(1)}, bf16[128,128]{1,0:T(8,128)(2,1)}, u32[]{:S(2)}) copy-start(bf16[128,128]{1,0:T(8,128)(2,1)} %param.14) | copy-start | bytes 98308
  6.5 2.4 %copy-start.2 = (f32[64,64,128]{2,1,0:T(8,128)S(1)}, f32[64,64,128]{2,1,0:T(8,128)}, u32[]{:S(2)}) copy-start(f32[64,64,128]{2,1,0:T(8,128)} %param.9) | copy-start | bytes 6291460
  6.5 3.8 %copy-start.7 = (f32[128]{0:T(128)S(1)}, f32[128]{0:T(128)}, u32[]{:S(2)}) copy-start(f32[128]{0:T(128)} %param.11) | copy-start | bytes 1540
  6.5 3.8 %copy-start.6 = (f32[128]{0:T(128)S(1)}, f32[128]{0:T(128)}, u32[]{:S(2)}) copy-start(f32[128]{0:T(128)} %param.12) | copy-start | bytes 1540
  6.5 126.0 %all-gather.2.cloned.1.call-start = ((), (), s32[]{:S(2)}) async-start(), calls=%async_computation.3 | async-start | bytes 5242880 | tf_op jit(solution)/shard_map/all_gather | solution.py:37
  10.3 1.3 copy-start.4
  12.3 0.8 copy-start.5
  143.6 17.6 %all-to-all-start.2 = ((bf16[4,2,65536]{2,1,0:T(2,128)(2,1)}), bf16[4,2,65536]{2,1,0:T(2,128)(2,1)}, u32[]{:S(2)}, u32[]{:S(2)}) async-start(bf16[4,2,65536]{2,1,0:T(2,128)(2,1)} %reshape.46), calls=%async_computation.2 | async-start | bytes 2097152 | tf_op jit(solution)/shard_map/all_to_all | solution.py:40
  168.1 3.4 %copy-start.1 = (f32[32,64,4,64]{3,1,0,2:T(8,128)S(1)}, f32[32,64,4,64]{3,1,0,2:T(8,128)}, u32[]{:S(2)}) copy-start(f32[32,64,4,64]{3,1,0,2:T(8,128)} %copy.24) | copy-start | bytes 6291460
  171.5 0.7 copy-start.8
  171.5 0.7 copy-start.9
  172.2 1.6 copy-start.3
  172.2 1.6 copy-start.10
Sparse Core Ops, SparseCore 0:
  50.4 82.0 all-gather.1
where the time goes:
time: 188 us; the launch traced here: 185 us
  waiting for transfers between devices  57.9 us (31%)
  local copies, waits for them, and re-layouts  48.9 us (26%)
  blocking collectives  36.4 us (19%)
  between operations  13.6 us (7%)
  matrix products  11.5 us (6%)
  other arithmetic  11.2 us (6%)
  starting transfers between devices  5.09 us (3%)
    all_gather x1, waiting for transfers between devices, per_device(): lax.all_gather(moved_b, 'rows', axis=1, tiled=True)  47.1 us
    unnamed x28, local copies, waits for them, and re-layouts  19 us
    all_to_all x1, blocking collectives, per_device(): lax.all_to_all(side_a, 'cols', split_axis=0, concat_axis=2, tiled=True)  18.7 us
    all_to_all x1, blocking collectives, per_device(): lax.all_to_all(side_b, 'cols', split_axis=0, concat_axis=2, tiled=True)  17.7 us
    all_to_all x1, waiting for transfers between devices, per_device(): lax.all_to_all(product, 'cols', split_axis=2, concat_axis=0, tiled=True)  10.8 us
    convert_element_type x2, local copies, waits for them, and re-layouts, gated_side(): return gated.astype(jnp.bfloat16)  7.87 us
    all_to_all x2, local copies, waits for them, and re-layouts, per_device(): lax.all_to_all(side_b, 'cols', split_axis=0, concat_axis=2, tiled=True)  7.59 us
    all_to_all x2, local copies, waits for them, and re-layouts, per_device(): lax.all_to_all(side_a, 'cols', split_axis=0, concat_axis=2, tiled=True)  6.76 us
  transfers between devices with their start and end apart: 2, of which 2 were waited for; matrix products, arithmetic and copies ran while one was open for 8% of the time, Pallas kernels for 0%

commit v1 on v0

v1 whole, which is shorter than its diff:
```python
import functools

import jax
import jax.numpy as jnp
from jax import lax
from jax.experimental import pallas as pl
from jax.experimental.pallas import tpu as pltpu
from jax.sharding import PartitionSpec as P

EPS = 1e-05
VMEM = pl.BlockSpec(memory_space=pltpu.VMEM)
LIMIT = 48 * 1024 * 1024


def call(body, out_shape, grid, in_specs, out_specs, scratch, flops, moved):
    return pl.pallas_call(
        body,
        out_shape=out_shape,
        grid=grid,
        in_specs=in_specs,
        out_specs=out_specs,
        scratch_shapes=scratch,
        compiler_params=pltpu.CompilerParams(vmem_limit_bytes=LIMIT),
        cost_estimate=pl.CostEstimate(flops=flops, bytes_accessed=moved, transcendentals=0),
    )


def sigmoid(values):
    return 0.5 * jnp.tanh(0.5 * values) + 0.5


def dot(left, right, dims):
    return lax.dot_general(left, right, (dims, ((), ())), preferred_element_type=jnp.float32)


def normalise(values, gain, shift):
    mean = jnp.mean(values, axis=-1, keepdims=True)
    centered = values - mean
    spread = jnp.mean(centered * centered, axis=-1, keepdims=True)
    return centered * lax.rsqrt(spread + EPS) * gain + shift


def norm_body(pair_ref, mask_ref, gain_ref, shift_ref, out_ref):
    keep = mask_ref[...].astype(jnp.float32).T
    gain, shift = gain_ref[...], shift_ref[...]
    for row in range(pair_ref.shape[0]):
        normed = normalise(pair_ref[row], gain, shift)
        out_ref[row] = (normed * keep[:, row : row + 1]).astype(jnp.bfloat16)


def masked_norm(pair, mask, gain, shift, step=16):
    rows, cols, channels = pair.shape
    return call(
        norm_body,
        jax.ShapeDtypeStruct(pair.shape, jnp.bfloat16),
        (rows // step,),
        [
            pl.BlockSpec((step, cols, channels), lambda g: (g, 0, 0)),
            pl.BlockSpec((step, cols), lambda g: (g, 0)),
            VMEM,
            VMEM,
        ],
        pl.BlockSpec((step, cols, channels), lambda g: (g, 0, 0)),
        [],
        10 * pair.size,
        6 * pair.size,
    )(pair, mask, gain, shift)


def gate_body(pair_ref, gain_ref, shift_ref, weight_ref, out_ref):
    rows, cols, channels = pair_ref.shape
    normed = normalise(pair_ref[...].reshape(rows * cols, channels), gain_ref[...], shift_ref[...])
    values = dot(normed.astype(jnp.bfloat16), weight_ref[...], ((1,), (0,)))
    out_ref[...] = sigmoid(values).reshape(rows, cols, channels)


def output_gate(pair, gain, shift, weight, step=8):
    rows, cols, channels = pair.shape
    return call(
        gate_body,
        jax.ShapeDtypeStruct(pair.shape, jnp.float32),
        (rows // step,),
        [pl.BlockSpec((step, cols, channels), lambda g: (g, 0, 0)), VMEM, VMEM, VMEM],
        pl.BlockSpec((step, cols, channels), lambda g: (g, 0, 0)),
        [],
        2 * pair.size * channels,
        8 * pair.size,
    )(pair, gain, shift, weight)


def side_body(own_ref, other_ref, weight_ref, out_ref, held):
    step, cols, _ = own_ref.shape
    half = out_ref.shape[0]
    weight = weight_ref[...]
    for row in range(step):
        normed = jnp.concatenate([own_ref[row], other_ref[row]], axis=0)
        values = dot(weight, normed, ((1,), (1,)))
        held[pl.ds(row, half, stride=step), :] = sigmoid(values[half:]) * values[:half]
    out_ref[...] = held[...].reshape(half, step, 2 * cols).astype(jnp.bfloat16)


def side(own, other, weight, step=16):
    rows, cols, channels = own.shape
    half = weight.shape[0] // 2
    block = pl.BlockSpec((step, cols, channels), lambda g: (g, 0, 0))
    return call(
        side_body,
        jax.ShapeDtypeStruct((half, rows, 2 * cols), jnp.bfloat16),
        (rows // step,),
        [block, block, VMEM],
        pl.BlockSpec((half, step, 2 * cols), lambda g: (0, g, 0)),
        [pltpu.VMEM((half * step, 2 * cols), jnp.float32)],
        8 * rows * cols * channels * half,
        4 * own.size + 4 * rows * cols * half,
    )(own, other, weight)


def triangle_body(first_ref, second_ref, out_ref):
    rows, deep = second_ref.shape[2:]
    zero = jnp.zeros((rows, deep), jnp.bfloat16)
    for at in range(out_ref.shape[0]):
        left = jnp.concatenate([first_ref[0, at], first_ref[1, at]], axis=1)
        right = jnp.concatenate(
            [
                jnp.concatenate([second_ref[0, at], zero], axis=1),
                jnp.concatenate([zero, second_ref[1, at]], axis=1),
            ],
            axis=0,
        )
        out_ref[at] = dot(left, right, ((1,), (1,))).astype(jnp.bfloat16)


def triangle(first, second, step=16):
    half, rows, deep = first.shape
    pairs = half // 2
    step = min(step, pairs)
    block = pl.BlockSpec((2, step, rows, deep), lambda g: (0, g, 0, 0))
    return call(
        triangle_body,
        jax.ShapeDtypeStruct((pairs, rows, 2 * rows), jnp.bfloat16),
        (pairs // step,),
        [block, block],
        pl.BlockSpec((step, rows, 2 * rows), lambda g: (g, 0, 0)),
        [],
        4 * half * rows * rows * deep,
        6 * first.size,
    )(first.reshape(2, pairs, rows, deep), second.reshape(2, pairs, rows, deep))


def finish_body(counts, *refs):
    flag_ref, parts, rest = refs[0], refs[1 : 1 + 2 * sum(counts)], refs[1 + 2 * sum(counts) :]
    gain_ref, shift_ref, weight_ref, gate_ref, out_ref, held = rest
    pairs, step, lanes = parts[0].shape
    width = lanes // 2
    early = flag_ref[0] == 1
    chunks = []
    at = 0
    for count in counts:
        total = None
        for _ in range(count):
            term = jnp.where(early, parts[at][...], parts[at + 1][...]).astype(jnp.float32)
            total = term if total is None else total + term
            at += 2
        chunks.append(total)
    total = jnp.concatenate(chunks, axis=0)
    planes = 2 * pairs

    def mean(values):
        added = jnp.sum(values, axis=0)
        return (added + pltpu.roll(added, width, 1)) * (1.0 / (2 * planes))

    centered = total - mean(total)[None]
    scale = lax.rsqrt(mean(centered * centered) + EPS)[None]
    normed = centered * scale * gain_ref[...] + shift_ref[...]
    for plane in range(planes):
        held[pl.ds(plane, step, stride=planes), :] = normed[plane]
    weight = weight_ref[...]
    for row in range(step):
        tile = held[row * planes : (row + 1) * planes, :].T.astype(jnp.bfloat16)
        update = dot(tile[:width], weight[:planes], ((1,), (0,)))
        update += dot(tile[width:], weight[planes:], ((1,), (0,)))
        out_ref[row] = update * gate_ref[row]


def finish(flag, halves, gain, shift, weight, gate, step=8):
    rows, cols, channels = gate.shape
    parts = [array for half in halves for pair in half for array in pair]
    pairs, _, lanes = parts[0].shape
    block = pl.BlockSpec((pairs, step, lanes), lambda g: (0, g, 0))
    tile = pl.BlockSpec((step, cols, channels), lambda g: (g, 0, 0))
    return call(
        functools.partial(finish_body, [len(half) for half in halves]),
        jax.ShapeDtypeStruct(gate.shape, jnp.float32),
        (rows // step,),
        [pl.BlockSpec(memory_space=pltpu.SMEM)] + [block] * len(parts) + [VMEM, VMEM, VMEM, tile],
        tile,
        [pltpu.VMEM((2 * pairs * step, lanes), jnp.float32)],
        2 * gate.size * channels,
        8 * gate.size,
    )(flag, *parts, gain, shift, weight, gate)


def planes_of(vector, width):
    pairs = vector.shape[0] // 4
    ordered = vector.reshape(2, 2, pairs).transpose(0, 2, 1).reshape(2 * pairs, 2)
    return jnp.repeat(ordered, width, axis=1)[:, None, :]


def per_device(
    mesh_rows,
    mesh_cols,
    pair,
    pair_mask,
    in_gain,
    in_bias,
    proj_weight,
    gate_weight,
    out_gain,
    out_bias,
    out_weight,
):
    rows, cols, channels = pair.shape
    half = channels // 2
    row, col = lax.axis_index("rows"), lax.axis_index("cols")
    core = col % 2
    both = ("rows", "cols")
    flip = [(at, at ^ 1) for at in range(mesh_cols)]

    weights = proj_weight.reshape(channels, 4, 2, half)
    weights = jnp.where(core == 0, weights[:, :, 0], weights[:, :, 1])
    weights = weights.transpose(1, 2, 0).reshape(2, 2 * half, channels)
    swap = lambda array: jnp.where(core == 0, array, jnp.roll(array, half, axis=0))
    last_gain, last_shift = planes_of(swap(out_gain), cols), planes_of(swap(out_bias), cols)
    last_weight = swap(out_weight).reshape(2, 2, half // 2, channels).transpose(1, 0, 2, 3)
    last_weight = last_weight.reshape(channels, channels)
    gain, shift = in_gain[None], in_bias[None]

    own = masked_norm(pair, pair_mask, gain, shift)
    other = lax.ppermute(own, "cols", flip)
    side_b = side(own, other, weights[1])

    if mesh_rows == 4 and mesh_cols == 4:
        swap_ends = [(0, 1), (1, 0), (2, 3), (3, 2)]
        swap_mid = [(1, 2), (2, 1)]
        to_ends = [(1, 0), (2, 3)]
        near_mid = lax.ppermute(side_b, "rows", swap_mid)
        partner = lax.ppermute(side_b, "rows", swap_ends)
        side_a = side(own, other, weights[0])
        gate = output_gate(pair, gain, shift, gate_weight)
        far_mid = lax.ppermute(partner, "rows", swap_mid)
        near_end = lax.ppermute(near_mid, "rows", to_ends)
        far_end = lax.ppermute(far_mid, "rows", to_ends)
        middle = (row == 1) | (row == 2)
        near = jnp.where(middle, near_mid, near_end)
        far = jnp.where(middle, far_mid, far_end)

        def spread(blocks, target):
            same = jnp.where(core == 0, blocks[0], blocks[1])
            cross = jnp.where(core == 0, blocks[1], blocks[0])
            at = lambda z, x, h: z * 4 + 2 * x + h
            places = [(z, h) for z in range(4) for h in range(2)]
            straight = [(at(z, 1 - target(z), h), at(z, target(z), h)) for z, h in places]
            diagonal = [(at(z, 1 - target(z), h), at(z, target(z), 1 - h)) for z, h in places]
            beside = [(at(z, target(z), h), at(z, target(z), 1 - h)) for z, h in places]
            return (
                same,
                lax.ppermute(same, both, straight),
                lax.ppermute(cross, both, beside),
                lax.ppermute(cross, both, diagonal),
            )

        product_own, product_partner = triangle(side_a, side_b), triangle(side_a, partner)
        even = row % 2 == 0
        early = spread(
            (
                jnp.where(even, product_own, product_partner),
                jnp.where(even, product_partner, product_own),
            ),
            lambda z: z // 2,
        )
        product_near, product_far = triangle(side_a, near), triangle(side_a, far)
        low = row < 2
        late = spread(
            (
                jnp.where(low, product_near, product_far),
                jnp.where(low, product_far, product_near),
            ),
            lambda z: 1 - z // 2,
        )
        flag = (col // 2 == row // 2).astype(jnp.int32)[None]
        halves = [
            [(early[0], late[0]), (early[1], late[1])],
            [(early[2], late[2]), (early[3], late[3])],
        ]
    else:
        side_a = side(own, other, weights[0])
        gate = output_gate(pair, gain, shift, gate_weight)
        gathered = lax.all_gather(side_b, "rows")
        products = jnp.stack([triangle(side_a, gathered[at]) for at in range(mesh_rows)])
        parts = lax.all_to_all(products, "cols", 0, 0, tiled=True).astype(jnp.float32)
        parts = jnp.sum(parts.reshape(mesh_cols // 2, 2, *parts.shape[1:]), axis=0)
        mine = jnp.where(core == 0, parts[0], parts[1])
        others = jnp.where(core == 0, parts[1], parts[0])
        flag = jnp.ones((1,), jnp.int32)
        halves = [[(mine, mine)], [(others, others)]]
    return finish(flag, halves, last_gain, last_shift, last_weight, gate)


def solution(mesh):
    tile = P(("groups", "rows"), "cols", None)
    return jax.shard_map(
        functools.partial(per_device, mesh.shape["rows"], mesh.shape["cols"]),
        mesh=mesh,
        in_specs=(tile, P(("groups", "rows"), "cols")) + (P(),) * 7,
        out_specs=tile,
        check_vma=False,
    )
```

time: 188 us -> 133 us (0.71)
  local copies, waits for them, and re-layouts: 48.9 us -> 6.96 us
  blocking collectives: 36.4 us -> 0 us
  Pallas kernels: 0 us -> 30.6 us
  starting transfers between devices: 5.09 us -> 22.5 us
  between operations: 13.6 us -> 0.38 us
  matrix products: 11.5 us -> 0 us
  waiting for transfers between devices: 57.9 us -> 67.5 us
  other arithmetic: 11.2 us -> 3.34 us
    ppermute x0 -> x12, waiting for transfers between devices: none -> 67.5 us  [the longest x1 21.5 us: per_device(): partner = lax.ppermute(side_b, 'rows', swap_ends)]
    all_gather x1 -> x0, waiting for transfers between devices: 47.1 us -> none  [per_device(): lax.all_gather(moved_b, 'rows', axis=1, tiled=True)]
    all_to_all x2 -> x0, blocking collectives: 36.4 us -> none  [the longest x1 18.7 us: per_device(): lax.all_to_all(side_a, 'cols', split_axis=0, concat_axis=2, tiled=True)]
    pallas_call x0 -> x9, Pallas kernels: none -> 30.6 us  [the longest x1 9.46 us: finish(): call(functools.partial(finish_body, [len(half) for half in halves]), jax....]
    ppermute x0 -> x12, starting transfers between devices: none -> 22.5 us  [the longest x2 6.09 us: spread(): lax.ppermute(cross, both, beside)]
    convert_element_type x4 -> x0, local copies, waits for them, and re-layouts: 15.5 us -> none  [the longest x2 7.87 us: gated_side(): return gated.astype(jnp.bfloat16)]
    all_to_all x4 -> x0, local copies, waits for them, and re-layouts: 14.4 us -> none  [the longest x2 7.59 us: per_device(): lax.all_to_all(side_b, 'cols', split_axis=0, concat_axis=2, tiled=True)]
    unnamed x28 -> x31, local copies, waits for them, and re-layouts: 19 us -> 5.97 us
  transfers between devices with their start and end apart: 2 -> 12, of which waited for: 2 -> 6; matrix products, arithmetic and copies ran while one was open for 8% -> 3% of each run, Pallas kernels for 0% -> 8%
where the time goes in v1:
time: 133 us; the launch traced here: 131 us
  waiting for transfers between devices  67.5 us (51%)
  Pallas kernels  30.6 us (23%)
  starting transfers between devices  22.5 us (17%)
  local copies, waits for them, and re-layouts  6.96 us (5%)
  other arithmetic  3.34 us (3%)
    ppermute x1, waiting for transfers between devices, per_device(): partner = lax.ppermute(side_b, 'rows', swap_ends)  21.5 us
    ppermute x1, waiting for transfers between devices, per_device(): far_end = lax.ppermute(far_mid, 'rows', to_ends)  19.3 us
    ppermute x2, waiting for transfers between devices, spread(): lax.ppermute(same, both, straight)  12.5 us
    ppermute x1, waiting for transfers between devices, per_device(): near_end = lax.ppermute(near_mid, 'rows', to_ends)  9.83 us
    pallas_call x1, Pallas kernels, finish(): call(functools.partial(finish_body, [len(half) for half in halves]), jax....  9.46 us
    pallas_call x1, Pallas kernels, masked_norm(): call(norm_body, jax.ShapeDtypeStruct(pair.shape, jnp.bfloat16), (rows //...  7.98 us
    ppermute x2, starting transfers between devices, spread(): lax.ppermute(cross, both, beside)  6.09 us
    unnamed x31, local copies, waits for them, and re-layouts  5.97 us
  transfers between devices with their start and end apart: 12, of which 6 were waited for; matrix products, arithmetic and copies ran while one was open for 3% of the time, Pallas kernels for 8%

profile of v1, /device:TPU:7, one launch (start us, length us, event | category | flops | bytes accessed | tf_op | source)
XLA Modules:
  0.0 131.3 jit_solution(4445107960522385987)
XLA Ops:
  0.0 1.6 %copy-done = f32[64,64,128]{2,1,0:T(8,128)S(1)} copy-done((f32[64,64,128]{2,1,0:T(8,128)S(1)}, f32[64,64,128]{2,1,0:T(8,128)}, u32[]{:S(2)}) %copy-start) | copy-done | bytes 2097176
  3.7 8.0 %shard_map.91.own_ref = bf16[64,64,128]{2,1,0:T(8,128)(2,1)S(1)} custom-call(f32[64,64,128]{2,1,0:T(8,128)S(1)} %copy-done, s32[64,64]{1,0:T(8,128)S(1)} %copy-done.5, f32[1,128]{1,0:T(1,128)S(1)} %bitcast.33, f32[1,128]{1,0:T(1,128)S(1)} %bitcast.35), custom_call_target="tpu_custom_call" | custom-call | flops 5242880 | bytes 3145728 | tf_op jit(solution)/shard_map/pallas_call | solution.py:53
  12.6 2.1 %collective-permute-done.other_ref = bf16[64,64,128]{2,1,0:T(8,128)(2,1)S(1)} collective-permute-done((bf16[64,64,128]{2,1,0:T(8,128)(2,1)S(1)}, bf16[64,64,128]{2,1,0:T(8,128)(2,1)S(1)}, u32[]{:S(2)}, u32[]{:S(2)}) %collective-permute-start) | collective-permute-done | bytes 1048608 | tf_op jit(solution)/shard_map/ppermute | solution.py:239
  14.7 2.3 %shard_map.93 = bf16[64,64,128]{2,1,0:T(8,128)(2,1)S(1)} custom-call(bf16[64,64,128]{2,1,0:T(8,128)(2,1)S(1)} %shard_map.91.own_ref, bf16[64,64,128]{2,1,0:T(8,128)(2,1)S(1)} %collective-permute-done.other_ref, bf16[128,128]{1,0:T(8,128)(2,1)S(1)} %bitcast.32), custom_call_target="tpu_custom_call" | custom-call | flops 268435456 | bytes 3145728 | tf_op jit(solution)/shard_map/pallas_call | solution.py:106
  17.0 1.4 %collective-permute-start.1 = (bf16[64,64,128]{2,1,0:T(8,128)(2,1)S(1)}, bf16[64,64,128]{2,1,0:T(8,128)(2,1)}, u32[]{:S(2)}, u32[]{:S(2)}) collective-permute-start(bf16[64,64,128]{2,1,0:T(8,128)(2,1)S(1)} %shard_map.93), channel_id=1, source_target_pairs={{0,4},{4,0},{8,12},{12,8},{1,5},{5,1},{9,13},{13,9},{2,6},{6,2},{1... | collective-permute-start | bytes 3145736 | tf_op jit(solution)/shard_map/ppermute | solution.py:247
  18.4 1.6 %collective-permute-start.2 = (bf16[64,64,128]{2,1,0:T(8,128)(2,1)S(1)}, bf16[64,64,128]{2,1,0:T(8,128)(2,1)}, u32[]{:S(2)}, u32[]{:S(2)}) collective-permute-start(bf16[64,64,128]{2,1,0:T(8,128)(2,1)S(1)} %shard_map.93), channel_id=1, source_target_pairs={{4,8},{8,4},{5,9},{9,5},{6,10},{10,6},{7,11},{11,7},{20,24},{24,20... | collective-permute-start | bytes 3145736 | tf_op jit(solution)/shard_map/ppermute | solution.py:246
  20.0 21.5 %collective-permute-done.1 = bf16[64,64,128]{2,1,0:T(8,128)(2,1)} collective-permute-done((bf16[64,64,128]{2,1,0:T(8,128)(2,1)S(1)}, bf16[64,64,128]{2,1,0:T(8,128)(2,1)}, u32[]{:S(2)}, u32[]{:S(2)}) %collective-permute-start.1) | collective-permute-done | bytes 1048608 | tf_op jit(solution)/shard_map/ppermute | solution.py:247
  41.6 1.6 %collective-permute-start.4 = (bf16[64,64,128]{2,1,0:T(8,128)(2,1)}, bf16[64,64,128]{2,1,0:T(8,128)(2,1)}, u32[]{:S(2)}, u32[]{:S(2)}) collective-permute-start(bf16[64,64,128]{2,1,0:T(8,128)(2,1)} %collective-permute-done.1), channel_id=1, source_target_pairs={{4,8},{8,4},{5,9},{9,5},{6,10},{10,6},{7,11},{11,7},{20,24},{24,20... | collective-permute-start | bytes 3145736 | tf_op jit(solution)/shard_map/ppermute | solution.py:250
  43.2 1.3 collective-permute-start.3
  44.5 1.3 collective-permute-start.5
  46.0 2.3 %shard_map.92 = bf16[64,64,128]{2,1,0:T(8,128)(2,1)S(1)} custom-call(bf16[64,64,128]{2,1,0:T(8,128)(2,1)S(1)} %shard_map.91.own_ref, bf16[64,64,128]{2,1,0:T(8,128)(2,1)S(1)} %collective-permute-done.other_ref, bf16[128,128]{1,0:T(8,128)(2,1)S(1)} %bitcast.31), custom_call_target="tpu_custom_call" | custom-call | flops 268435456 | bytes 3145728 | tf_op jit(solution)/shard_map/pallas_call | solution.py:106
  49.5 2.1 %shard_map.95 = bf16[32,64,128]{2,1,0:T(8,128)(2,1)S(1)} custom-call(bf16[2,32,64,128]{3,2,1,0:T(8,128)(2,1)S(1)} %bitcast.24, bf16[2,32,64,128]{3,2,1,0:T(8,128)(2,1)} %bitcast.11.second_ref), custom_call_target="tpu_custom_call" | custom-call | flops 134217728 | bytes 3145728 | tf_op jit(solution)/shard_map/pallas_call | solution.py:138
  52.5 3.3 %collective-permute-start.10 = (bf16[32,64,128]{2,1,0:T(8,128)(2,1)}, bf16[32,64,128]{2,1,0:T(8,128)(2,1)S(1)}, u32[]{:S(2)}, u32[]{:S(2)}) collective-permute-start(bf16[32,64,128]{2,1,0:T(8,128)(2,1)} %get-tuple-element.7), channel_id=1, source_target_pairs={{2,1},{3,0},{6,5},{7,4},{8,11},{9,10},{12,15},{13,14},{18,17},{19,... | collective-permute-start | bytes 1572872 | tf_op jit(solution)/shard_map/ppermute | solution.py:269
  55.7 1.5 %collective-permute-start.8 = (bf16[32,64,128]{2,1,0:T(8,128)(2,1)}, bf16[32,64,128]{2,1,0:T(8,128)(2,1)}, u32[]{:S(2)}, u32[]{:S(2)}) collective-permute-start(bf16[32,64,128]{2,1,0:T(8,128)(2,1)} %get-tuple-element.7), channel_id=1, source_target_pairs={{0,1},{1,0},{4,5},{5,4},{10,11},{11,10},{14,15},{15,14},{16,17},{1... | collective-permute-start | bytes 1572872 | tf_op jit(solution)/shard_map/ppermute | solution.py:268
  57.2 2.6 %collective-permute-start.6 = (bf16[32,64,128]{2,1,0:T(8,128)(2,1)S(1)}, bf16[32,64,128]{2,1,0:T(8,128)(2,1)}, u32[]{:S(2)}, u32[]{:S(2)}) collective-permute-start(bf16[32,64,128]{2,1,0:T(8,128)(2,1)S(1)} %get-tuple-element.8.refs_1_), channel_id=1, source_target_pairs={{2,0},{3,1},{6,4},{7,5},{8,10},{9,11},{12,14},{13,15},{18,16},{19,... | collective-permute-start | bytes 1572872 | tf_op jit(solution)/shard_map/ppermute | solution.py:267
  59.8 9.8 %collective-permute-done.3 = bf16[64,64,128]{2,1,0:T(8,128)(2,1)} collective-permute-done((bf16[64,64,128]{2,1,0:T(8,128)(2,1)}, bf16[64,64,128]{2,1,0:T(8,128)(2,1)}, u32[]{:S(2)}, u32[]{:S(2)}) %collective-permute-start.3) | collective-permute-done | bytes 1048608 | tf_op jit(solution)/shard_map/ppermute | solution.py:251
  69.7 1.3 %broadcast_select_fusion.1 = bf16[64,64,128]{2,1,0:T(8,128)(2,1)S(1)} fusion(bf16[64,64,128]{2,1,0:T(8,128)(2,1)} %collective-permute-done.2, bf16[64,64,128]{2,1,0:T(8,128)(2,1)} %collective-permute-done.3, pred[]{:T(512)S(6)} %or.3), kind=kLoop, calls=%fused_computation.1 | loop fusion | flops 524288 | bytes 3145729 | tf_op jit(solution)/shard_map/jit(_where)/select_n | solution.py:254
  72.2 19.3 %collective-permute-done.5 = bf16[64,64,128]{2,1,0:T(8,128)(2,1)S(1)} collective-permute-done((bf16[64,64,128]{2,1,0:T(8,128)(2,1)}, bf16[64,64,128]{2,1,0:T(8,128)(2,1)S(1)}, u32[]{:S(2)}, u32[]{:S(2)}) %collective-permute-start.5) | collective-permute-done | bytes 1048608 | tf_op jit(solution)/shard_map/ppermute | solution.py:252
  95.0 4.6 %collective-permute-start.9 = (bf16[32,64,128]{2,1,0:T(8,128)(2,1)}, bf16[32,64,128]{2,1,0:T(8,128)(2,1)}, u32[]{:S(2)}, u32[]{:S(2)}) collective-permute-start(bf16[32,64,128]{2,1,0:T(8,128)(2,1)} %get-tuple-element.5), channel_id=1, source_target_pairs={{2,3},{3,2},{6,7},{7,6},{8,9},{9,8},{12,13},{13,12},{18,19},{19,18... | collective-permute-start | bytes 1572872 | tf_op jit(solution)/shard_map/ppermute | solution.py:268
  102.8 3.0 %shard_map.98.refs_12_ = f32[64,64,128]{2,1,0:T(8,128)S(1)} custom-call(f32[64,64,128]{2,1,0:T(8,128)S(1)} %copy-done.1, f32[1,128]{1,0:T(1,128)S(1)} %bitcast.34, f32[1,128]{1,0:T(1,128)S(1)} %bitcast.36, bf16[128,128]{1,0:T(8,128)(2,1)S(1)} %copy-done.6), custom_call_target="tpu_custom_call" | custom-call | flops 134217728 | bytes 4194304 | tf_op jit(solution)/shard_map/pallas_call | solution.py:79
  105.8 1.3 %copy-done.2 = f32[64,64,128]{2,1,0:T(8,128)} copy-done((f32[64,64,128]{2,1,0:T(8,128)}, f32[64,64,128]{2,1,0:T(8,128)S(1)}, u32[]{:S(2)}) %copy-start.2) | copy-done | bytes 2097176
  107.1 2.2 %collective-permute-done.11.refs_8_ = bf16[32,64,128]{2,1,0:T(8,128)(2,1)} collective-permute-done((bf16[32,64,128]{2,1,0:T(8,128)(2,1)}, bf16[32,64,128]{2,1,0:T(8,128)(2,1)}, u32[]{:S(2)}, u32[]{:S(2)}) %collective-permute-start.11) | collective-permute-done | bytes 524320 | tf_op jit(solution)/shard_map/ppermute | solution.py:269
  109.3 12.5 %collective-permute-done.7.refs_4_ = bf16[32,64,128]{2,1,0:T(8,128)(2,1)} collective-permute-done((bf16[32,64,128]{2,1,0:T(8,128)(2,1)S(1)}, bf16[32,64,128]{2,1,0:T(8,128)(2,1)}, u32[]{:S(2)}, u32[]{:S(2)}) %collective-permute-start.7) | collective-permute-done | bytes 524320 | tf_op jit(solution)/shard_map/ppermute | solution.py:267
  121.8 9.5 %shard_map.99 = f32[64,64,128]{2,1,0:T(8,128)} custom-call(s32[1]{0:T(128)} %bitcast.refs_0_, bf16[32,64,128]{2,1,0:T(8,128)(2,1)S(1)} %get-tuple-element.8.refs_1_, bf16[32,64,128]{2,1,0:T(8,128)(2,1)S(1)} %get-tuple-element.6.refs_2_, bf16[32,64,128]{2,1,0:T(8,128)(2,1)} %collective-permute-done.6.refs_3_, ...), custom_call_target="tpu_custom_call" | custom-call | flops 134217728 | bytes 4194304 | tf_op jit(solution)/shard_map/pallas_call | solution.py:191
  (60 shorter events, 12.8 us)
Async XLA Ops:
  0.0 1.6 %copy-start = (f32[64,64,128]{2,1,0:T(8,128)S(1)}, f32[64,64,128]{2,1,0:T(8,128)}, u32[]{:S(2)}) copy-start(f32[64,64,128]{2,1,0:T(8,128)} %pair_ref.3) | copy-start | bytes 6291460
  3.7 8.8 %copy-start.12 = (bf16[128,512]{1,0:T(8,128)(2,1)S(1)}, bf16[128,512]{1,0:T(8,128)(2,1)}, u32[]{:S(2)}) copy-start(bf16[128,512]{1,0:T(8,128)(2,1)} %param.13) | copy-start | bytes 393220
  11.7 34.2 %copy-start.14 = (f32[128]{0:T(128)S(1)}, f32[128]{0:T(128)}, u32[]{:S(2)}) copy-start(f32[128]{0:T(128)} %param.15) | copy-start | bytes 1540
  11.7 34.3 %copy-start.13 = (f32[128]{0:T(128)S(1)}, f32[128]{0:T(128)}, u32[]{:S(2)}) copy-start(f32[128]{0:T(128)} %param.16) | copy-start | bytes 1540
  11.7 3.0 %collective-permute-start = (bf16[64,64,128]{2,1,0:T(8,128)(2,1)S(1)}, bf16[64,64,128]{2,1,0:T(8,128)(2,1)S(1)}, u32[]{:S(2)}, u32[]{:S(2)}) collective-permute-start(bf16[64,64,128]{2,1,0:T(8,128)(2,1)S(1)} %shard_map.91.own_ref), channel_id=1, source_target_pairs={{0,1},{1,0},{2,3},{3,2},{4,5},{5,4},{6,7},{7,6},{8,9},{9,8},{10,11... | collective-permute-start | bytes 3145736 | tf_op jit(solution)/shard_map/ppermute | solution.py:239
  17.0 24.5 %collective-permute-start.1 = (bf16[64,64,128]{2,1,0:T(8,128)(2,1)S(1)}, bf16[64,64,128]{2,1,0:T(8,128)(2,1)}, u32[]{:S(2)}, u32[]{:S(2)}) collective-permute-start(bf16[64,64,128]{2,1,0:T(8,128)(2,1)S(1)} %shard_map.93), channel_id=1, source_target_pairs={{0,4},{4,0},{8,12},{12,8},{1,5},{5,1},{9,13},{13,9},{2,6},{6,2},{1... | collective-permute-start | bytes 3145736 | tf_op jit(solution)/shard_map/ppermute | solution.py:247
  18.4 24.8 %collective-permute-start.2 = (bf16[64,64,128]{2,1,0:T(8,128)(2,1)S(1)}, bf16[64,64,128]{2,1,0:T(8,128)(2,1)}, u32[]{:S(2)}, u32[]{:S(2)}) collective-permute-start(bf16[64,64,128]{2,1,0:T(8,128)(2,1)S(1)} %shard_map.93), channel_id=1, source_target_pairs={{4,8},{8,4},{5,9},{9,5},{6,10},{10,6},{7,11},{11,7},{20,24},{24,20... | collective-permute-start | bytes 3145736 | tf_op jit(solution)/shard_map/ppermute | solution.py:246
  41.6 2.9 %collective-permute-start.4 = (bf16[64,64,128]{2,1,0:T(8,128)(2,1)}, bf16[64,64,128]{2,1,0:T(8,128)(2,1)}, u32[]{:S(2)}, u32[]{:S(2)}) collective-permute-start(bf16[64,64,128]{2,1,0:T(8,128)(2,1)} %collective-permute-done.1), channel_id=1, source_target_pairs={{4,8},{8,4},{5,9},{9,5},{6,10},{10,6},{7,11},{11,7},{20,24},{24,20... | collective-permute-start | bytes 3145736 | tf_op jit(solution)/shard_map/ppermute | solution.py:250
  43.2 26.5 %collective-permute-start.3 = (bf16[64,64,128]{2,1,0:T(8,128)(2,1)}, bf16[64,64,128]{2,1,0:T(8,128)(2,1)}, u32[]{:S(2)}, u32[]{:S(2)}) collective-permute-start(bf16[64,64,128]{2,1,0:T(8,128)(2,1)} %collective-permute-done.2), channel_id=1, source_target_pairs={{4,0},{8,12},{5,1},{9,13},{6,2},{10,14},{7,3},{11,15},{20,16},{24,... | collective-permute-start | bytes 3145736 | tf_op jit(solution)/shard_map/ppermute | solution.py:251
  44.5 46.9 %collective-permute-start.5 = (bf16[64,64,128]{2,1,0:T(8,128)(2,1)}, bf16[64,64,128]{2,1,0:T(8,128)(2,1)S(1)}, u32[]{:S(2)}, u32[]{:S(2)}) collective-permute-start(bf16[64,64,128]{2,1,0:T(8,128)(2,1)} %collective-permute-done.4), channel_id=1, source_target_pairs={{4,0},{8,12},{5,1},{9,13},{6,2},{10,14},{7,3},{11,15},{20,16},{24,... | collective-permute-start | bytes 3145736 | tf_op jit(solution)/shard_map/ppermute | solution.py:252
  52.5 47.1 %collective-permute-start.10 = (bf16[32,64,128]{2,1,0:T(8,128)(2,1)}, bf16[32,64,128]{2,1,0:T(8,128)(2,1)S(1)}, u32[]{:S(2)}, u32[]{:S(2)}) collective-permute-start(bf16[32,64,128]{2,1,0:T(8,128)(2,1)} %get-tuple-element.7), channel_id=1, source_target_pairs={{2,1},{3,0},{6,5},{7,4},{8,11},{9,10},{12,15},{13,14},{18,17},{19,... | collective-permute-start | bytes 1572872 | tf_op jit(solution)/shard_map/ppermute | solution.py:269
  55.7 51.4 %collective-permute-start.8 = (bf16[32,64,128]{2,1,0:T(8,128)(2,1)}, bf16[32,64,128]{2,1,0:T(8,128)(2,1)}, u32[]{:S(2)}, u32[]{:S(2)}) collective-permute-start(bf16[32,64,128]{2,1,0:T(8,128)(2,1)} %get-tuple-element.7), channel_id=1, source_target_pairs={{0,1},{1,0},{4,5},{5,4},{10,11},{11,10},{14,15},{15,14},{16,17},{1... | collective-permute-start | bytes 1572872 | tf_op jit(solution)/shard_map/ppermute | solution.py:268
  57.2 49.9 %collective-permute-start.6 = (bf16[32,64,128]{2,1,0:T(8,128)(2,1)S(1)}, bf16[32,64,128]{2,1,0:T(8,128)(2,1)}, u32[]{:S(2)}, u32[]{:S(2)}) collective-permute-start(bf16[32,64,128]{2,1,0:T(8,128)(2,1)S(1)} %get-tuple-element.8.refs_1_), channel_id=1, source_target_pairs={{2,0},{3,1},{6,4},{7,5},{8,10},{9,11},{12,14},{13,15},{18,16},{19,... | collective-permute-start | bytes 1572872 | tf_op jit(solution)/shard_map/ppermute | solution.py:267
  91.6 11.1 %copy-start.11 = (bf16[128,128]{1,0:T(8,128)(2,1)S(1)}, bf16[128,128]{1,0:T(8,128)(2,1)}, u32[]{:S(2)}) copy-start(bf16[128,128]{1,0:T(8,128)(2,1)} %param.17) | copy-start | bytes 98308
  91.6 11.1 %copy-start.1 = (f32[64,64,128]{2,1,0:T(8,128)S(1)}, f32[64,64,128]{2,1,0:T(8,128)}, u32[]{:S(2)}) copy-start(f32[64,64,128]{2,1,0:T(8,128)} %pair_ref.3) | copy-start | bytes 6291460
  91.6 11.1 %copy-start.6 = (bf16[128,128]{1,0:T(8,128)(2,1)S(1)}, bf16[128,128]{1,0:T(8,128)(2,1)}, u32[]{:S(2)}) copy-start(bf16[128,128]{1,0:T(8,128)(2,1)} %weight_ref.1) | copy-start | bytes 98308
  91.6 11.1 %copy-start.8 = (f32[128]{0:T(128)S(1)}, f32[128]{0:T(128)}, u32[]{:S(2)}) copy-start(f32[128]{0:T(128)} %param.11) | copy-start | bytes 1540
  91.6 11.1 %copy-start.10 = (f32[128]{0:T(128)S(1)}, f32[128]{0:T(128)}, u32[]{:S(2)}) copy-start(f32[128]{0:T(128)} %param.12) | copy-start | bytes 1540
  93.7 15.6 %collective-permute-start.11 = (bf16[32,64,128]{2,1,0:T(8,128)(2,1)}, bf16[32,64,128]{2,1,0:T(8,128)(2,1)}, u32[]{:S(2)}, u32[]{:S(2)}) collective-permute-start(bf16[32,64,128]{2,1,0:T(8,128)(2,1)} %get-tuple-element.5), channel_id=1, source_target_pairs={{0,3},{1,2},{4,7},{5,6},{10,9},{11,8},{14,13},{15,12},{16,19},{17,... | collective-permute-start | bytes 1572872 | tf_op jit(solution)/shard_map/ppermute | solution.py:269
  95.0 14.4 %collective-permute-start.9 = (bf16[32,64,128]{2,1,0:T(8,128)(2,1)}, bf16[32,64,128]{2,1,0:T(8,128)(2,1)}, u32[]{:S(2)}, u32[]{:S(2)}) collective-permute-start(bf16[32,64,128]{2,1,0:T(8,128)(2,1)} %get-tuple-element.5), channel_id=1, source_target_pairs={{2,3},{3,2},{6,7},{7,6},{8,9},{9,8},{12,13},{13,12},{18,19},{19,18... | collective-permute-start | bytes 1572872 | tf_op jit(solution)/shard_map/ppermute | solution.py:268
  99.6 0.8 copy-start.3
  100.4 21.4 %collective-permute-start.7 = (bf16[32,64,128]{2,1,0:T(8,128)(2,1)S(1)}, bf16[32,64,128]{2,1,0:T(8,128)(2,1)}, u32[]{:S(2)}, u32[]{:S(2)}) collective-permute-start(bf16[32,64,128]{2,1,0:T(8,128)(2,1)S(1)} %get-tuple-element.6.refs_2_), channel_id=1, source_target_pairs={{0,2},{1,3},{4,6},{5,7},{10,8},{11,9},{14,12},{15,13},{16,18},{17,... | collective-permute-start | bytes 1572872 | tf_op jit(solution)/shard_map/ppermute | solution.py:267
  102.7 19.1 %copy-start.4 = (bf16[32,64,128]{2,1,0:T(8,128)(2,1)S(1)}, bf16[32,64,128]{2,1,0:T(8,128)(2,1)}, u32[]{:S(2)}) copy-start(bf16[32,64,128]{2,1,0:T(8,128)(2,1)} %copy-done.3) | copy-start | bytes 1572868
  105.7 1.4 %copy-start.2 = (f32[64,64,128]{2,1,0:T(8,128)}, f32[64,64,128]{2,1,0:T(8,128)S(1)}, u32[]{:S(2)}) copy-start(f32[64,64,128]{2,1,0:T(8,128)S(1)} %shard_map.98.refs_12_) | copy-start | bytes 6291460
  (3 other events, 2.1 us)

commit v2 on v0

v2 whole, which is shorter than its diff:
```python
import functools

import jax
import jax.numpy as jnp
from jax import lax
from jax.experimental import pallas as pl
from jax.experimental.pallas import tpu as pltpu
from jax.sharding import PartitionSpec as P

EPS = 1e-05
VMEM = pl.BlockSpec(memory_space=pltpu.VMEM)
SMEM = pl.BlockSpec(memory_space=pltpu.SMEM)
HBM = pl.BlockSpec(memory_space=pltpu.HBM)
LIMIT = 24 * 1024 * 1024
STEP = 16
CHUNKS = 4


def call(body, out_shape, in_specs, out_specs, scratch, flops, moved):
    return pl.pallas_call(
        body,
        out_shape=out_shape,
        in_specs=in_specs,
        out_specs=out_specs,
        scratch_shapes=scratch,
        compiler_params=pltpu.CompilerParams(vmem_limit_bytes=LIMIT),
        cost_estimate=pl.CostEstimate(flops=flops, bytes_accessed=moved, transcendentals=0),
    )


def sigmoid(values):
    return 0.5 * jnp.tanh(0.5 * values) + 0.5


def dot(left, right, dims):
    return lax.dot_general(left, right, (dims, ((), ())), preferred_element_type=jnp.float32)


def split(values):
    high = values.astype(jnp.bfloat16)
    low = (values - high.astype(jnp.float32)).astype(jnp.bfloat16)
    return jnp.concatenate([high, low], axis=1)


def norm_body(pair_ref, gain_ref, shift_ref, out_ref, held, sems):
    rows, cols, channels = out_ref.shape
    span = lambda at: pl.ds(at * STEP, STEP)
    copies = [
        pltpu.make_async_copy(pair_ref.at[span(at)], held.at[span(at)], sems.at[at])
        for at in range(rows // STEP)
    ]
    for copy in copies:
        copy.start()
    ones = jnp.full((2 * channels, channels), 1.0 / channels, jnp.bfloat16)
    gain, shift = gain_ref[...], shift_ref[...]
    for at, copy in enumerate(copies):
        copy.wait()
        values = held[span(at)].reshape(STEP * cols, channels)
        centered = values - dot(split(values), ones, ((1,), (0,)))
        spread = dot(split(centered * centered), ones, ((1,), (0,)))
        normed = centered * lax.rsqrt(spread + EPS) * gain + shift
        out_ref[span(at)] = normed.astype(jnp.bfloat16).reshape(STEP, cols, channels)


def layer_norm(pair, gain, shift):
    return call(
        norm_body,
        jax.ShapeDtypeStruct(pair.shape, jnp.bfloat16),
        [HBM, VMEM, VMEM],
        VMEM,
        [pltpu.VMEM(pair.shape, jnp.float32), pltpu.SemaphoreType.DMA((pair.shape[0] // STEP,))],
        16 * pair.size,
        6 * pair.size,
    )(pair, gain, shift)


def gate_body(normed_ref, weight_ref, out_ref):
    rows, cols, channels = normed_ref.shape
    weight = weight_ref[...]

    def part(at, carry):
        span = pl.ds(pl.multiple_of(at * STEP, STEP), STEP)
        values = dot(normed_ref[span].reshape(STEP * cols, channels), weight, ((1,), (0,)))
        out_ref[span] = sigmoid(values).reshape(STEP, cols, channels)
        return carry

    lax.fori_loop(0, rows // STEP, part, 0)


def output_gate(normed, weight):
    return call(
        gate_body,
        jax.ShapeDtypeStruct(normed.shape, jnp.float32),
        [VMEM, VMEM],
        VMEM,
        [],
        2 * normed.size * normed.shape[2],
        6 * normed.size,
    )(normed, weight)


def side_body(normed_ref, mask_ref, weight_ref, *rest):
    outs, held = rest[:-1], rest[-1]
    rows, cols, channels = normed_ref.shape
    planes = channels // 2
    weight = weight_ref[...]
    zero = jnp.zeros((cols, channels), jnp.bfloat16)

    def part(at, carry):
        span = pl.ds(pl.multiple_of(at * STEP, STEP), STEP)
        keep = mask_ref[span].astype(jnp.float32)
        keep = jnp.concatenate([keep, keep], axis=1)
        normed = normed_ref[span]
        for row in range(0, STEP, 2):
            parts = []
            for tile in (normed[row], normed[row + 1]):
                parts += [jnp.concatenate([tile, zero], 1), jnp.concatenate([zero, tile], 1)]
            both = dot(weight, jnp.concatenate(parts, axis=0), ((1,), (1,)))
            for more in range(2):
                values = both[:, 2 * cols * more : 2 * cols * (more + 1)]
                kept = values[:planes] * keep[row + more : row + more + 1]
                held[pl.ds(row + more, planes, stride=STEP), :] = sigmoid(values[planes:]) * kept
        done = 0
        for out in outs:
            first = done % planes
            count = out.shape[0]
            value = held[first * STEP : (first + count) * STEP, :]
            out[:, span, :] = value.reshape(count, STEP, 2 * cols).astype(jnp.bfloat16)
            done += count
        return carry

    lax.fori_loop(0, rows // STEP, part, 0)


def side(normed, mask, weight, counts):
    rows, cols, channels = normed.shape
    return call(
        side_body,
        [jax.ShapeDtypeStruct((count, rows, 2 * cols), jnp.bfloat16) for count in counts],
        [VMEM, VMEM, VMEM],
        [VMEM] * len(counts),
        [pltpu.VMEM((channels // 2 * STEP, 2 * cols), jnp.float32)],
        4 * normed.size * channels,
        4 * normed.size,
    )(normed, mask, weight)


def paired(tiles):
    low = lax.broadcasted_iota(jnp.int32, tiles[0].shape, 1) < tiles[0].shape[1] // 2
    zero = jnp.zeros(tiles[0].shape, jnp.bfloat16)
    first = jnp.concatenate([jnp.where(low, tile, zero) for tile in tiles], axis=1)
    second = jnp.concatenate([jnp.where(low, zero, tile) for tile in tiles], axis=1)
    return jnp.concatenate([first, second], axis=0)


def triangle_body(flags_ref, *refs):
    out_ref, count = refs[-1], (len(refs) - 1) // 3
    left, yes, no = refs[:count], refs[count : 2 * count], refs[2 * count : 3 * count]
    flag = flags_ref[0] == 1

    def part(at, carry):
        first = jnp.concatenate([ref[at] for ref in left], axis=1)
        second = paired([jnp.where(flag, one[at], two[at]) for one, two in zip(yes, no)])
        out_ref[at] = dot(first, second, ((1,), (1,))).astype(jnp.bfloat16)
        return carry

    lax.fori_loop(0, out_ref.shape[0], part, 0, unroll=8)


def triangle(flags, left, yes, no):
    planes, rows, lanes = left[0].shape
    return call(
        triangle_body,
        jax.ShapeDtypeStruct((planes, rows, 2 * rows), jnp.bfloat16),
        [SMEM] + [VMEM] * (3 * len(left)),
        VMEM,
        [],
        4 * planes * rows * rows * lanes * len(left),
        6 * left[0].size * len(left),
    )(flags, *left, *yes, *no)


def served_body(start, flags_ref, *refs):
    mine, ends, far, near, outs = (refs[at : at + 2] for at in range(0, 10, 2))
    use_far, swap = flags_ref[0] == 1, flags_ref[1] == 1
    rows = mine[0].shape[1]

    def part(at, carry):
        own = jnp.concatenate([ref[start + at] for ref in mine], axis=1)
        end = jnp.concatenate([ref[start + at] for ref in ends], axis=1)
        first = jnp.concatenate([jnp.where(swap, end, own), jnp.where(swap, own, end)], axis=0)
        second = paired(
            [jnp.where(use_far, one[at], two[start + at]) for one, two in zip(far, near)]
        )
        both = dot(first, second, ((1,), (1,))).astype(jnp.bfloat16)
        outs[0][at] = both[:rows]
        outs[1][at] = both[rows:]
        return carry

    lax.fori_loop(0, outs[0].shape[0], part, 0, unroll=8)


def served(start, flags, mine, ends, far, near):
    count, rows, lanes = far[0].shape
    return call(
        functools.partial(served_body, start),
        [jax.ShapeDtypeStruct((count, rows, 2 * rows), jnp.bfloat16)] * 2,
        [SMEM] + [VMEM] * 8,
        [VMEM] * 2,
        [],
        16 * count * rows * rows * lanes,
        16 * count * rows * lanes,
    )(flags, *mine, *ends, *far, *near)


def finish_body(counts, flags_ref, *refs):
    early, rest = refs[:2], refs[2:]
    chunks = [rest[3 * at : 3 * at + 3] for at in range(len(counts))]
    gain_ref, shift_ref, weight_ref, gate_ref, out_ref = rest[3 * len(counts) :][:5]
    total, held, made, sems = rest[3 * len(counts) + 5 :]
    planes, rows, lanes = early[0].shape
    width = lanes // 2
    is_early, is_middle = flags_ref[2] == 1, flags_ref[3] == 1
    weight = weight_ref[...]

    def mean(values):
        return (values + pltpu.roll(values, width, 1)) * (1.0 / (2 * planes))

    def part(at, carry):
        span = pl.ds(pl.multiple_of(at * STEP, STEP), STEP)
        added = jnp.zeros((STEP, lanes), jnp.float32)
        plane = 0
        for chunk, count in zip(chunks, counts):
            for inner in range(count):
                received, mine, others = (ref[inner, span] for ref in chunk)
                one = jnp.where(is_early, early[0][plane, span], received)
                two = jnp.where(is_middle, mine, others)
                two = jnp.where(is_early, early[1][plane, span], two)
                value = one.astype(jnp.float32) + two.astype(jnp.float32)
                total[plane] = value
                added = added + value
                plane += 1
        middle = mean(added)
        added = jnp.zeros((STEP, lanes), jnp.float32)
        for plane in range(planes):
            centered = total[plane] - middle
            added = added + centered * centered
        scale = lax.rsqrt(mean(added) + EPS)
        for plane in range(planes):
            normed = (total[plane] - middle) * scale * gain_ref[plane] + shift_ref[plane]
            held[pl.ds(plane, STEP, stride=planes), :] = normed
        for row in range(STEP):
            tile = held[row * planes : (row + 1) * planes, :].T.astype(jnp.bfloat16)
            update = dot(tile[:width], weight[:planes], ((1,), (0,)))
            update += dot(tile[width:], weight[planes:], ((1,), (0,)))
            made[at * STEP + row] = update * gate_ref[at * STEP + row]
        pltpu.make_async_copy(made.at[span], out_ref.at[span], sems.at[at]).start()
        return carry

    lax.fori_loop(0, rows // STEP, part, 0)
    for at in range(rows // STEP):
        span = pl.ds(at * STEP, STEP)
        pltpu.make_async_copy(made.at[span], out_ref.at[span], sems.at[at]).wait()


def finish(flags, early, chunks, gain, shift, weight, gate):
    planes, rows, lanes = early[0].shape
    counts = [chunk[0].shape[0] for chunk in chunks]
    parts = [array for chunk in chunks for array in chunk]
    return call(
        functools.partial(finish_body, counts),
        jax.ShapeDtypeStruct(gate.shape, jnp.float32),
        [SMEM] + [VMEM] * (2 + len(parts) + 4),
        HBM,
        [
            pltpu.VMEM((planes, STEP, lanes), jnp.float32),
            pltpu.VMEM((planes * STEP, lanes), jnp.float32),
            pltpu.VMEM(gate.shape, jnp.float32),
            pltpu.SemaphoreType.DMA((rows // STEP,)),
        ],
        2 * gate.size * gate.shape[2],
        8 * gate.size,
    )(flags, *early, *parts, gain, shift, weight, gate)


def planes_of(vector, width):
    return jnp.repeat(vector.reshape(2, -1).T, width, axis=1)[:, None, :]


def per_device(
    mesh_rows,
    mesh_cols,
    pair,
    pair_mask,
    in_gain,
    in_bias,
    proj_weight,
    gate_weight,
    out_gain,
    out_bias,
    out_weight,
):
    rows, cols, channels = pair.shape
    planes = channels // 2
    row, col = lax.axis_index("rows"), lax.axis_index("cols")
    chip, core = col // 2, col % 2

    weights = proj_weight.reshape(channels, 2, 2, 2, planes).transpose(1, 2, 4, 3, 0)
    weights = weights.reshape(2, 2 * planes, 2 * channels)
    gain, shift = planes_of(out_gain, cols), planes_of(out_bias, cols)

    if mesh_rows == 4 and mesh_cols == 4:
        both = ("rows", "cols")
        at = lambda z, x, h: z * 4 + 2 * x + h
        places = [(z, x, h) for z in range(4) for x in range(2) for h in range(2)]
        whole = core == row % 2
        is_early, is_middle = chip == row // 2, (row == 1) | (row == 2)
        flags = jnp.stack([whole, ~is_early, is_early, is_middle]).astype(jnp.int32)
        flip = [(at(z, x, h), at(z, x, 1 - h)) for z, x, h in places]
        to_whole = [(at(z, x, h), at(z, x, 1 - h)) for z, x, h in places if h != z % 2]
        from_whole = [(at(z, x, h), at(z, x, 1 - h)) for z, x, h in places if h == z % 2]
        partners = [(at(z, x, h), at(z ^ 1, x, h)) for z, x, h in places]
        mids = [place for place in places if place[0] in (1, 2)]
        near_straight = [(at(z, x, h), at(3 - z, x, h)) for z, x, h in mids if h == z % 2]
        near_across = [(at(z, x, h), at(3 - z, x, 1 - h)) for z, x, h in mids if h != z % 2]
        far_straight = [(at(z, x, h), at(3 - z, x, h)) for z, x, h in mids if h != z % 2]
        far_across = [(at(z, x, h), at(3 - z, x, 1 - h)) for z, x, h in mids if h == z % 2]
        owner = lambda z: 1 - z // 2
        early_pairs = [(at(z, x, h), at(z, 1 - x, h)) for z, x, h in places if x == owner(z)]
        first_pairs = [(at(z, x, h), at(z ^ 1, x, h)) for z, x, h in mids if x == owner(z)]
        first_pairs += [(at(z, x, h), at(z, 1 - x, h)) for z, x, h in mids if x != owner(z)]
        second_pairs = [(at(z, x, h), at(z ^ 1, 1 - x, h)) for z, x, h in mids if x != owner(z)]
        move = lambda array, pairs: lax.ppermute(array, both, pairs)

        mask_partner = move(pair_mask, partners)
        normed = layer_norm(pair, in_gain[None], in_bias[None])
        normed_partner = move(normed, partners)
        (b_own,) = side(normed, pair_mask, weights[1], [planes])
        near = [move(b_own, near_straight), move(b_own, near_across)]
        b_other = move(b_own, to_whole)
        (a_own,) = side(normed, pair_mask, weights[0], [planes])
        a_other = move(a_own, flip)
        gate = output_gate(normed, gate_weight)
        normed_partner, gate, gain, shift = lax.optimization_barrier(
            (normed_partner, gate, gain, shift)
        )
        count = planes // CHUNKS
        b_partner, *pieces = side(
            normed_partner, mask_partner, weights[1], [planes] + [count] * CHUNKS
        )
        far = [[move(piece, far_straight), move(piece, far_across)] for piece in pieces]
        (a_end,) = side(normed_partner, mask_partner, weights[0], [planes])
        a_end_other = move(a_end, flip)
        b_partner_other = move(b_partner, from_whole)
        product = triangle(
            flags, [a_own, a_other], [b_own, b_other], [b_partner, b_partner_other]
        )
        early = [product, move(product, early_pairs)]
        chunks = []
        for index in range(CHUNKS):
            one, two = served(
                index * count,
                flags,
                [a_own, a_other],
                [a_end, a_end_other],
                far[index],
                near,
            )
            chunks.append([move(one, first_pairs), two, move(two, second_pairs)])
    else:
        flags = jnp.array([1, 0, 1, 0], jnp.int32)
        normed = layer_norm(pair, in_gain[None], in_bias[None])
        count = planes // CHUNKS
        pieces = side(normed, pair_mask, weights[1], [count] * CHUNKS)
        lefts = side(normed, pair_mask, weights[0], [count] * CHUNKS)
        gate = output_gate(normed, gate_weight)
        sums = []
        for piece, left in zip(pieces, lefts):
            gathered = lax.all_gather(piece, "rows")
            blocks = [gathered[index] for index in range(mesh_rows)]
            product = jnp.stack([triangle(flags, [left], [block], [block]) for block in blocks])
            parts = lax.all_to_all(product, "cols", 0, 0, tiled=True)
            sums.append(jnp.sum(parts.astype(jnp.float32), axis=0))
        total = jnp.concatenate(sums, axis=0)
        zero = jnp.zeros_like(total)
        early, chunks = [total, zero], [[total, total, total]]
    return finish(flags, early, chunks, gain, shift, out_weight, gate)


def solution(mesh):
    tile = P(("groups", "rows"), "cols", None)
    return jax.shard_map(
        functools.partial(per_device, mesh.shape["rows"], mesh.shape["cols"]),
        mesh=mesh,
        in_specs=(tile, P(("groups", "rows"), "cols")) + (P(),) * 7,
        out_specs=tile,
        check_vma=False,
    )
```

time: 188 us -> 111 us (0.59); the launches traced: 185 us -> 110 us
  local copies, waits for them, and re-layouts: 48.9 us -> 7.54 us
  Pallas kernels: 0 us -> 37.9 us
  blocking collectives: 36.4 us -> 0 us
  starting transfers between devices: 5.09 us -> 30.9 us
  waiting for transfers between devices: 57.9 us -> 32.9 us
  between operations: 13.6 us -> 0.55 us
  matrix products: 11.5 us -> 0 us
  other arithmetic: 11.2 us -> 0.08 us
    all_gather x1 -> x0, waiting for transfers between devices: 47.1 us -> none  [per_device(): lax.all_gather(moved_b, 'rows', axis=1, tiled=True)]
    pallas_call x0 -> x12, Pallas kernels: none -> 37.9 us  [the longest x4 13.7 us: side(): call(side_body, [jax.ShapeDtypeStruct((count, rows, 2 * cols), jnp.bfloat...]
    all_to_all x2 -> x0, blocking collectives: 36.4 us -> none  [the longest x1 18.7 us: per_device(): lax.all_to_all(side_a, 'cols', split_axis=0, concat_axis=2, tiled=True)]
    ppermute x0 -> x25, waiting for transfers between devices: none -> 32.9 us  [per_device(): move = lambda array, pairs: lax.ppermute(array, both, pairs)]
    ppermute x0 -> x25, starting transfers between devices: none -> 30.9 us  [per_device(): move = lambda array, pairs: lax.ppermute(array, both, pairs)]
    convert_element_type x4 -> x0, local copies, waits for them, and re-layouts: 15.5 us -> none  [the longest x2 7.87 us: gated_side(): return gated.astype(jnp.bfloat16)]
    all_to_all x4 -> x0, local copies, waits for them, and re-layouts: 14.4 us -> none  [the longest x2 7.59 us: per_device(): lax.all_to_all(side_b, 'cols', split_axis=0, concat_axis=2, tiled=True)]
    unnamed x28 -> x35, local copies, waits for them, and re-layouts: 19 us -> 6.56 us
  transfers between devices with their start and end apart: 2 -> 25, of which waited for: 2 -> 9; matrix products, arithmetic and copies ran while one was open for 8% -> 1% of each run, Pallas kernels for 0% -> 27%
where the time goes in v2:
time: 111 us; the launch traced here: 110 us
  Pallas kernels  37.9 us (34%)
  waiting for transfers between devices  32.9 us (30%)
  starting transfers between devices  30.9 us (28%)
  local copies, waits for them, and re-layouts  7.54 us (7%)
    ppermute x25, waiting for transfers between devices, per_device(): move = lambda array, pairs: lax.ppermute(array, both, pairs)  32.9 us
    ppermute x25, starting transfers between devices, per_device(): move = lambda array, pairs: lax.ppermute(array, both, pairs)  30.9 us
    pallas_call x4, Pallas kernels, side(): call(side_body, [jax.ShapeDtypeStruct((count, rows, 2 * cols), jnp.bfloat...  13.7 us
    pallas_call x4, Pallas kernels, served(): call(functools.partial(served_body, start), [jax.ShapeDtypeStruct((count,...  10.1 us
    unnamed x35, local copies, waits for them, and re-layouts  6.56 us
    pallas_call x1, Pallas kernels, finish(): call(functools.partial(finish_body, counts), jax.ShapeDtypeStruct(gate.sh...  6.22 us
    pallas_call x1, Pallas kernels, triangle(): call(triangle_body, jax.ShapeDtypeStruct((planes, rows, 2 * rows), jnp.bf...  4.63 us
    pallas_call x1, Pallas kernels, layer_norm(): call(norm_body, jax.ShapeDtypeStruct(pair.shape, jnp.bfloat16), [HBM, VME...  2.4 us
  transfers between devices with their start and end apart: 25, of which 9 were waited for; matrix products, arithmetic and copies ran while one was open for 1% of the time, Pallas kernels for 27%

profile of v2, /device:TPU:7, one launch (start us, length us, event | category | flops | bytes accessed | tf_op | source)
XLA Modules:
  0.0 109.9 jit_solution(10119849961513137113)
XLA Ops:
  0.0 1.6 %copy-done.2 = f32[64,64,128]{2,1,0:T(8,128)S(1)} copy-done((f32[64,64,128]{2,1,0:T(8,128)S(1)}, f32[64,64,128]{2,1,0:T(8,128)}, u32[]{:S(2)}) %copy-start.2) | copy-done | bytes 2097176
  2.9 2.4 %shard_map.91.normed_ref = bf16[64,64,128]{2,1,0:T(8,128)(2,1)S(1)} custom-call(f32[64,64,128]{2,1,0:T(8,128)S(1)} %copy-done.2, f32[1,128]{1,0:T(1,128)S(1)} %bitcast.25, f32[1,128]{1,0:T(1,128)S(1)} %bitcast.26), custom_call_target="tpu_custom_call" | custom-call | flops 8388608 | bytes 3145728 | tf_op jit(solution)/shard_map/pallas_call | solution.py:66
  7.0 2.2 %shard_map.92.refs_0_ = bf16[64,64,128]{2,1,0:T(8,128)(2,1)S(1)} custom-call(bf16[64,64,128]{2,1,0:T(8,128)(2,1)S(1)} %shard_map.91.normed_ref, s32[64,64]{1,0:T(8,128)S(1)} %copy-done.3, bf16[128,256]{1,0:T(8,128)(2,1)S(1)} %bitcast.21), custom_call_target="tpu_custom_call" | custom-call | flops 268435456 | bytes 2097152 | tf_op jit(solution)/shard_map/pallas_call | solution.py:137
  10.3 3.2 %shard_map.93.refs_2_ = bf16[64,64,128]{2,1,0:T(8,128)(2,1)} custom-call(bf16[64,64,128]{2,1,0:T(8,128)(2,1)S(1)} %shard_map.91.normed_ref, s32[64,64]{1,0:T(8,128)S(1)} %copy-done.3, bf16[128,256]{1,0:T(8,128)(2,1)S(1)} %bitcast.23), custom_call_target="tpu_custom_call" | custom-call | flops 268435456 | bytes 2097152 | tf_op jit(solution)/shard_map/pallas_call | solution.py:137
  13.6 2.9 %collective-permute-start.1 = (bf16[64,64,128]{2,1,0:T(8,128)(2,1)}, bf16[64,64,128]{2,1,0:T(8,128)(2,1)}, u32[]{:S(2)}, u32[]{:S(2)}) collective-permute-start(bf16[64,64,128]{2,1,0:T(8,128)(2,1)} %shard_map.93.refs_2_), channel_id=1, source_target_pairs={{1,0},{3,2},{4,5},{6,7},{9,8},{11,10},{12,13},{14,15},{17,16},{19,... | collective-permute-start | bytes 3145736 | tf_op jit(solution)/shard_map/ppermute | solution.py:333
  16.5 1.7 %collective-permute-start.9 = (bf16[64,64,128]{2,1,0:T(8,128)(2,1)}, bf16[64,64,128]{2,1,0:T(8,128)(2,1)}, u32[]{:S(2)}, u32[]{:S(2)}) collective-permute-start(bf16[64,64,128]{2,1,0:T(8,128)(2,1)} %shard_map.93.refs_2_), channel_id=1, source_target_pairs={{5,9},{7,11},{8,4},{10,6},{21,25},{23,27},{24,20},{26,22}} | collective-permute-start | bytes 3145736 | tf_op jit(solution)/shard_map/ppermute | solution.py:333
  21.2 8.3 %collective-permute-done.2.normed_ref = bf16[64,64,128]{2,1,0:T(8,128)(2,1)} collective-permute-done((bf16[64,64,128]{2,1,0:T(8,128)(2,1)S(1)}, bf16[64,64,128]{2,1,0:T(8,128)(2,1)}, u32[]{:S(2)}, u32[]{:S(2)}) %collective-permute-start.2) | collective-permute-done | bytes 1048608 | tf_op jit(solution)/shard_map/ppermute | solution.py:333
  29.5 1.6 %collective-permute-start.10 = (bf16[64,64,128]{2,1,0:T(8,128)(2,1)}, bf16[64,64,128]{2,1,0:T(8,128)(2,1)}, u32[]{:S(2)}, u32[]{:S(2)}) collective-permute-start(bf16[64,64,128]{2,1,0:T(8,128)(2,1)} %shard_map.93.refs_2_), channel_id=1, source_target_pairs={{4,9},{6,11},{9,4},{11,6},{20,25},{22,27},{25,20},{27,22}} | collective-permute-start | bytes 3145736 | tf_op jit(solution)/shard_map/ppermute | solution.py:333
  31.2 4.7 %shard_map.95 = (bf16[64,64,128]{2,1,0:T(8,128)(2,1)}, bf16[16,64,128]{2,1,0:T(8,128)(2,1)}, bf16[16,64,128]{2,1,0:T(8,128)(2,1)S(1)}, bf16[16,64,128]{2,1,0:T(8,128)(2,1)S(1)}, bf16[16,64,128]{2,1,0:T(8,128)(2,1)S(1)}) custom-call(bf16[64,64,128]{2,1,0:T(8,128)(2,1)} %collective-permute-done.2.normed_ref, s32[64,64]{1,0:T(8,128)S(1)} %collective-permute-done.3.mask_ref, ...), custom_call_target="tpu_custom_call" | custom-call | flops 268435456 | bytes 2097152 | tf_op jit(solution)/shard_map/pallas_call | solution.py:137
  39.3 3.5 %shard_map.97.refs_2_ = bf16[64,64,128]{2,1,0:T(8,128)(2,1)S(1)} custom-call(bf16[64,64,128]{2,1,0:T(8,128)(2,1)} %collective-permute-done.2.normed_ref, s32[64,64]{1,0:T(8,128)S(1)} %collective-permute-done.3.mask_ref, bf16[128,256]{1,0:T(8,128)(2,1)S(1)} %bitcast.22), custom_call_target="tpu_custom_call" | custom-call | flops 268435456 | bytes 2097152 | tf_op jit(solution)/shard_map/pallas_call | solution.py:137
  42.8 2.9 %collective-permute-start.6 = (bf16[64,64,128]{2,1,0:T(8,128)(2,1)S(1)}, bf16[64,64,128]{2,1,0:T(8,128)(2,1)}, u32[]{:S(2)}, u32[]{:S(2)}) collective-permute-start(bf16[64,64,128]{2,1,0:T(8,128)(2,1)S(1)} %shard_map.97.refs_2_), channel_id=1, source_target_pairs={{0,1},{1,0},{2,3},{3,2},{4,5},{5,4},{6,7},{7,6},{8,9},{9,8},{10,11... | collective-permute-start | bytes 3145736 | tf_op jit(solution)/shard_map/ppermute | solution.py:333
  48.8 4.6 %shard_map.96.refs_0_ = bf16[64,64,128]{2,1,0:T(8,128)(2,1)S(1)} custom-call(s32[4]{0:T(128)S(1)} %add_convert_fusion.flags_ref, bf16[64,64,128]{2,1,0:T(8,128)(2,1)S(1)} %shard_map.92.refs_0_, bf16[64,64,128]{2,1,0:T(8,128)(2,1)S(1)} %collective-permute-done.refs_1_, bf16[64,64,128]{2,1,0:T(8,128)(2,1)} %shard_map.93.refs_2_, ...), custom_call_target="tpu_custom_call" | custom-call | flops 268435456 | bytes 6291456 | tf_op jit(solution)/shard_map/pallas_call | solution.py:172
  53.4 2.2 %collective-permute-start.5 = (bf16[64,64,128]{2,1,0:T(8,128)(2,1)S(1)}, bf16[64,64,128]{2,1,0:T(8,128)(2,1)S(1)}, u32[]{:S(2)}, u32[]{:S(2)}) collective-permute-start(bf16[64,64,128]{2,1,0:T(8,128)(2,1)S(1)} %shard_map.96.refs_0_), channel_id=1, source_target_pairs={{2,0},{3,1},{6,4},{7,5},{8,10},{9,11},{12,14},{13,15},{18,16},{19,... | collective-permute-start | bytes 3145736 | tf_op jit(solution)/shard_map/ppermute | solution.py:333
  58.4 2.5 %shard_map.98 = (bf16[16,64,128]{2,1,0:T(8,128)(2,1)S(1)}, bf16[16,64,128]{2,1,0:T(8,128)(2,1)S(1)}) custom-call(s32[4]{0:T(128)S(1)} %add_convert_fusion.flags_ref, bf16[64,64,128]{2,1,0:T(8,128)(2,1)S(1)} %shard_map.92.refs_0_, bf16[64,64,128]{2,1,0:T(8,128)(2,1)S(1)} %collective-permute-done.refs_1_, bf16[64,64,128]{2,1,0:T(8,128)(2,1)S(1)} %shard_map.97.refs_2_, ...), custom_call_target="tpu_custom_call" | custom-call | flops 134217728 | bytes 2097152 | tf_op jit(solution)/shard_map/pallas_call | solution.py:205
  60.9 2.5 %shard_map.99 = (bf16[16,64,128]{2,1,0:T(8,128)(2,1)S(1)}, bf16[16,64,128]{2,1,0:T(8,128)(2,1)S(1)}) custom-call(s32[4]{0:T(128)S(1)} %add_convert_fusion.flags_ref, bf16[64,64,128]{2,1,0:T(8,128)(2,1)S(1)} %shard_map.92.refs_0_, bf16[64,64,128]{2,1,0:T(8,128)(2,1)S(1)} %collective-permute-done.refs_1_, bf16[64,64,128]{2,1,0:T(8,128)(2,1)S(1)} %shard_map.97.refs_2_, ...), custom_call_target="tpu_custom_call" | custom-call | flops 134217728 | bytes 2097152 | tf_op jit(solution)/shard_map/pallas_call | solution.py:205
  68.7 2.5 %shard_map.100 = (bf16[16,64,128]{2,1,0:T(8,128)(2,1)S(1)}, bf16[16,64,128]{2,1,0:T(8,128)(2,1)S(1)}) custom-call(s32[4]{0:T(128)S(1)} %add_convert_fusion.flags_ref, bf16[64,64,128]{2,1,0:T(8,128)(2,1)S(1)} %shard_map.92.refs_0_, bf16[64,64,128]{2,1,0:T(8,128)(2,1)S(1)} %collective-permute-done.refs_1_, bf16[64,64,128]{2,1,0:T(8,128)(2,1)S(1)} %shard_map.97.refs_2_, ...), custom_call_target="tpu_custom_call" | custom-call | flops 134217728 | bytes 2097152 | tf_op jit(solution)/shard_map/pallas_call | solution.py:205
  71.2 2.6 %shard_map.101 = (bf16[16,64,128]{2,1,0:T(8,128)(2,1)S(1)}, bf16[16,64,128]{2,1,0:T(8,128)(2,1)S(1)}) custom-call(s32[4]{0:T(128)S(1)} %add_convert_fusion.flags_ref, bf16[64,64,128]{2,1,0:T(8,128)(2,1)S(1)} %shard_map.92.refs_0_, bf16[64,64,128]{2,1,0:T(8,128)(2,1)S(1)} %collective-permute-done.refs_1_, bf16[64,64,128]{2,1,0:T(8,128)(2,1)S(1)} %shard_map.97.refs_2_, ...), custom_call_target="tpu_custom_call" | custom-call | flops 134217728 | bytes 2097152 | tf_op jit(solution)/shard_map/pallas_call | solution.py:205
  73.9 11.4 %collective-permute-done.11.refs_2_ = bf16[16,64,128]{2,1,0:T(8,128)(2,1)S(1)} collective-permute-done((bf16[16,64,128]{2,1,0:T(8,128)(2,1)S(1)}, bf16[16,64,128]{2,1,0:T(8,128)(2,1)S(1)}, u32[]{:S(2)}, u32[]{:S(2)}) %collective-permute-start.11) | collective-permute-done | bytes 262176 | tf_op jit(solution)/shard_map/ppermute | solution.py:333
  88.8 2.1 %collective-permute-done.15.refs_5_ = bf16[16,64,128]{2,1,0:T(8,128)(2,1)S(1)} collective-permute-done((bf16[16,64,128]{2,1,0:T(8,128)(2,1)S(1)}, bf16[16,64,128]{2,1,0:T(8,128)(2,1)S(1)}, u32[]{:S(2)}, u32[]{:S(2)}) %collective-permute-start.15) | collective-permute-done | bytes 262176 | tf_op jit(solution)/shard_map/ppermute | solution.py:333
  94.5 2.1 %collective-permute-done.19.refs_8_ = bf16[16,64,128]{2,1,0:T(8,128)(2,1)S(1)} collective-permute-done((bf16[16,64,128]{2,1,0:T(8,128)(2,1)S(1)}, bf16[16,64,128]{2,1,0:T(8,128)(2,1)S(1)}, u32[]{:S(2)}, u32[]{:S(2)}) %collective-permute-start.19) | collective-permute-done | bytes 262176 | tf_op jit(solution)/shard_map/ppermute | solution.py:333
  96.6 1.5 %collective-permute-done.20.refs_10_ = bf16[16,64,128]{2,1,0:T(8,128)(2,1)S(1)} collective-permute-done((bf16[16,64,128]{2,1,0:T(8,128)(2,1)S(1)}, bf16[16,64,128]{2,1,0:T(8,128)(2,1)S(1)}, u32[]{:S(2)}, u32[]{:S(2)}) %collective-permute-start.20) | collective-permute-done | bytes 262176 | tf_op jit(solution)/shard_map/ppermute | solution.py:333
  98.0 4.1 %collective-permute-done.23.refs_11_ = bf16[16,64,128]{2,1,0:T(8,128)(2,1)S(1)} collective-permute-done((bf16[16,64,128]{2,1,0:T(8,128)(2,1)S(1)}, bf16[16,64,128]{2,1,0:T(8,128)(2,1)S(1)}, u32[]{:S(2)}, u32[]{:S(2)}) %collective-permute-start.23) | collective-permute-done | bytes 262176 | tf_op jit(solution)/shard_map/ppermute | solution.py:333
  102.1 1.5 %collective-permute-done.24.refs_13_ = bf16[16,64,128]{2,1,0:T(8,128)(2,1)S(1)} collective-permute-done((bf16[16,64,128]{2,1,0:T(8,128)(2,1)S(1)}, bf16[16,64,128]{2,1,0:T(8,128)(2,1)S(1)}, u32[]{:S(2)}, u32[]{:S(2)}) %collective-permute-start.24) | collective-permute-done | bytes 262176 | tf_op jit(solution)/shard_map/ppermute | solution.py:333
  103.6 6.2 %shard_map.102 = f32[64,64,128]{2,1,0:T(8,128)} custom-call(s32[4]{0:T(128)S(1)} %add_convert_fusion.flags_ref, bf16[64,64,128]{2,1,0:T(8,128)(2,1)S(1)} %shard_map.96.refs_0_, bf16[64,64,128]{2,1,0:T(8,128)(2,1)S(1)} %collective-permute-done.5.refs_1_, bf16[16,64,128]{2,1,0:T(8,128)(2,1)S(1)} %collective-permute-done.11.refs_2_, ...), custom_call_target="tpu_custom_call" | custom-call | flops 134217728 | bytes 4194304 | tf_op jit(solution)/shard_map/pallas_call | solution.py:270
  (85 shorter events, 28.3 us)
Async XLA Ops:
  5.3 24.2 %collective-permute-start.2 = (bf16[64,64,128]{2,1,0:T(8,128)(2,1)S(1)}, bf16[64,64,128]{2,1,0:T(8,128)(2,1)}, u32[]{:S(2)}, u32[]{:S(2)}) collective-permute-start(bf16[64,64,128]{2,1,0:T(8,128)(2,1)S(1)} %shard_map.91.normed_ref), channel_id=1, source_target_pairs={{0,4},{1,5},{2,6},{3,7},{4,0},{5,1},{6,2},{7,3},{8,12},{9,13},{10,... | collective-permute-start | bytes 3145736 | tf_op jit(solution)/shard_map/ppermute | solution.py:333
  9.2 33.6 %collective-permute-start = (bf16[64,64,128]{2,1,0:T(8,128)(2,1)S(1)}, bf16[64,64,128]{2,1,0:T(8,128)(2,1)S(1)}, u32[]{:S(2)}, u32[]{:S(2)}) collective-permute-start(bf16[64,64,128]{2,1,0:T(8,128)(2,1)S(1)} %shard_map.92.refs_0_), channel_id=1, source_target_pairs={{0,1},{1,0},{2,3},{3,2},{4,5},{5,4},{6,7},{7,6},{8,9},{9,8},{10,11... | collective-permute-start | bytes 3145736 | tf_op jit(solution)/shard_map/ppermute | solution.py:333
  13.6 32.2 %collective-permute-start.1 = (bf16[64,64,128]{2,1,0:T(8,128)(2,1)}, bf16[64,64,128]{2,1,0:T(8,128)(2,1)}, u32[]{:S(2)}, u32[]{:S(2)}) collective-permute-start(bf16[64,64,128]{2,1,0:T(8,128)(2,1)} %shard_map.93.refs_2_), channel_id=1, source_target_pairs={{1,0},{3,2},{4,5},{6,7},{9,8},{11,10},{12,13},{14,15},{17,16},{19,... | collective-permute-start | bytes 3145736 | tf_op jit(solution)/shard_map/ppermute | solution.py:333
  16.5 14.7 %collective-permute-start.3 = (s32[64,64]{1,0:T(8,128)S(1)}, s32[64,64]{1,0:T(8,128)S(1)}, u32[]{:S(2)}, u32[]{:S(2)}) collective-permute-start(s32[64,64]{1,0:T(8,128)S(1)} %copy-done.3), channel_id=1, source_target_pairs={{0,4},{1,5},{2,6},{3,7},{4,0},{5,1},{6,2},{7,3},{8,12},{9,13},{10,... | collective-permute-start | bytes 49160 | tf_op jit(solution)/shard_map/ppermute | solution.py:333
  16.5 30.1 %collective-permute-start.9 = (bf16[64,64,128]{2,1,0:T(8,128)(2,1)}, bf16[64,64,128]{2,1,0:T(8,128)(2,1)}, u32[]{:S(2)}, u32[]{:S(2)}) collective-permute-start(bf16[64,64,128]{2,1,0:T(8,128)(2,1)} %shard_map.93.refs_2_), channel_id=1, source_target_pairs={{5,9},{7,11},{8,4},{10,6},{21,25},{23,27},{24,20},{26,22}} | collective-permute-start | bytes 3145736 | tf_op jit(solution)/shard_map/ppermute | solution.py:333
  29.5 17.7 %collective-permute-start.10 = (bf16[64,64,128]{2,1,0:T(8,128)(2,1)}, bf16[64,64,128]{2,1,0:T(8,128)(2,1)}, u32[]{:S(2)}, u32[]{:S(2)}) collective-permute-start(bf16[64,64,128]{2,1,0:T(8,128)(2,1)} %shard_map.93.refs_2_), channel_id=1, source_target_pairs={{4,9},{6,11},{9,4},{11,6},{20,25},{22,27},{25,20},{27,22}} | collective-permute-start | bytes 3145736 | tf_op jit(solution)/shard_map/ppermute | solution.py:333
  38.0 10.0 %collective-permute-start.4 = (bf16[64,64,128]{2,1,0:T(8,128)(2,1)}, bf16[64,64,128]{2,1,0:T(8,128)(2,1)}, u32[]{:S(2)}, u32[]{:S(2)}) collective-permute-start(bf16[64,64,128]{2,1,0:T(8,128)(2,1)} %get-tuple-element.23.refs_4_), channel_id=1, source_target_pairs={{0,1},{2,3},{5,4},{7,6},{8,9},{10,11},{13,12},{15,14},{16,17},{18,... | collective-permute-start | bytes 3145736 | tf_op jit(solution)/shard_map/ppermute | solution.py:333
  42.8 14.9 %collective-permute-start.6 = (bf16[64,64,128]{2,1,0:T(8,128)(2,1)S(1)}, bf16[64,64,128]{2,1,0:T(8,128)(2,1)}, u32[]{:S(2)}, u32[]{:S(2)}) collective-permute-start(bf16[64,64,128]{2,1,0:T(8,128)(2,1)S(1)} %shard_map.97.refs_2_), channel_id=1, source_target_pairs={{0,1},{1,0},{2,3},{3,2},{4,5},{5,4},{6,7},{7,6},{8,9},{9,8},{10,11... | collective-permute-start | bytes 3145736 | tf_op jit(solution)/shard_map/ppermute | solution.py:333
  46.5 9.1 %collective-permute-start.8 = (bf16[16,64,128]{2,1,0:T(8,128)(2,1)}, bf16[16,64,128]{2,1,0:T(8,128)(2,1)S(1)}, u32[]{:S(2)}, u32[]{:S(2)}) collective-permute-start(bf16[16,64,128]{2,1,0:T(8,128)(2,1)} %get-tuple-element.24), channel_id=1, source_target_pairs={{5,8},{7,10},{8,5},{10,7},{21,24},{23,26},{24,21},{26,23}} | collective-permute-start | bytes 786440 | tf_op jit(solution)/shard_map/ppermute | solution.py:333
  47.2 9.1 %collective-permute-start.13 = (bf16[16,64,128]{2,1,0:T(8,128)(2,1)}, bf16[16,64,128]{2,1,0:T(8,128)(2,1)S(1)}, u32[]{:S(2)}, u32[]{:S(2)}) collective-permute-start(bf16[16,64,128]{2,1,0:T(8,128)(2,1)} %copy-done.12), channel_id=1, source_target_pairs={{4,8},{6,10},{9,5},{11,7},{20,24},{22,26},{25,21},{27,23}} | collective-permute-start | bytes 786440 | tf_op jit(solution)/shard_map/ppermute | solution.py:333
  48.1 9.0 %collective-permute-start.14 = (bf16[16,64,128]{2,1,0:T(8,128)(2,1)}, bf16[16,64,128]{2,1,0:T(8,128)(2,1)S(1)}, u32[]{:S(2)}, u32[]{:S(2)}) collective-permute-start(bf16[16,64,128]{2,1,0:T(8,128)(2,1)} %copy-done.12), channel_id=1, source_target_pairs={{5,8},{7,10},{8,5},{10,7},{21,24},{23,26},{24,21},{26,23}} | collective-permute-start | bytes 786440 | tf_op jit(solution)/shard_map/ppermute | solution.py:333
  53.4 50.2 %collective-permute-start.5 = (bf16[64,64,128]{2,1,0:T(8,128)(2,1)S(1)}, bf16[64,64,128]{2,1,0:T(8,128)(2,1)S(1)}, u32[]{:S(2)}, u32[]{:S(2)}) collective-permute-start(bf16[64,64,128]{2,1,0:T(8,128)(2,1)S(1)} %shard_map.96.refs_0_), channel_id=1, source_target_pairs={{2,0},{3,1},{6,4},{7,5},{8,10},{9,11},{12,14},{13,15},{18,16},{19,... | collective-permute-start | bytes 3145736 | tf_op jit(solution)/shard_map/ppermute | solution.py:333
  55.7 7.8 %collective-permute-start.17 = (bf16[16,64,128]{2,1,0:T(8,128)(2,1)S(1)}, bf16[16,64,128]{2,1,0:T(8,128)(2,1)S(1)}, u32[]{:S(2)}, u32[]{:S(2)}) collective-permute-start(bf16[16,64,128]{2,1,0:T(8,128)(2,1)S(1)} %copy-done.11), channel_id=1, source_target_pairs={{4,8},{6,10},{9,5},{11,7},{20,24},{22,26},{25,21},{27,23}} | collective-permute-start | bytes 786440 | tf_op jit(solution)/shard_map/ppermute | solution.py:333
  56.4 8.4 %collective-permute-start.18 = (bf16[16,64,128]{2,1,0:T(8,128)(2,1)S(1)}, bf16[16,64,128]{2,1,0:T(8,128)(2,1)S(1)}, u32[]{:S(2)}, u32[]{:S(2)}) collective-permute-start(bf16[16,64,128]{2,1,0:T(8,128)(2,1)S(1)} %copy-done.11), channel_id=1, source_target_pairs={{5,8},{7,10},{8,5},{10,7},{21,24},{23,26},{24,21},{26,23}} | collective-permute-start | bytes 786440 | tf_op jit(solution)/shard_map/ppermute | solution.py:333
  57.1 9.0 %collective-permute-start.21 = (bf16[16,64,128]{2,1,0:T(8,128)(2,1)S(1)}, bf16[16,64,128]{2,1,0:T(8,128)(2,1)S(1)}, u32[]{:S(2)}, u32[]{:S(2)}) collective-permute-start(bf16[16,64,128]{2,1,0:T(8,128)(2,1)S(1)} %copy-done.9), channel_id=1, source_target_pairs={{4,8},{6,10},{9,5},{11,7},{20,24},{22,26},{25,21},{27,23}} | collective-permute-start | bytes 786440 | tf_op jit(solution)/shard_map/ppermute | solution.py:333
  57.8 9.6 %collective-permute-start.22 = (bf16[16,64,128]{2,1,0:T(8,128)(2,1)S(1)}, bf16[16,64,128]{2,1,0:T(8,128)(2,1)S(1)}, u32[]{:S(2)}, u32[]{:S(2)}) collective-permute-start(bf16[16,64,128]{2,1,0:T(8,128)(2,1)S(1)} %copy-done.9), channel_id=1, source_target_pairs={{5,8},{7,10},{8,5},{10,7},{21,24},{23,26},{24,21},{26,23}} | collective-permute-start | bytes 786440 | tf_op jit(solution)/shard_map/ppermute | solution.py:333
  63.5 21.9 %collective-permute-start.11 = (bf16[16,64,128]{2,1,0:T(8,128)(2,1)S(1)}, bf16[16,64,128]{2,1,0:T(8,128)(2,1)S(1)}, u32[]{:S(2)}, u32[]{:S(2)}) collective-permute-start(bf16[16,64,128]{2,1,0:T(8,128)(2,1)S(1)} %get-tuple-element.25), channel_id=1, source_target_pairs={{6,2},{7,3},{8,12},{9,13},{4,6},{5,7},{10,8},{11,9},{22,18},{23,19... | collective-permute-start | bytes 786440 | tf_op jit(solution)/shard_map/ppermute | solution.py:333
  64.8 22.8 %collective-permute-start.12 = (bf16[16,64,128]{2,1,0:T(8,128)(2,1)S(1)}, bf16[16,64,128]{2,1,0:T(8,128)(2,1)S(1)}, u32[]{:S(2)}, u32[]{:S(2)}) collective-permute-start(bf16[16,64,128]{2,1,0:T(8,128)(2,1)S(1)} %get-tuple-element.26.refs_3_), channel_id=1, source_target_pairs={{4,2},{5,3},{10,12},{11,13},{20,18},{21,19},{26,28},{27,29}} | collective-permute-start | bytes 786440 | tf_op jit(solution)/shard_map/ppermute | solution.py:333
  66.1 24.8 %collective-permute-start.15 = (bf16[16,64,128]{2,1,0:T(8,128)(2,1)S(1)}, bf16[16,64,128]{2,1,0:T(8,128)(2,1)S(1)}, u32[]{:S(2)}, u32[]{:S(2)}) collective-permute-start(bf16[16,64,128]{2,1,0:T(8,128)(2,1)S(1)} %get-tuple-element.28), channel_id=1, source_target_pairs={{6,2},{7,3},{8,12},{9,13},{4,6},{5,7},{10,8},{11,9},{22,18},{23,19... | collective-permute-start | bytes 786440 | tf_op jit(solution)/shard_map/ppermute | solution.py:333
  67.4 25.8 %collective-permute-start.16 = (bf16[16,64,128]{2,1,0:T(8,128)(2,1)S(1)}, bf16[16,64,128]{2,1,0:T(8,128)(2,1)S(1)}, u32[]{:S(2)}, u32[]{:S(2)}) collective-permute-start(bf16[16,64,128]{2,1,0:T(8,128)(2,1)S(1)} %get-tuple-element.29.refs_6_), channel_id=1, source_target_pairs={{4,2},{5,3},{10,12},{11,13},{20,18},{21,19},{26,28},{27,29}} | collective-permute-start | bytes 786440 | tf_op jit(solution)/shard_map/ppermute | solution.py:333
  85.3 11.2 %collective-permute-start.19 = (bf16[16,64,128]{2,1,0:T(8,128)(2,1)S(1)}, bf16[16,64,128]{2,1,0:T(8,128)(2,1)S(1)}, u32[]{:S(2)}, u32[]{:S(2)}) collective-permute-start(bf16[16,64,128]{2,1,0:T(8,128)(2,1)S(1)} %get-tuple-element.31), channel_id=1, source_target_pairs={{6,2},{7,3},{8,12},{9,13},{4,6},{5,7},{10,8},{11,9},{22,18},{23,19... | collective-permute-start | bytes 786440 | tf_op jit(solution)/shard_map/ppermute | solution.py:333
  87.6 10.4 %collective-permute-start.20 = (bf16[16,64,128]{2,1,0:T(8,128)(2,1)S(1)}, bf16[16,64,128]{2,1,0:T(8,128)(2,1)S(1)}, u32[]{:S(2)}, u32[]{:S(2)}) collective-permute-start(bf16[16,64,128]{2,1,0:T(8,128)(2,1)S(1)} %get-tuple-element.32.refs_9_), channel_id=1, source_target_pairs={{4,2},{5,3},{10,12},{11,13},{20,18},{21,19},{26,28},{27,29}} | collective-permute-start | bytes 786440 | tf_op jit(solution)/shard_map/ppermute | solution.py:333
  90.9 11.2 %collective-permute-start.23 = (bf16[16,64,128]{2,1,0:T(8,128)(2,1)S(1)}, bf16[16,64,128]{2,1,0:T(8,128)(2,1)S(1)}, u32[]{:S(2)}, u32[]{:S(2)}) collective-permute-start(bf16[16,64,128]{2,1,0:T(8,128)(2,1)S(1)} %get-tuple-element.34), channel_id=1, source_target_pairs={{6,2},{7,3},{8,12},{9,13},{4,6},{5,7},{10,8},{11,9},{22,18},{23,19... | collective-permute-start | bytes 786440 | tf_op jit(solution)/shard_map/ppermute | solution.py:333
  93.2 10.5 %collective-permute-start.24 = (bf16[16,64,128]{2,1,0:T(8,128)(2,1)S(1)}, bf16[16,64,128]{2,1,0:T(8,128)(2,1)S(1)}, u32[]{:S(2)}, u32[]{:S(2)}) collective-permute-start(bf16[16,64,128]{2,1,0:T(8,128)(2,1)S(1)} %get-tuple-element.35.refs_12_), channel_id=1, source_target_pairs={{4,2},{5,3},{10,12},{11,13},{20,18},{21,19},{26,28},{27,29}} | collective-permute-start | bytes 786440 | tf_op jit(solution)/shard_map/ppermute | solution.py:333
  (17 other events, 139.8 us)

commit v3 on v0

v3 whole, which is shorter than its diff:
```python
import functools

import jax
import jax.numpy as jnp
from jax import lax
from jax.experimental import pallas as pl
from jax.experimental.pallas import tpu as pltpu
from jax.sharding import PartitionSpec as P

EPS = 1e-05
VMEM = pl.BlockSpec(memory_space=pltpu.VMEM)
SMEM = pl.BlockSpec(memory_space=pltpu.SMEM)
HBM = pl.BlockSpec(memory_space=pltpu.HBM)
STEP = 16


def call(body, out_shape, in_specs, out_specs, scratch, limit=12):
    return pl.pallas_call(
        body,
        out_shape=out_shape,
        in_specs=in_specs,
        out_specs=out_specs,
        scratch_shapes=scratch,
        compiler_params=pltpu.CompilerParams(vmem_limit_bytes=limit * 1024 * 1024),
        cost_estimate=pl.CostEstimate(flops=1, bytes_accessed=1, transcendentals=0),
    )


def sigmoid(values):
    return 0.5 * jnp.tanh(0.5 * values) + 0.5


def dot(left, right, dims):
    return lax.dot_general(left, right, (dims, ((), ())), preferred_element_type=jnp.float32)


def split(values):
    high = values.astype(jnp.bfloat16)
    low = (values - high.astype(jnp.float32)).astype(jnp.bfloat16)
    return jnp.concatenate([high, low], axis=1)


def norm_body(pair_ref, mask_ref, gain_ref, shift_ref, *refs):
    out_ref, kept_ref, held, mask, gain_held, shift_held, sems = refs
    rows, cols, channels = out_ref.shape
    steps = rows // STEP
    span = lambda at: pl.ds(at * STEP, STEP)
    small = [
        pltpu.make_async_copy(mask_ref, mask, sems.at[steps]),
        pltpu.make_async_copy(gain_ref, gain_held, sems.at[steps + 1]),
        pltpu.make_async_copy(shift_ref, shift_held, sems.at[steps + 2]),
    ]
    copies = [
        pltpu.make_async_copy(pair_ref.at[span(at)], held.at[span(at)], sems.at[at])
        for at in range(steps)
    ]
    for copy in copies[:1] + small + copies[1:]:
        copy.start()
    ones = jnp.full((2 * channels, channels), 1.0 / channels, jnp.bfloat16)
    for copy in small:
        copy.wait()
    gain, shift = gain_held[...], shift_held[...]
    for at, copy in enumerate(copies):
        copy.wait()
        values = held[span(at)].reshape(STEP * cols, channels)
        centered = values - dot(split(values), ones, ((1,), (0,)))
        squares = (centered * centered).astype(jnp.bfloat16)
        spread = dot(squares, ones[:channels], ((1,), (0,)))
        normed = centered * lax.rsqrt(spread + EPS) * gain + shift
        out_ref[span(at)] = normed.astype(jnp.bfloat16).reshape(STEP, cols, channels)
        keep = mask[span(at)].astype(jnp.float32).T
        for row in range(STEP):
            tile = normed[row * cols : (row + 1) * cols] * keep[:, row : row + 1]
            kept_ref[at * STEP + row] = tile.astype(jnp.bfloat16)


def layer_norm(pair, mask, gain, shift):
    return call(
        norm_body,
        [jax.ShapeDtypeStruct(pair.shape, jnp.bfloat16)] * 2,
        [HBM] * 4,
        [VMEM] * 2,
        [
            pltpu.VMEM(pair.shape, jnp.float32),
            pltpu.VMEM(mask.shape, jnp.int32),
            pltpu.VMEM(gain.shape, jnp.float32),
            pltpu.VMEM(shift.shape, jnp.float32),
            pltpu.SemaphoreType.DMA((pair.shape[0] // STEP + 3,)),
        ],
        limit=58,
    )(pair, mask, gain, shift)


def gate_body(normed_ref, weight_ref, out_ref, held, sems):
    rows, cols, channels = normed_ref.shape
    weight = weight_ref[...]
    copies = []
    for at in range(rows // STEP):
        span = pl.ds(at * STEP, STEP)
        values = dot(normed_ref[span].reshape(STEP * cols, channels), weight, ((1,), (0,)))
        held[span] = sigmoid(values).reshape(STEP, cols, channels)
        copies.append(pltpu.make_async_copy(held.at[span], out_ref.at[span], sems.at[at]))
        copies[-1].start()
    for copy in copies:
        copy.wait()


def output_gate(normed, weight):
    return call(
        gate_body,
        jax.ShapeDtypeStruct(normed.shape, jnp.float32),
        [VMEM, VMEM],
        HBM,
        [
            pltpu.VMEM(normed.shape, jnp.float32),
            pltpu.SemaphoreType.DMA((normed.shape[0] // STEP,)),
        ],
    )(normed, weight)


def side_body(cases, flags_ref, weight_ref, *refs):
    tiles, outs, held = refs[: -1 - len(cases[0][1])], refs[-1 - len(cases[0][1]) : -1], refs[-1]
    rows, cols, channels = tiles[0].shape
    planes = channels // 2
    zero = jnp.zeros((cols, channels), jnp.bfloat16)

    def project(tile_ref, first, out_ref):
        count = out_ref.shape[0]
        weight = jnp.concatenate(
            [weight_ref[first : first + count], weight_ref[planes + first : planes + first + count]], axis=0
        )

        def part(at, carry):
            span = pl.ds(pl.multiple_of(at * STEP, STEP), STEP)
            normed = tile_ref[span]
            for row in range(0, STEP, 2):
                parts = []
                for tile in (normed[row], normed[row + 1]):
                    parts += [jnp.concatenate([tile, zero], 1), jnp.concatenate([zero, tile], 1)]
                both = dot(weight, jnp.concatenate(parts, axis=0), ((1,), (1,)))
                for more in range(2):
                    values = both[:, 2 * cols * more : 2 * cols * (more + 1)]
                    held[pl.ds(row + more, count, stride=STEP), :] = (
                        sigmoid(values[count:]) * values[:count]
                    )
            value = held[: count * STEP, :].reshape(count, STEP, 2 * cols)
            out_ref[:, span, :] = value.astype(jnp.bfloat16)
            return carry

        lax.fori_loop(0, rows // STEP, part, 0)

    def work(jobs):
        for tile, first, out, index in jobs:
            project(tiles[tile], first, outs[out] if index is None else outs[out].at[index])

    if len(cases) == 1:
        work(cases[0][0])
    else:
        for value, (jobs, _) in enumerate(cases):
            pl.when(flags_ref[0] == value)(functools.partial(work, jobs))


def side(cases, shapes, flags, weight, tiles):
    cases = [(jobs, shapes) for jobs in cases]
    rows, cols, channels = tiles[0].shape
    return call(
        functools.partial(side_body, cases),
        [jax.ShapeDtypeStruct(shape + (rows, 2 * cols), jnp.bfloat16) for shape in shapes],
        [SMEM] + [VMEM] * (1 + len(tiles)),
        [VMEM] * len(shapes),
        [pltpu.VMEM((channels // 2 * STEP, 2 * cols), jnp.float32)],
    )(flags, weight, *tiles)


def paired(tiles):
    low = lax.broadcasted_iota(jnp.int32, tiles[0].shape, 1) < tiles[0].shape[1] // 2
    zero = jnp.zeros(tiles[0].shape, jnp.bfloat16)
    first = jnp.concatenate([jnp.where(low, tile, zero) for tile in tiles], axis=1)
    second = jnp.concatenate([jnp.where(low, zero, tile) for tile in tiles], axis=1)
    return jnp.concatenate([first, second], axis=0)


def triangle_body(cases, flags_ref, *refs):
    left, right, out_ref = refs[:2], refs[2:-1], refs[-1]

    def work(places):
        for plane, place in enumerate(places):
            first = jnp.concatenate([ref[plane] for ref in left], axis=1)
            second = paired([right[at[0]][at[1:]] for at in place])
            value = dot(first, second, ((1,), (1,)))
            out_ref[plane] = value.astype(jnp.bfloat16)

    for case, places in enumerate(cases):
        pl.when(flags_ref[0] == case)(functools.partial(work, places))


def triangle(cases, flags, left, right):
    planes, rows, lanes = left[0].shape
    return call(
        functools.partial(triangle_body, cases),
        jax.ShapeDtypeStruct((planes, rows, 2 * rows), jnp.bfloat16),
        [SMEM] + [VMEM] * (2 + len(right)),
        VMEM,
        [],
    )(flags, *left, *right)


def served_body(which, start, flags_ref, *refs):
    mine, ends, right, outs = refs[:2], refs[2:4], refs[4:-2], refs[-2:]
    rows = mine[0].shape[1]
    tiles = right if len(right) == 2 else [right[0].at[0], right[0].at[1]]

    def work(firsts):
        for at in range(outs[0].shape[0]):
            both = [
                jnp.concatenate([ref[start + at] for ref in first], axis=1) for first in firsts
            ]
            second = paired([ref[at] for ref in tiles])
            value = dot(jnp.concatenate(both, axis=0), second, ((1,), (1,)))
            value = value.astype(jnp.bfloat16)
            outs[0][at] = value[:rows]
            outs[1][at] = value[rows:]

    @pl.when((flags_ref[0] == which) & (flags_ref[1] == 1))
    def _():
        work([ends, mine])

    @pl.when((flags_ref[0] == which) & (flags_ref[1] == 0))
    def _():
        work([mine, ends])


def served(which, start, flags, mine, ends, right):
    count, rows, lanes = right[0].shape[-3:]
    return call(
        functools.partial(served_body, which, start),
        [jax.ShapeDtypeStruct((count, rows, 2 * rows), jnp.bfloat16)] * 2,
        [SMEM] + [VMEM] * (4 + len(right)),
        [VMEM] * 2,
        [],
    )(flags, *mine, *ends, *right)


def finish_body(cases, flags_ref, *refs):
    parts, (gain_ref, shift_ref, weight_ref, gate_ref, out_ref) = refs[:-10], refs[-10:-5]
    total, held, made, gate, sems = refs[-5:]
    planes, _, lanes = total.shape
    rows = gate.shape[0]
    steps = rows // STEP
    width = lanes // 2
    weight = weight_ref[...]
    spans = [pl.ds(at * STEP, STEP) for at in range(steps)]
    loads = [
        pltpu.make_async_copy(gate_ref.at[span], gate.at[span], sems.at[at])
        for at, span in enumerate(spans)
    ]
    for load in loads:
        load.start()

    def mean(values):
        return (values + pltpu.roll(values, width, 1)) * (1.0 / (2 * planes))

    def part(at, carry):
        span = pl.ds(pl.multiple_of(at * STEP, STEP), STEP)
        for case, (first, second) in enumerate(cases):

            @pl.when(flags_ref[2] == case)
            def _():
                ones = [(index, at) for index in first for at in range(parts[index].shape[0])]
                twos = [(index, at) for index in second for at in range(parts[index].shape[0])]
                for plane in range(planes):
                    (one, here), (two, there) = ones[plane], twos[plane]
                    value = parts[one][here, span].astype(jnp.float32)
                    total[plane] = value + parts[two][there, span].astype(jnp.float32)

        added = jnp.zeros((STEP, lanes), jnp.float32)
        for plane in range(planes):
            added = added + total[plane]
        middle = mean(added)
        added = jnp.zeros((STEP, lanes), jnp.float32)
        for plane in range(planes):
            centered = total[plane] - middle
            added = added + centered * centered
        scale = lax.rsqrt(mean(added) + EPS)
        for plane in range(planes):
            normed = (total[plane] - middle) * scale * gain_ref[plane] + shift_ref[plane]
            held[pl.ds(plane, STEP, stride=planes), :] = normed
        pltpu.make_async_copy(gate_ref.at[span], gate.at[span], sems.at[at]).wait()
        for row in range(STEP):
            tile = held[row * planes : (row + 1) * planes, :].T.astype(jnp.bfloat16)
            update = dot(tile[:width], weight[:planes], ((1,), (0,)))
            update += dot(tile[width:], weight[planes:], ((1,), (0,)))
            made[at * STEP + row] = update * gate[at * STEP + row]
        pltpu.make_async_copy(made.at[span], out_ref.at[span], sems.at[steps + at]).start()
        return carry

    lax.fori_loop(0, steps, part, 0)
    for at, span in enumerate(spans):
        pltpu.make_async_copy(made.at[span], out_ref.at[span], sems.at[steps + at]).wait()


def finish(flags, cases, parts, gain, shift, weight, gate):
    planes, _, lanes = gain.shape
    rows = gate.shape[0]
    return call(
        functools.partial(finish_body, cases),
        jax.ShapeDtypeStruct(gate.shape, jnp.float32),
        [SMEM] + [VMEM] * (len(parts) + 3) + [HBM],
        HBM,
        [
            pltpu.VMEM((planes, STEP, lanes), jnp.float32),
            pltpu.VMEM((planes * STEP, lanes), jnp.float32),
            pltpu.VMEM(gate.shape, jnp.float32),
            pltpu.VMEM(gate.shape, jnp.float32),
            pltpu.SemaphoreType.DMA((2 * rows // STEP,)),
        ],
    )(flags, *parts, gain, shift, weight, gate)


def planes_of(vector, width):
    return jnp.repeat(vector.reshape(2, -1).T, width, axis=1)[:, None, :]


def arranged(weight):
    channels = weight.shape[0]
    weight = weight.reshape(channels, 2, 2, 2, channels // 2).transpose(1, 2, 4, 3, 0)
    return weight.reshape(2, channels, 2 * channels)


def per_device(
    mesh_rows,
    mesh_cols,
    pair,
    pair_mask,
    in_gain,
    in_bias,
    proj_weight,
    gate_weight,
    out_gain,
    out_bias,
    out_weight,
):
    rows, cols, channels = pair.shape
    planes = channels // 2
    row, col = lax.axis_index("rows"), lax.axis_index("cols")
    chip, core = col // 2, col % 2

    gain, shift = planes_of(out_gain, cols), planes_of(out_bias, cols)

    if mesh_rows == 4 and mesh_cols == 4:
        both = ("rows", "cols")
        at = lambda z, x, h: z * 4 + 2 * x + h
        places = [(z, x, h) for z in range(4) for x in range(2) for h in range(2)]
        whole = core == row % 2
        is_early, is_middle = chip == row // 2, (row == 1) | (row == 2)
        late = jnp.where(is_middle, 1, 2) + jnp.where(whole == is_middle, 0, 2)
        case = jnp.where(is_early, 0, late)
        flags = jnp.stack([whole, ~is_early, case]).astype(jnp.int32)
        flip = [(at(z, x, h), at(z, x, 1 - h)) for z, x, h in places]
        wholes = [place for place in places if place[2] == place[0] % 2]
        others = [place for place in places if place[2] != place[0] % 2]
        partners = [(at(z, x, h), at(z ^ 1, x, h)) for z, x, h in places]
        swap = lambda some: [(at(z, x, h), at(z, x, 1 - h)) for z, x, h in some]
        middles = lambda some: [place for place in some if place[0] in (1, 2)]
        straight = lambda some: [(at(z, x, h), at(3 - z, x, h)) for z, x, h in middles(some)]
        diagonal = lambda some: [(at(z, x, h), at(3 - z, x, 1 - h)) for z, x, h in middles(some)]
        owner = lambda z: 1 - z // 2
        early_pairs = [(at(z, x, h), at(z, 1 - x, h)) for z, x, h in places if x == owner(z)]
        first_pairs = lambda some: [
            (at(z, x, h), at(z ^ 1, x, h) if x == owner(z) else at(z, 1 - x, h))
            for z, x, h in middles(some)
        ]
        second_pairs = lambda some: [
            (at(z, x, h), at(z ^ 1, 1 - x, h)) for z, x, h in middles(some) if x != owner(z)
        ]
        move = lambda array, pairs: lax.ppermute(array, both, pairs)
        tie = lax.optimization_barrier
        full = [[(0, 0, 0, None)]]
        side_of = lambda column, tile: side(full, [(planes,)], flags, weights[column], [tile])

        normed, kept = layer_norm(pair, pair_mask, in_gain[None], in_bias[None])
        kept_partner = move(kept, partners)
        kept_other = move(kept, flip)
        kept, proj_weight = tie((kept, proj_weight))
        weights = arranged(proj_weight)
        (b_own,) = side_of(1, kept)
        near = [move(b_own, straight(wholes)), move(b_own, diagonal(others))]
        kept, b_own = tie((kept, b_own))
        (a_own,) = side_of(0, kept)
        (a_other,) = side_of(0, kept_other)
        (b_other,) = side([[], full[0]], [(planes,)], flags, weights[1], [kept_other])
        gate = output_gate(normed, gate_weight)
        kept_partner, a_own, a_other, b_other, gate, gain, shift = tie(
            (kept_partner, a_own, a_other, b_other, gate, gain, shift)
        )
        kept_partner_other = move(kept_partner, flip)
        (b_partner,) = side_of(1, kept_partner)
        far = [move(b_partner, straight(others)), move(b_partner, diagonal(wholes))]
        b_partner_other = move(b_partner, swap(wholes))
        kept_partner, b_partner, near = tie((kept_partner, b_partner, near))
        (a_end,) = side_of(0, kept_partner)
        kept_partner_other, a_end = tie((kept_partner_other, a_end))
        (a_end_other,) = side_of(0, kept_partner_other)
        b_partner, a_end, a_end_other = tie((b_partner, a_end, a_end_other))
        mine, ends = [a_own, a_other], [a_end, a_end_other]
        cases = [
            [[(2 * case + tile, plane) for tile in (0, 1)] for plane in range(planes)]
            for case in (0, 1)
        ]
        early = triangle(cases, flags, mine, [b_partner, b_partner_other, b_own, b_other])
        early_other = move(early, early_pairs)
        near, early = tie((near, early))
        parts = [early, early_other]
        one, two = served(0, 0, flags, mine, ends, near)
        parts += [move(one, first_pairs(others)), two, move(two, second_pairs(others))]
        far, parts = tie((far, parts[:1] + parts[2:])), [parts[1]]
        far, parts = far[0], far[1][:1] + parts + far[1][1:]
        one, two = served(1, 0, flags, mine, ends, far)
        parts += [move(one, first_pairs(wholes)), two, move(two, second_pairs(wholes))]
        cases = [([0], [1]), ([5], [6]), ([5], [7]), ([2], [3]), ([2], [4])]
    else:
        flags = jnp.zeros((3,), jnp.int32)
        normed, kept = layer_norm(pair, pair_mask, in_gain[None], in_bias[None])
        quarters = [[(0, planes // 4 * at, at, None) for at in range(4)]]
        shapes = [(planes // 4,)] * 4
        weights = arranged(proj_weight)
        pieces = side(quarters, shapes, flags, weights[1], [kept])
        lefts = side(quarters, shapes, flags, weights[0], [kept])
        gate = output_gate(normed, gate_weight)
        places = [[[(0, plane), (1, plane)] for plane in range(planes // 4)]]
        sums = []
        for piece, left in zip(pieces, lefts):
            gathered = lax.all_gather(piece, "rows")
            zero = jnp.zeros_like(left)
            product = jnp.stack(
                [
                    triangle(places, flags, [left, zero], [gathered[at], zero])
                    for at in range(mesh_rows)
                ]
            )
            gathered = lax.all_to_all(product, "cols", 0, 0, tiled=True)
            sums.append(jnp.sum(gathered.astype(jnp.float32), axis=0))
        total = jnp.concatenate(sums, axis=0)
        parts, cases = [total, jnp.zeros_like(total)], [([0], [1])]
    return finish(flags, cases, parts, gain, shift, out_weight, gate)


def solution(mesh):
    tile = P(("groups", "rows"), "cols", None)
    return jax.shard_map(
        functools.partial(per_device, mesh.shape["rows"], mesh.shape["cols"]),
        mesh=mesh,
        in_specs=(tile, P(("groups", "rows"), "cols")) + (P(),) * 7,
        out_specs=tile,
        check_vma=False,
    )
```

time: 188 us -> 91.2 us (0.49); the launches traced: 185 us -> 89.9 us
  local copies, waits for them, and re-layouts: 48.9 us -> 2.38 us
  Pallas kernels: 0 us -> 39.6 us
  blocking collectives: 36.4 us -> 0 us
  waiting for transfers between devices: 57.9 us -> 32.2 us
  between operations: 13.6 us -> 0.51 us
  matrix products: 11.5 us -> 0 us
  other arithmetic: 11.2 us -> 0.08 us
  starting transfers between devices: 5.09 us -> 15.2 us
    all_gather x1 -> x0, waiting for transfers between devices: 47.1 us -> none  [per_device(): lax.all_gather(moved_b, 'rows', axis=1, tiled=True)]
    pallas_call x0 -> x13, Pallas kernels: none -> 39.6 us  [the longest x7 21.1 us: side(): call(functools.partial(side_body, cases), [jax.ShapeDtypeStruct(shape + (...]
    all_to_all x2 -> x0, blocking collectives: 36.4 us -> none  [the longest x1 18.7 us: per_device(): lax.all_to_all(side_a, 'cols', split_axis=0, concat_axis=2, tiled=True)]
    ppermute x0 -> x13, waiting for transfers between devices: none -> 32.2 us  [per_device(): move = lambda array, pairs: lax.ppermute(array, both, pairs)]
    unnamed x28 -> x16, local copies, waits for them, and re-layouts: 19 us -> 1.28 us
    convert_element_type x4 -> x0, local copies, waits for them, and re-layouts: 15.5 us -> none  [the longest x2 7.87 us: gated_side(): return gated.astype(jnp.bfloat16)]
    ppermute x0 -> x13, starting transfers between devices: none -> 15.2 us  [per_device(): move = lambda array, pairs: lax.ppermute(array, both, pairs)]
    all_to_all x4 -> x0, local copies, waits for them, and re-layouts: 14.4 us -> none  [the longest x2 7.59 us: per_device(): lax.all_to_all(side_b, 'cols', split_axis=0, concat_axis=2, tiled=True)]
  transfers between devices with their start and end apart: 2 -> 13, of which waited for: 2 -> 4; matrix products, arithmetic and copies ran while one was open for 8% -> 1% of each run, Pallas kernels for 0% -> 32%
where the time goes in v3:
time: 91.2 us; the launch traced here: 89.9 us
  Pallas kernels  39.6 us (43%)
  waiting for transfers between devices  32.2 us (35%)
  starting transfers between devices  15.2 us (17%)
  local copies, waits for them, and re-layouts  2.38 us (3%)
    ppermute x13, waiting for transfers between devices, per_device(): move = lambda array, pairs: lax.ppermute(array, both, pairs)  32.2 us
    pallas_call x7, Pallas kernels, side(): call(functools.partial(side_body, cases), [jax.ShapeDtypeStruct(shape + (...  21.1 us
    ppermute x13, starting transfers between devices, per_device(): move = lambda array, pairs: lax.ppermute(array, both, pairs)  15.2 us
    pallas_call x1, Pallas kernels, finish(): call(functools.partial(finish_body, cases), jax.ShapeDtypeStruct(gate.sha...  6.04 us
    pallas_call x1, Pallas kernels, layer_norm(): call(norm_body, [jax.ShapeDtypeStruct(pair.shape, jnp.bfloat16)] * 2, [HB...  4.72 us
    pallas_call x2, Pallas kernels, served(): call(functools.partial(served_body, which, start), [jax.ShapeDtypeStruct(...  3.6 us
    pallas_call x1, Pallas kernels, triangle(): call(functools.partial(triangle_body, cases), jax.ShapeDtypeStruct((plane...  2.83 us
  transfers between devices with their start and end apart: 13, of which 4 were waited for; matrix products, arithmetic and copies ran while one was open for 1% of the time, Pallas kernels for 32%

profile of v3, /device:TPU:7, one launch (start us, length us, event | category | flops | bytes accessed | tf_op | source)
XLA Modules:
  0.0 89.9 jit_solution(4373838593755396355)
XLA Ops:
  0.0 4.7 %shard_map.91 = (bf16[64,64,128]{2,1,0:T(8,128)(2,1)}, bf16[64,64,128]{2,1,0:T(8,128)(2,1)}) custom-call(f32[64,64,128]{2,1,0:T(8,128)} %pair_ref.1, s32[64,64]{1,0:T(8,128)} %mask_ref.1, f32[1,128]{1,0:T(1,128)} %bitcast.32, f32[1,128]{1,0:T(1,128)} %bitcast.33), custom_call_target="tpu_custom_call" | custom-call | flops 1 | bytes 1 | tf_op jit(solution)/shard_map/pallas_call | solution.py:78
  5.5 1.3 %collective-permute-start = (bf16[64,64,128]{2,1,0:T(8,128)(2,1)}, bf16[64,64,128]{2,1,0:T(8,128)(2,1)}, u32[]{:S(2)}, u32[]{:S(2)}) collective-permute-start(bf16[64,64,128]{2,1,0:T(8,128)(2,1)} %get-tuple-element.43.refs_0_), channel_id=1, source_target_pairs={{0,4},{1,5},{2,6},{3,7},{4,0},{5,1},{6,2},{7,3},{8,12},{9,13},{10,... | collective-permute-start | bytes 3145736 | tf_op jit(solution)/shard_map/ppermute | solution.py:376
  7.1 1.2 %copy-done = bf16[64,64,128]{2,1,0:T(8,128)(2,1)S(1)} copy-done((bf16[64,64,128]{2,1,0:T(8,128)(2,1)S(1)}, bf16[64,64,128]{2,1,0:T(8,128)(2,1)}, u32[]{:S(2)}) %copy-start) | copy-done | bytes 1048600
  8.3 3.8 %shard_map.92.refs_4_ = bf16[64,64,128]{2,1,0:T(8,128)(2,1)} custom-call(s32[3]{0:T(128)S(1)} %pad_add_fusion.flags_ref, bf16[128,256]{1,0:T(8,128)(2,1)S(1)} %bitcast.24, bf16[64,64,128]{2,1,0:T(8,128)(2,1)S(1)} %copy-done), custom_call_target="tpu_custom_call" | custom-call | flops 1 | bytes 1 | tf_op jit(solution)/shard_map/pallas_call | solution.py:166
  12.1 1.6 %collective-permute-start.4 = (bf16[64,64,128]{2,1,0:T(8,128)(2,1)}, bf16[64,64,128]{2,1,0:T(8,128)(2,1)}, u32[]{:S(2)}, u32[]{:S(2)}) collective-permute-start(bf16[64,64,128]{2,1,0:T(8,128)(2,1)} %shard_map.92.refs_4_), channel_id=1, source_target_pairs={{5,9},{7,11},{8,4},{10,6},{21,25},{23,27},{24,20},{26,22}} | collective-permute-start | bytes 3145736 | tf_op jit(solution)/shard_map/ppermute | solution.py:376
  13.8 1.6 %collective-permute-start.5 = (bf16[64,64,128]{2,1,0:T(8,128)(2,1)}, bf16[64,64,128]{2,1,0:T(8,128)(2,1)}, u32[]{:S(2)}, u32[]{:S(2)}) collective-permute-start(bf16[64,64,128]{2,1,0:T(8,128)(2,1)} %shard_map.92.refs_4_), channel_id=1, source_target_pairs={{4,9},{6,11},{9,4},{11,6},{20,25},{22,27},{25,20},{27,22}} | collective-permute-start | bytes 3145736 | tf_op jit(solution)/shard_map/ppermute | solution.py:376
  15.5 2.8 %shard_map.93.refs_0_ = bf16[64,64,128]{2,1,0:T(8,128)(2,1)S(1)} custom-call(s32[3]{0:T(128)S(1)} %pad_add_fusion.flags_ref, bf16[128,256]{1,0:T(8,128)(2,1)S(1)} %bitcast.20, bf16[64,64,128]{2,1,0:T(8,128)(2,1)S(1)} %copy-done), custom_call_target="tpu_custom_call" | custom-call | flops 1 | bytes 1 | tf_op jit(solution)/shard_map/pallas_call | solution.py:166
  18.4 1.3 %shard_map.96.refs_11_ = f32[64,64,128]{2,1,0:T(8,128)S(1)} custom-call(bf16[64,64,128]{2,1,0:T(8,128)(2,1)S(1)} %copy-done.1, bf16[128,128]{1,0:T(8,128)(2,1)S(1)} %copy-done.2), custom_call_target="tpu_custom_call" | custom-call | flops 1 | bytes 1 | tf_op jit(solution)/shard_map/pallas_call | solution.py:109
  20.6 3.5 %shard_map.94.refs_1_ = bf16[64,64,128]{2,1,0:T(8,128)(2,1)S(1)} custom-call(s32[3]{0:T(128)S(1)} %pad_add_fusion.flags_ref, bf16[128,256]{1,0:T(8,128)(2,1)S(1)} %bitcast.21, bf16[64,64,128]{2,1,0:T(8,128)(2,1)} %collective-permute-done.1.refs_0_), custom_call_target="tpu_custom_call" | custom-call | flops 1 | bytes 1 | tf_op jit(solution)/shard_map/pallas_call | solution.py:166
  24.1 1.2 %shard_map.95.refs_5_ = bf16[64,64,128]{2,1,0:T(8,128)(2,1)S(1)} custom-call(s32[3]{0:T(128)S(1)} %pad_add_fusion.flags_ref, bf16[128,256]{1,0:T(8,128)(2,1)S(1)} %bitcast.25, bf16[64,64,128]{2,1,0:T(8,128)(2,1)} %collective-permute-done.1.refs_0_), custom_call_target="tpu_custom_call" | custom-call | flops 1 | bytes 1 | tf_op jit(solution)/shard_map/pallas_call | solution.py:166
  25.3 5.2 %collective-permute-done.refs_0_ = bf16[64,64,128]{2,1,0:T(8,128)(2,1)} collective-permute-done((bf16[64,64,128]{2,1,0:T(8,128)(2,1)}, bf16[64,64,128]{2,1,0:T(8,128)(2,1)}, u32[]{:S(2)}, u32[]{:S(2)}) %collective-permute-start) | collective-permute-done | bytes 1048608 | tf_op jit(solution)/shard_map/ppermute | solution.py:376
  31.4 3.5 %shard_map.97.refs_2_ = bf16[64,64,128]{2,1,0:T(8,128)(2,1)S(1)} custom-call(s32[3]{0:T(128)S(1)} %pad_add_fusion.flags_ref, bf16[128,256]{1,0:T(8,128)(2,1)S(1)} %bitcast.26, bf16[64,64,128]{2,1,0:T(8,128)(2,1)} %collective-permute-done.refs_0_), custom_call_target="tpu_custom_call" | custom-call | flops 1 | bytes 1 | tf_op jit(solution)/shard_map/pallas_call | solution.py:166
  34.9 1.3 %collective-permute-start.7 = (bf16[64,64,128]{2,1,0:T(8,128)(2,1)S(1)}, bf16[64,64,128]{2,1,0:T(8,128)(2,1)S(1)}, u32[]{:S(2)}, u32[]{:S(2)}) collective-permute-start(bf16[64,64,128]{2,1,0:T(8,128)(2,1)S(1)} %shard_map.97.refs_2_), channel_id=1, source_target_pairs={{0,1},{2,3},{5,4},{7,6},{8,9},{10,11},{13,12},{15,14},{16,17},{18,... | collective-permute-start | bytes 3145736 | tf_op jit(solution)/shard_map/ppermute | solution.py:376
  37.7 3.5 %shard_map.98.refs_2_ = bf16[64,64,128]{2,1,0:T(8,128)(2,1)S(1)} custom-call(s32[3]{0:T(128)S(1)} %pad_add_fusion.flags_ref, bf16[128,256]{1,0:T(8,128)(2,1)S(1)} %bitcast.22, bf16[64,64,128]{2,1,0:T(8,128)(2,1)} %collective-permute-done.refs_0_), custom_call_target="tpu_custom_call" | custom-call | flops 1 | bytes 1 | tf_op jit(solution)/shard_map/pallas_call | solution.py:166
  41.2 2.8 %shard_map.99.refs_3_ = bf16[64,64,128]{2,1,0:T(8,128)(2,1)S(1)} custom-call(s32[3]{0:T(128)S(1)} %pad_add_fusion.flags_ref, bf16[128,256]{1,0:T(8,128)(2,1)S(1)} %bitcast.23, bf16[64,64,128]{2,1,0:T(8,128)(2,1)S(1)} %collective-permute-done.6.refs_0_), custom_call_target="tpu_custom_call" | custom-call | flops 1 | bytes 1 | tf_op jit(solution)/shard_map/pallas_call | solution.py:166
  44.0 2.8 %shard_map.100.refs_0_ = bf16[64,64,128]{2,1,0:T(8,128)(2,1)S(1)} custom-call(s32[3]{0:T(128)S(1)} %pad_add_fusion.flags_ref, bf16[64,64,128]{2,1,0:T(8,128)(2,1)S(1)} %shard_map.93.refs_0_, bf16[64,64,128]{2,1,0:T(8,128)(2,1)S(1)} %shard_map.94.refs_1_, bf16[64,64,128]{2,1,0:T(8,128)(2,1)S(1)} %shard_map.97.refs_2_, ...), custom_call_target="tpu_custom_call" | custom-call | flops 1 | bytes 1 | tf_op jit(solution)/shard_map/pallas_call | solution.py:199
  46.8 3.0 %shard_map.101 = (bf16[64,64,128]{2,1,0:T(8,128)(2,1)S(1)}, bf16[64,64,128]{2,1,0:T(8,128)(2,1)S(1)}) custom-call(s32[3]{0:T(128)S(1)} %pad_add_fusion.flags_ref, bf16[64,64,128]{2,1,0:T(8,128)(2,1)S(1)} %shard_map.93.refs_0_, bf16[64,64,128]{2,1,0:T(8,128)(2,1)S(1)} %shard_map.94.refs_1_, bf16[64,64,128]{2,1,0:T(8,128)(2,1)S(1)} %shard_map.98.refs_2_, ...), custom_call_target="tpu_custom_call" | custom-call | flops 1 | bytes 1 | tf_op jit(solution)/shard_map/pallas_call | solution.py:235
  51.4 2.2 %collective-permute-start.10 = (bf16[64,64,128]{2,1,0:T(8,128)(2,1)S(1)}, bf16[64,64,128]{2,1,0:T(8,128)(2,1)S(1)}, u32[]{:S(2)}, u32[]{:S(2)}) collective-permute-start(bf16[64,64,128]{2,1,0:T(8,128)(2,1)S(1)} %shard_map.100.refs_0_), channel_id=1, source_target_pairs={{2,0},{3,1},{6,4},{7,5},{8,10},{9,11},{12,14},{13,15},{18,16},{19,... | collective-permute-start | bytes 3145736 | tf_op jit(solution)/shard_map/ppermute | solution.py:376
  54.2 1.3 %collective-permute-start.11 = (bf16[64,64,128]{2,1,0:T(8,128)(2,1)S(1)}, bf16[64,64,128]{2,1,0:T(8,128)(2,1)S(1)}, u32[]{:S(2)}, u32[]{:S(2)}) collective-permute-start(bf16[64,64,128]{2,1,0:T(8,128)(2,1)S(1)} %get-tuple-element.70), channel_id=1, source_target_pairs={{5,7},{7,3},{8,12},{10,8},{21,23},{23,19},{24,28},{26,24}} | collective-permute-start | bytes 3145736 | tf_op jit(solution)/shard_map/ppermute | solution.py:376
  55.5 1.3 %collective-permute-start.12 = (bf16[64,64,128]{2,1,0:T(8,128)(2,1)S(1)}, bf16[64,64,128]{2,1,0:T(8,128)(2,1)S(1)}, u32[]{:S(2)}, u32[]{:S(2)}) collective-permute-start(bf16[64,64,128]{2,1,0:T(8,128)(2,1)S(1)} %get-tuple-element.71.refs_6_), channel_id=1, source_target_pairs={{5,3},{10,12},{21,19},{26,28}} | collective-permute-start | bytes 3145736 | tf_op jit(solution)/shard_map/ppermute | solution.py:376
  56.8 19.4 %collective-permute-done.10.refs_1_ = bf16[64,64,128]{2,1,0:T(8,128)(2,1)S(1)} collective-permute-done((bf16[64,64,128]{2,1,0:T(8,128)(2,1)S(1)}, bf16[64,64,128]{2,1,0:T(8,128)(2,1)S(1)}, u32[]{:S(2)}, u32[]{:S(2)}) %collective-permute-start.10) | collective-permute-done | bytes 1048608 | tf_op jit(solution)/shard_map/ppermute | solution.py:376
  76.2 5.0 %collective-permute-done.11.refs_5_ = bf16[64,64,128]{2,1,0:T(8,128)(2,1)S(1)} collective-permute-done((bf16[64,64,128]{2,1,0:T(8,128)(2,1)S(1)}, bf16[64,64,128]{2,1,0:T(8,128)(2,1)S(1)}, u32[]{:S(2)}, u32[]{:S(2)}) %collective-permute-start.11) | collective-permute-done | bytes 1048608 | tf_op jit(solution)/shard_map/ppermute | solution.py:376
  81.2 2.5 %collective-permute-done.12.refs_7_ = bf16[64,64,128]{2,1,0:T(8,128)(2,1)S(1)} collective-permute-done((bf16[64,64,128]{2,1,0:T(8,128)(2,1)S(1)}, bf16[64,64,128]{2,1,0:T(8,128)(2,1)S(1)}, u32[]{:S(2)}, u32[]{:S(2)}) %collective-permute-start.12) | collective-permute-done | bytes 1048608 | tf_op jit(solution)/shard_map/ppermute | solution.py:376
  83.7 6.0 %shard_map.103 = f32[64,64,128]{2,1,0:T(8,128)} custom-call(s32[3]{0:T(128)S(1)} %pad_add_fusion.flags_ref, bf16[64,64,128]{2,1,0:T(8,128)(2,1)S(1)} %shard_map.100.refs_0_, bf16[64,64,128]{2,1,0:T(8,128)(2,1)S(1)} %collective-permute-done.10.refs_1_, bf16[64,64,128]{2,1,0:T(8,128)(2,1)S(1)} %collective-permute-done.8.refs_2_, ...), custom_call_target="tpu_custom_call" | custom-call | flops 1 | bytes 1 | tf_op jit(solution)/shard_map/pallas_call | solution.py:305
  (44 shorter events, 6.3 us)
Async XLA Ops:
  0.0 6.8 %copy-start.4 = (bf16[128,512]{1,0:T(8,128)(2,1)S(1)}, bf16[128,512]{1,0:T(8,128)(2,1)}, u32[]{:S(2)}) copy-start(bf16[128,512]{1,0:T(8,128)(2,1)} %param.13) | copy-start | bytes 393220
  4.7 15.8 %collective-permute-start.1 = (bf16[64,64,128]{2,1,0:T(8,128)(2,1)}, bf16[64,64,128]{2,1,0:T(8,128)(2,1)}, u32[]{:S(2)}, u32[]{:S(2)}) collective-permute-start(bf16[64,64,128]{2,1,0:T(8,128)(2,1)} %get-tuple-element.43.refs_0_), channel_id=1, source_target_pairs={{0,1},{1,0},{2,3},{3,2},{4,5},{5,4},{6,7},{7,6},{8,9},{9,8},{10,11... | collective-permute-start | bytes 3145736 | tf_op jit(solution)/shard_map/ppermute | solution.py:376
  5.5 25.1 %collective-permute-start = (bf16[64,64,128]{2,1,0:T(8,128)(2,1)}, bf16[64,64,128]{2,1,0:T(8,128)(2,1)}, u32[]{:S(2)}, u32[]{:S(2)}) collective-permute-start(bf16[64,64,128]{2,1,0:T(8,128)(2,1)} %get-tuple-element.43.refs_0_), channel_id=1, source_target_pairs={{0,4},{1,5},{2,6},{3,7},{4,0},{5,1},{6,2},{7,3},{8,12},{9,13},{10,... | collective-permute-start | bytes 3145736 | tf_op jit(solution)/shard_map/ppermute | solution.py:376
  7.1 1.2 %copy-start = (bf16[64,64,128]{2,1,0:T(8,128)(2,1)S(1)}, bf16[64,64,128]{2,1,0:T(8,128)(2,1)}, u32[]{:S(2)}) copy-start(bf16[64,64,128]{2,1,0:T(8,128)(2,1)} %get-tuple-element.43.refs_0_) | copy-start | bytes 3145732
  8.3 10.0 %copy-start.1 = (bf16[64,64,128]{2,1,0:T(8,128)(2,1)S(1)}, bf16[64,64,128]{2,1,0:T(8,128)(2,1)}, u32[]{:S(2)}) copy-start(bf16[64,64,128]{2,1,0:T(8,128)(2,1)} %get-tuple-element.44.normed_ref) | copy-start | bytes 3145732
  8.3 10.0 %copy-start.2 = (bf16[128,128]{1,0:T(8,128)(2,1)S(1)}, bf16[128,128]{1,0:T(8,128)(2,1)}, u32[]{:S(2)}) copy-start(bf16[128,128]{1,0:T(8,128)(2,1)} %weight_ref.1) | copy-start | bytes 98308
  12.1 24.8 %collective-permute-start.4 = (bf16[64,64,128]{2,1,0:T(8,128)(2,1)}, bf16[64,64,128]{2,1,0:T(8,128)(2,1)}, u32[]{:S(2)}, u32[]{:S(2)}) collective-permute-start(bf16[64,64,128]{2,1,0:T(8,128)(2,1)} %shard_map.92.refs_4_), channel_id=1, source_target_pairs={{5,9},{7,11},{8,4},{10,6},{21,25},{23,27},{24,20},{26,22}} | collective-permute-start | bytes 3145736 | tf_op jit(solution)/shard_map/ppermute | solution.py:376
  13.8 23.9 %collective-permute-start.5 = (bf16[64,64,128]{2,1,0:T(8,128)(2,1)}, bf16[64,64,128]{2,1,0:T(8,128)(2,1)}, u32[]{:S(2)}, u32[]{:S(2)}) collective-permute-start(bf16[64,64,128]{2,1,0:T(8,128)(2,1)} %shard_map.92.refs_4_), channel_id=1, source_target_pairs={{4,9},{6,11},{9,4},{11,6},{20,25},{22,27},{25,20},{27,22}} | collective-permute-start | bytes 3145736 | tf_op jit(solution)/shard_map/ppermute | solution.py:376
  18.3 1.3 %copy-start.5 = (f32[128]{0:T(128)S(1)}, f32[128]{0:T(128)}, u32[]{:S(2)}) copy-start(f32[128]{0:T(128)} %param.15) | copy-start | bytes 1540
  18.3 1.8 %copy-start.6 = (f32[128]{0:T(128)S(1)}, f32[128]{0:T(128)}, u32[]{:S(2)}) copy-start(f32[128]{0:T(128)} %param.16) | copy-start | bytes 1540
  30.5 10.7 %collective-permute-start.6 = (bf16[64,64,128]{2,1,0:T(8,128)(2,1)}, bf16[64,64,128]{2,1,0:T(8,128)(2,1)S(1)}, u32[]{:S(2)}, u32[]{:S(2)}) collective-permute-start(bf16[64,64,128]{2,1,0:T(8,128)(2,1)} %collective-permute-done.refs_0_), channel_id=1, source_target_pairs={{0,1},{1,0},{2,3},{3,2},{4,5},{5,4},{6,7},{7,6},{8,9},{9,8},{10,11... | collective-permute-start | bytes 3145736 | tf_op jit(solution)/shard_map/ppermute | solution.py:376
  34.9 9.1 %collective-permute-start.7 = (bf16[64,64,128]{2,1,0:T(8,128)(2,1)S(1)}, bf16[64,64,128]{2,1,0:T(8,128)(2,1)S(1)}, u32[]{:S(2)}, u32[]{:S(2)}) collective-permute-start(bf16[64,64,128]{2,1,0:T(8,128)(2,1)S(1)} %shard_map.97.refs_2_), channel_id=1, source_target_pairs={{0,1},{2,3},{5,4},{7,6},{8,9},{10,11},{13,12},{15,14},{16,17},{18,... | collective-permute-start | bytes 3145736 | tf_op jit(solution)/shard_map/ppermute | solution.py:376
  36.2 17.4 %collective-permute-start.2 = (bf16[64,64,128]{2,1,0:T(8,128)(2,1)S(1)}, bf16[64,64,128]{2,1,0:T(8,128)(2,1)S(1)}, u32[]{:S(2)}, u32[]{:S(2)}) collective-permute-start(bf16[64,64,128]{2,1,0:T(8,128)(2,1)S(1)} %shard_map.97.refs_2_), channel_id=1, source_target_pairs={{4,8},{6,10},{9,5},{11,7},{20,24},{22,26},{25,21},{27,23}} | collective-permute-start | bytes 3145736 | tf_op jit(solution)/shard_map/ppermute | solution.py:376
  36.9 16.7 %collective-permute-start.3 = (bf16[64,64,128]{2,1,0:T(8,128)(2,1)S(1)}, bf16[64,64,128]{2,1,0:T(8,128)(2,1)S(1)}, u32[]{:S(2)}, u32[]{:S(2)}) collective-permute-start(bf16[64,64,128]{2,1,0:T(8,128)(2,1)S(1)} %shard_map.97.refs_2_), channel_id=1, source_target_pairs={{5,8},{7,10},{8,5},{10,7},{21,24},{23,26},{24,21},{26,23}} | collective-permute-start | bytes 3145736 | tf_op jit(solution)/shard_map/ppermute | solution.py:376
  49.9 3.7 %collective-permute-start.8 = (bf16[64,64,128]{2,1,0:T(8,128)(2,1)S(1)}, bf16[64,64,128]{2,1,0:T(8,128)(2,1)S(1)}, u32[]{:S(2)}, u32[]{:S(2)}) collective-permute-start(bf16[64,64,128]{2,1,0:T(8,128)(2,1)S(1)} %get-tuple-element.62), channel_id=1, source_target_pairs={{4,6},{6,2},{9,13},{11,9},{20,22},{22,18},{25,29},{27,25}} | collective-permute-start | bytes 3145736 | tf_op jit(solution)/shard_map/ppermute | solution.py:376
  50.6 33.1 %copy-start.3 = (bf16[128,128]{1,0:T(8,128)(2,1)S(1)}, bf16[128,128]{1,0:T(8,128)(2,1)}, u32[]{:S(2)}) copy-start(bf16[128,128]{1,0:T(8,128)(2,1)} %refs_10_.1) | copy-start | bytes 98308
  50.6 3.0 %collective-permute-start.9 = (bf16[64,64,128]{2,1,0:T(8,128)(2,1)S(1)}, bf16[64,64,128]{2,1,0:T(8,128)(2,1)S(1)}, u32[]{:S(2)}, u32[]{:S(2)}) collective-permute-start(bf16[64,64,128]{2,1,0:T(8,128)(2,1)S(1)} %get-tuple-element.66.refs_3_), channel_id=1, source_target_pairs={{4,2},{11,13},{20,18},{27,29}} | collective-permute-start | bytes 3145736 | tf_op jit(solution)/shard_map/ppermute | solution.py:376
  51.4 24.8 %collective-permute-start.10 = (bf16[64,64,128]{2,1,0:T(8,128)(2,1)S(1)}, bf16[64,64,128]{2,1,0:T(8,128)(2,1)S(1)}, u32[]{:S(2)}, u32[]{:S(2)}) collective-permute-start(bf16[64,64,128]{2,1,0:T(8,128)(2,1)S(1)} %shard_map.100.refs_0_), channel_id=1, source_target_pairs={{2,0},{3,1},{6,4},{7,5},{8,10},{9,11},{12,14},{13,15},{18,16},{19,... | collective-permute-start | bytes 3145736 | tf_op jit(solution)/shard_map/ppermute | solution.py:376
  54.2 27.0 %collective-permute-start.11 = (bf16[64,64,128]{2,1,0:T(8,128)(2,1)S(1)}, bf16[64,64,128]{2,1,0:T(8,128)(2,1)S(1)}, u32[]{:S(2)}, u32[]{:S(2)}) collective-permute-start(bf16[64,64,128]{2,1,0:T(8,128)(2,1)S(1)} %get-tuple-element.70), channel_id=1, source_target_pairs={{5,7},{7,3},{8,12},{10,8},{21,23},{23,19},{24,28},{26,24}} | collective-permute-start | bytes 3145736 | tf_op jit(solution)/shard_map/ppermute | solution.py:376
  55.5 28.3 %collective-permute-start.12 = (bf16[64,64,128]{2,1,0:T(8,128)(2,1)S(1)}, bf16[64,64,128]{2,1,0:T(8,128)(2,1)S(1)}, u32[]{:S(2)}, u32[]{:S(2)}) collective-permute-start(bf16[64,64,128]{2,1,0:T(8,128)(2,1)S(1)} %get-tuple-element.71.refs_6_), channel_id=1, source_target_pairs={{5,3},{10,12},{21,19},{26,28}} | collective-permute-start | bytes 3145736 | tf_op jit(solution)/shard_map/ppermute | solution.py:376

commit v4 on v3

--- a/solution.py
+++ b/solution.py
@@ -9,9 +9,16 @@
 
 EPS = 1e-05
 VMEM = pl.BlockSpec(memory_space=pltpu.VMEM)
-SMEM = pl.BlockSpec(memory_space=pltpu.SMEM)
 HBM = pl.BlockSpec(memory_space=pltpu.HBM)
 STEP = 16
+
+
+def place():
+    row, col = lax.axis_index("rows"), lax.axis_index("cols")
+    whole = col % 2 == row % 2
+    early, middle = col // 2 == row // 2, (row == 1) | (row == 2)
+    late = jnp.where(middle, 1, 2) + jnp.where(whole == middle, 0, 2)
+    return whole.astype(jnp.int32), ~early, jnp.where(early, 0, late)
 
 
 def call(body, out_shape, in_specs, out_specs, scratch, limit=12):
@@ -118,7 +125,7 @@
     )(normed, weight)
 
 
-def side_body(cases, flags_ref, weight_ref, *refs):
+def side_body(cases, weight_ref, *refs):
     tiles, outs, held = refs[: -1 - len(cases[0][1])], refs[-1 - len(cases[0][1]) : -1], refs[-1]
     rows, cols, channels = tiles[0].shape
     planes = channels // 2
@@ -147,7 +154,7 @@
             out_ref[:, span, :] = value.astype(jnp.bfloat16)
             return carry
 
-        lax.fori_loop(0, rows // STEP, part, 0)
+        lax.fori_loop(0, rows // STEP, part, 0, unroll=True)
 
     def work(jobs):
         for tile, first, out, index in jobs:
@@ -156,20 +163,21 @@
     if len(cases) == 1:
         work(cases[0][0])
     else:
+        whole = place()[0]
         for value, (jobs, _) in enumerate(cases):
-            pl.when(flags_ref[0] == value)(functools.partial(work, jobs))
-
-
-def side(cases, shapes, flags, weight, tiles):
+            pl.when(whole == value)(functools.partial(work, jobs))
+
+
+def side(cases, shapes, weight, tiles):
     cases = [(jobs, shapes) for jobs in cases]
     rows, cols, channels = tiles[0].shape
     return call(
         functools.partial(side_body, cases),
         [jax.ShapeDtypeStruct(shape + (rows, 2 * cols), jnp.bfloat16) for shape in shapes],
-        [SMEM] + [VMEM] * (1 + len(tiles)),
+        [VMEM] * (1 + len(tiles)),
         [VMEM] * len(shapes),
         [pltpu.VMEM((channels // 2 * STEP, 2 * cols), jnp.float32)],
-    )(flags, weight, *tiles)
+    )(weight, *tiles)
 
 
 def paired(tiles):
@@ -180,7 +188,7 @@
     return jnp.concatenate([first, second], axis=0)
 
 
-def triangle_body(cases, flags_ref, *refs):
+def triangle_body(cases, *refs):
     left, right, out_ref = refs[:2], refs[2:-1], refs[-1]
 
     def work(places):
@@ -190,58 +198,61 @@
             value = dot(first, second, ((1,), (1,)))
             out_ref[plane] = value.astype(jnp.bfloat16)
 
-    for case, places in enumerate(cases):
-        pl.when(flags_ref[0] == case)(functools.partial(work, places))
-
-
-def triangle(cases, flags, left, right):
+    if len(cases) == 1:
+        work(cases[0])
+    else:
+        whole = place()[0]
+        for case, places in enumerate(cases):
+            pl.when(whole == case)(functools.partial(work, places))
+
+
+def triangle(cases, left, right):
     planes, rows, lanes = left[0].shape
     return call(
         functools.partial(triangle_body, cases),
         jax.ShapeDtypeStruct((planes, rows, 2 * rows), jnp.bfloat16),
-        [SMEM] + [VMEM] * (2 + len(right)),
+        [VMEM] * (2 + len(right)),
         VMEM,
         [],
-    )(flags, *left, *right)
-
-
-def served_body(which, start, flags_ref, *refs):
-    mine, ends, right, outs = refs[:2], refs[2:4], refs[4:-2], refs[-2:]
-    rows = mine[0].shape[1]
-    tiles = right if len(right) == 2 else [right[0].at[0], right[0].at[1]]
+    )(*left, *right)
+
+
+def served_body(which, mine_ref, other_ref, ends_ref, right_ref, *outs):
+    mine, ends = [mine_ref, other_ref], [ends_ref.at[which], ends_ref.at[1 - which]]
+    rows = mine_ref.shape[1]
 
     def work(firsts):
         for at in range(outs[0].shape[0]):
-            both = [
-                jnp.concatenate([ref[start + at] for ref in first], axis=1) for first in firsts
-            ]
-            second = paired([ref[at] for ref in tiles])
+            both = [jnp.concatenate([ref[at] for ref in first], axis=1) for first in firsts]
+            second = paired([right_ref[0, at], right_ref[1, at]])
             value = dot(jnp.concatenate(both, axis=0), second, ((1,), (1,)))
             value = value.astype(jnp.bfloat16)
             outs[0][at] = value[:rows]
             outs[1][at] = value[rows:]
 
-    @pl.when((flags_ref[0] == which) & (flags_ref[1] == 1))
+    whole, owner, _ = place()
+
+    @pl.when((whole == which) & owner)
     def _():
         work([ends, mine])
 
-    @pl.when((flags_ref[0] == which) & (flags_ref[1] == 0))
+    @pl.when((whole == which) & ~owner)
     def _():
         work([mine, ends])
 
 
-def served(which, start, flags, mine, ends, right):
-    count, rows, lanes = right[0].shape[-3:]
-    return call(
-        functools.partial(served_body, which, start),
-        [jax.ShapeDtypeStruct((count, rows, 2 * rows), jnp.bfloat16)] * 2,
-        [SMEM] + [VMEM] * (4 + len(right)),
+def served(which, mine, ends, right):
+    planes, rows, _ = mine[0].shape
+    return call(
+        functools.partial(served_body, which),
+        [jax.ShapeDtypeStruct((planes, rows, 2 * rows), jnp.bfloat16)] * 2,
+        [VMEM] * 4,
         [VMEM] * 2,
         [],
-    )(flags, *mine, *ends, *right)
-
-
-def finish_body(cases, flags_ref, *refs):
+    )(*mine, ends, right)
+
+
+def finish_body(cases, *refs):
     parts, (gain_ref, shift_ref, weight_ref, gate_ref, out_ref) = refs[:-10], refs[-10:-5]
     total, held, made, gate, sems = refs[-5:]
     planes, _, lanes = total.shape
@@ -250,6 +261,7 @@
     width = lanes // 2
     weight = weight_ref[...]
     spans = [pl.ds(at * STEP, STEP) for at in range(steps)]
+    mine = place()[2] if len(cases) > 1 else 0
     loads = [
         pltpu.make_async_copy(gate_ref.at[span], gate.at[span], sems.at[at])
         for at, span in enumerate(spans)
@@ -264,7 +276,7 @@
         span = pl.ds(pl.multiple_of(at * STEP, STEP), STEP)
         for case, (first, second) in enumerate(cases):
 
-            @pl.when(flags_ref[2] == case)
+            @pl.when(mine == case)
             def _():
                 ones = [(index, at) for index in first for at in range(parts[index].shape[0])]
                 twos = [(index, at) for index in second for at in range(parts[index].shape[0])]
@@ -299,13 +311,13 @@
         pltpu.make_async_copy(made.at[span], out_ref.at[span], sems.at[steps + at]).wait()
 
 
-def finish(flags, cases, parts, gain, shift, weight, gate):
+def finish(cases, parts, gain, shift, weight, gate):
     planes, _, lanes = gain.shape
     rows = gate.shape[0]
     return call(
         functools.partial(finish_body, cases),
         jax.ShapeDtypeStruct(gate.shape, jnp.float32),
-        [SMEM] + [VMEM] * (len(parts) + 3) + [HBM],
+        [VMEM] * (len(parts) + 3) + [HBM],
         HBM,
         [
             pltpu.VMEM((planes, STEP, lanes), jnp.float32),
@@ -314,7 +326,7 @@
             pltpu.VMEM(gate.shape, jnp.float32),
             pltpu.SemaphoreType.DMA((2 * rows // STEP,)),
         ],
-    )(flags, *parts, gain, shift, weight, gate)
+    )(*parts, gain, shift, weight, gate)
 
 
 def planes_of(vector, width):
@@ -342,28 +354,21 @@
 ):
     rows, cols, channels = pair.shape
     planes = channels // 2
-    row, col = lax.axis_index("rows"), lax.axis_index("cols")
-    chip, core = col // 2, col % 2
-
     gain, shift = planes_of(out_gain, cols), planes_of(out_bias, cols)
 
     if mesh_rows == 4 and mesh_cols == 4:
         both = ("rows", "cols")
         at = lambda z, x, h: z * 4 + 2 * x + h
         places = [(z, x, h) for z in range(4) for x in range(2) for h in range(2)]
-        whole = core == row % 2
-        is_early, is_middle = chip == row // 2, (row == 1) | (row == 2)
-        late = jnp.where(is_middle, 1, 2) + jnp.where(whole == is_middle, 0, 2)
-        case = jnp.where(is_early, 0, late)
-        flags = jnp.stack([whole, ~is_early, case]).astype(jnp.int32)
         flip = [(at(z, x, h), at(z, x, 1 - h)) for z, x, h in places]
         wholes = [place for place in places if place[2] == place[0] % 2]
         others = [place for place in places if place[2] != place[0] % 2]
-        partners = [(at(z, x, h), at(z ^ 1, x, h)) for z, x, h in places]
-        swap = lambda some: [(at(z, x, h), at(z, x, 1 - h)) for z, x, h in some]
         middles = lambda some: [place for place in some if place[0] in (1, 2)]
-        straight = lambda some: [(at(z, x, h), at(3 - z, x, h)) for z, x, h in middles(some)]
-        diagonal = lambda some: [(at(z, x, h), at(3 - z, x, 1 - h)) for z, x, h in middles(some)]
+        partners = [(at(z, x, h), at(z ^ 1, x, h)) for z, x, h in wholes]
+        from_others = [(at(z, x, h), at(z, x, 1 - h)) for z, x, h in others]
+        straight = [(at(z, x, h), at(3 - z, x, h)) for z, x, h in middles(wholes)]
+        diagonal = [(at(z, x, h), at(3 - z, x, 1 - h)) for z, x, h in middles(others)]
+        two_hops = [(at(z, x, h), at(2 - z // 3, x, h)) for z, x, h in wholes if z in (0, 3)]
         owner = lambda z: 1 - z // 2
         early_pairs = [(at(z, x, h), at(z, 1 - x, h)) for z, x, h in places if x == owner(z)]
         first_pairs = lambda some: [
@@ -376,56 +381,52 @@
         move = lambda array, pairs: lax.ppermute(array, both, pairs)
         tie = lax.optimization_barrier
         full = [[(0, 0, 0, None)]]
-        side_of = lambda column, tile: side(full, [(planes,)], flags, weights[column], [tile])
+        side_of = lambda column, tile: side(full, [(planes,)], weights[column], [tile])
 
         normed, kept = layer_norm(pair, pair_mask, in_gain[None], in_bias[None])
-        kept_partner = move(kept, partners)
         kept_other = move(kept, flip)
+        near = [move(kept, straight), move(kept, diagonal)]
+        partner = move(kept, partners)
+        partner_other = move(kept_other, partners)
         kept, proj_weight = tie((kept, proj_weight))
         weights = arranged(proj_weight)
-        (b_own,) = side_of(1, kept)
-        near = [move(b_own, straight(wholes)), move(b_own, diagonal(others))]
+        tiles = [(0, 0, 0, 0), (1, 0, 0, 1)]
+        both_tiles = [(2, planes)]
+        (b_own,) = side([[], tiles], both_tiles, weights[1], [kept, kept_other])
         kept, b_own = tie((kept, b_own))
         (a_own,) = side_of(0, kept)
         (a_other,) = side_of(0, kept_other)
-        (b_other,) = side([[], full[0]], [(planes,)], flags, weights[1], [kept_other])
         gate = output_gate(normed, gate_weight)
-        kept_partner, a_own, a_other, b_other, gate, gain, shift = tie(
-            (kept_partner, a_own, a_other, b_other, gate, gain, shift)
+        near, a_own, a_other, b_own, gate, gain, shift = tie(
+            (near, a_own, a_other, b_own, gate, gain, shift)
         )
-        kept_partner_other = move(kept_partner, flip)
-        (b_partner,) = side_of(1, kept_partner)
-        far = [move(b_partner, straight(others)), move(b_partner, diagonal(wholes))]
-        b_partner_other = move(b_partner, swap(wholes))
-        kept_partner, b_partner, near = tie((kept_partner, b_partner, near))
-        (a_end,) = side_of(0, kept_partner)
-        kept_partner_other, a_end = tie((kept_partner_other, a_end))
-        (a_end_other,) = side_of(0, kept_partner_other)
-        b_partner, a_end, a_end_other = tie((b_partner, a_end, a_end_other))
-        mine, ends = [a_own, a_other], [a_end, a_end_other]
-        cases = [
-            [[(2 * case + tile, plane) for tile in (0, 1)] for plane in range(planes)]
-            for case in (0, 1)
-        ]
-        early = triangle(cases, flags, mine, [b_partner, b_partner_other, b_own, b_other])
+        far = move(b_own, two_hops)
+        partner, near = tie((partner, near))
+        (b_near,) = side([tiles, []], both_tiles, weights[1], near)
+        partner_other, partner, b_near = tie((partner_other, partner, b_near))
+        (a_end,) = side([tiles, []], both_tiles, weights[0], [partner, partner_other])
+        a_end_moved = move(a_end, from_others)
+        mine = [a_own, a_other]
+        one, two = served(0, mine, a_end, b_near)
+        near = [move(one, first_pairs(others)), two, move(two, second_pairs(others))]
+        partner_other, one = tie((partner_other, one))
+        (b_partner,) = side([tiles, []], both_tiles, weights[1], [partner, partner_other])
+        cases = [[[(case, 0, at), (case, 1, at)] for at in range(planes)] for case in (0, 1)]
+        early = triangle(cases, mine, [b_partner, b_own])
         early_other = move(early, early_pairs)
-        near, early = tie((near, early))
-        parts = [early, early_other]
-        one, two = served(0, 0, flags, mine, ends, near)
-        parts += [move(one, first_pairs(others)), two, move(two, second_pairs(others))]
-        far, parts = tie((far, parts[:1] + parts[2:])), [parts[1]]
-        far, parts = far[0], far[1][:1] + parts + far[1][1:]
-        one, two = served(1, 0, flags, mine, ends, far)
-        parts += [move(one, first_pairs(wholes)), two, move(two, second_pairs(wholes))]
+        far, near, early = tie((far, near, early))
+        a_end_moved, far = tie((a_end_moved, far))
+        one, two = served(1, mine, a_end_moved, far)
+        late = [move(one, first_pairs(wholes)), two, move(two, second_pairs(wholes))]
+        parts = [early, early_other] + near + late
         cases = [([0], [1]), ([5], [6]), ([5], [7]), ([2], [3]), ([2], [4])]
     else:
-        flags = jnp.zeros((3,), jnp.int32)
         normed, kept = layer_norm(pair, pair_mask, in_gain[None], in_bias[None])
         quarters = [[(0, planes // 4 * at, at, None) for at in range(4)]]
         shapes = [(planes // 4,)] * 4
         weights = arranged(proj_weight)
-        pieces = side(quarters, shapes, flags, weights[1], [kept])
-        lefts = side(quarters, shapes, flags, weights[0], [kept])
+        pieces = side(quarters, shapes, weights[1], [kept])
+        lefts = side(quarters, shapes, weights[0], [kept])
         gate = output_gate(normed, gate_weight)
         places = [[[(0, plane), (1, plane)] for plane in range(planes // 4)]]
         sums = []
@@ -434,7 +435,7 @@
             zero = jnp.zeros_like(left)
             product = jnp.stack(
                 [
-                    triangle(places, flags, [left, zero], [gathered[at], zero])
+                    triangle(places, [left, zero], [gathered[at], zero])
                     for at in range(mesh_rows)
                 ]
             )
@@ -442,7 +443,7 @@
             sums.append(jnp.sum(gathered.astype(jnp.float32), axis=0))
         total = jnp.concatenate(sums, axis=0)
         parts, cases = [total, jnp.zeros_like(total)], [([0], [1])]
-    return finish(flags, cases, parts, gain, shift, out_weight, gate)
+    return finish(cases, parts, gain, shift, out_weight, gate)
 
 
 def solution(mesh):

time: 91.2 us -> 85.5 us (0.938)
  Pallas kernels: 39.6 us -> 32.4 us
  local copies, waits for them, and re-layouts: 2.38 us -> 3.58 us
    pallas_call x7 -> x6, Pallas kernels: 21.1 us -> 17.8 us  [side(): call(functools.partial(side_body, cases), [jax.ShapeDtypeStruct(shape + (...]
    pallas_call x2, Pallas kernels: 3.6 us -> 1.32 us  [served(): call(functools.partial(served_body, which), [jax.ShapeDtypeStruct((planes...]
    unnamed x16, local copies, waits for them, and re-layouts: 1.28 us -> 2.48 us
    pallas_call x1, Pallas kernels: 2.83 us -> 1.81 us  [triangle(): call(functools.partial(triangle_body, cases), jax.ShapeDtypeStruct((plane...]
    ppermute x13 -> x12, waiting for transfers between devices: 32.2 us -> 32.5 us  [per_device(): move = lambda array, pairs: lax.ppermute(array, both, pairs)]
    ppermute x13 -> x12, starting transfers between devices: 15.2 us -> 15.1 us  [per_device(): move = lambda array, pairs: lax.ppermute(array, both, pairs)]
  transfers between devices with their start and end apart: 13 -> 12, of which waited for: 4 -> 5; matrix products, arithmetic and copies ran while one was open for 1% -> 1% of each run, Pallas kernels for 32% -> 26%
where the time goes in v4:
time: 85.5 us; the launch traced here: 84.1 us
  waiting for transfers between devices  32.5 us (38%)
  Pallas kernels  32.4 us (38%)
  starting transfers between devices  15.1 us (18%)
  local copies, waits for them, and re-layouts  3.58 us (4%)
    ppermute x12, waiting for transfers between devices, per_device(): move = lambda array, pairs: lax.ppermute(array, both, pairs)  32.5 us
    pallas_call x6, Pallas kernels, side(): call(functools.partial(side_body, cases), [jax.ShapeDtypeStruct(shape + (...  17.8 us
    ppermute x12, starting transfers between devices, per_device(): move = lambda array, pairs: lax.ppermute(array, both, pairs)  15.1 us
    pallas_call x1, Pallas kernels, finish(): call(functools.partial(finish_body, cases), jax.ShapeDtypeStruct(gate.sha...  5.47 us
    pallas_call x1, Pallas kernels, layer_norm(): call(norm_body, [jax.ShapeDtypeStruct(pair.shape, jnp.bfloat16)] * 2, [HB...  4.72 us
    unnamed x16, local copies, waits for them, and re-layouts  2.48 us
    pallas_call x1, Pallas kernels, triangle(): call(functools.partial(triangle_body, cases), jax.ShapeDtypeStruct((plane...  1.81 us
  transfers between devices with their start and end apart: 12, of which 5 were waited for; matrix products, arithmetic and copies ran while one was open for 1% of the time, Pallas kernels for 26%

profile of v4, /device:TPU:7, one launch (start us, length us, event | category | flops | bytes accessed | tf_op | source)
XLA Modules:
  0.0 84.1 jit_solution(15144119181018541931)
XLA Ops:
  0.0 4.7 %shard_map.91 = (bf16[64,64,128]{2,1,0:T(8,128)(2,1)}, bf16[64,64,128]{2,1,0:T(8,128)(2,1)}) custom-call(f32[64,64,128]{2,1,0:T(8,128)} %pair_ref.1, s32[64,64]{1,0:T(8,128)} %mask_ref.1, f32[1,128]{1,0:T(1,128)} %bitcast.28, f32[1,128]{1,0:T(1,128)} %bitcast.29), custom_call_target="tpu_custom_call" | custom-call | flops 1 | bytes 1 | tf_op jit(solution)/shard_map/pallas_call | solution.py:85
  5.5 1.6 %collective-permute-start = (bf16[64,64,128]{2,1,0:T(8,128)(2,1)}, bf16[64,64,128]{2,1,0:T(8,128)(2,1)}, u32[]{:S(2)}, u32[]{:S(2)}) collective-permute-start(bf16[64,64,128]{2,1,0:T(8,128)(2,1)} %get-tuple-element.40.refs_0_), channel_id=1, source_target_pairs={{5,9},{7,11},{8,4},{10,6},{21,25},{23,27},{24,20},{26,22}} | collective-permute-start | bytes 3145736 | tf_op jit(solution)/shard_map/ppermute | solution.py:381
  7.1 1.6 %collective-permute-start.1 = (bf16[64,64,128]{2,1,0:T(8,128)(2,1)}, bf16[64,64,128]{2,1,0:T(8,128)(2,1)}, u32[]{:S(2)}, u32[]{:S(2)}) collective-permute-start(bf16[64,64,128]{2,1,0:T(8,128)(2,1)} %get-tuple-element.40.refs_0_), channel_id=1, source_target_pairs={{4,9},{6,11},{9,4},{11,6},{20,25},{22,27},{25,20},{27,22}} | collective-permute-start | bytes 3145736 | tf_op jit(solution)/shard_map/ppermute | solution.py:381
  8.8 1.3 %collective-permute-start.5 = (bf16[64,64,128]{2,1,0:T(8,128)(2,1)}, bf16[64,64,128]{2,1,0:T(8,128)(2,1)}, u32[]{:S(2)}, u32[]{:S(2)}) collective-permute-start(bf16[64,64,128]{2,1,0:T(8,128)(2,1)} %get-tuple-element.40.refs_0_), channel_id=1, source_target_pairs={{0,4},{2,6},{5,1},{7,3},{8,12},{10,14},{13,9},{15,11},{16,20},{18,... | collective-permute-start | bytes 3145736 | tf_op jit(solution)/shard_map/ppermute | solution.py:381
  10.1 1.3 %collective-permute-start.4 = (bf16[64,64,128]{2,1,0:T(8,128)(2,1)S(1)}, bf16[64,64,128]{2,1,0:T(8,128)(2,1)}, u32[]{:S(2)}, u32[]{:S(2)}) collective-permute-start(bf16[64,64,128]{2,1,0:T(8,128)(2,1)S(1)} %collective-permute-done.2.refs_1_.refs_0_), channel_id=1, source_target_pairs={{0,4},{2,6},{5,1},{7,3},{8,12},{10,14},{13,9},{15,11},{16,20},{18,... | collective-permute-start | bytes 3145736 | tf_op jit(solution)/shard_map/ppermute | solution.py:381
  11.4 1.2 %copy-done.1 = bf16[64,64,128]{2,1,0:T(8,128)(2,1)S(1)} copy-done((bf16[64,64,128]{2,1,0:T(8,128)(2,1)S(1)}, bf16[64,64,128]{2,1,0:T(8,128)(2,1)}, u32[]{:S(2)}) %copy-start.1) | copy-done | bytes 1048600
  12.6 1.3 %shard_map.95.refs_11_ = f32[64,64,128]{2,1,0:T(8,128)S(1)} custom-call(bf16[64,64,128]{2,1,0:T(8,128)(2,1)S(1)} %copy-done.1, bf16[128,128]{1,0:T(8,128)(2,1)S(1)} %copy-done.2), custom_call_target="tpu_custom_call" | custom-call | flops 1 | bytes 1 | tf_op jit(solution)/shard_map/pallas_call | solution.py:116
  16.3 1.7 %shard_map.93.mine_ref.refs_0_ = bf16[64,64,128]{2,1,0:T(8,128)(2,1)S(1)} custom-call(bf16[128,256]{1,0:T(8,128)(2,1)S(1)} %bitcast.20, bf16[64,64,128]{2,1,0:T(8,128)(2,1)S(1)} %copy-done), custom_call_target="tpu_custom_call" | custom-call | flops 1 | bytes 1 | tf_op jit(solution)/shard_map/pallas_call | solution.py:174
  18.1 1.7 %shard_map.94.other_ref.refs_1_ = bf16[64,64,128]{2,1,0:T(8,128)(2,1)S(1)} custom-call(bf16[128,256]{1,0:T(8,128)(2,1)S(1)} %bitcast.21, bf16[64,64,128]{2,1,0:T(8,128)(2,1)S(1)} %collective-permute-done.2.refs_1_.refs_0_), custom_call_target="tpu_custom_call" | custom-call | flops 1 | bytes 1 | tf_op jit(solution)/shard_map/pallas_call | solution.py:174
  19.8 6.5 %collective-permute-done.5.refs_0_ = bf16[64,64,128]{2,1,0:T(8,128)(2,1)} collective-permute-done((bf16[64,64,128]{2,1,0:T(8,128)(2,1)}, bf16[64,64,128]{2,1,0:T(8,128)(2,1)}, u32[]{:S(2)}, u32[]{:S(2)}) %collective-permute-start.5) | collective-permute-done | bytes 1048608 | tf_op jit(solution)/shard_map/ppermute | solution.py:381
  27.1 4.8 %shard_map.96.right_ref = bf16[2,64,64,128]{3,2,1,0:T(8,128)(2,1)S(1)} custom-call(bf16[128,256]{1,0:T(8,128)(2,1)S(1)} %bitcast.18, bf16[64,64,128]{2,1,0:T(8,128)(2,1)} %collective-permute-done.refs_0_, bf16[64,64,128]{2,1,0:T(8,128)(2,1)} %collective-permute-done.1.refs_1_), custom_call_target="tpu_custom_call" | custom-call | flops 1 | bytes 1 | tf_op jit(solution)/shard_map/pallas_call | solution.py:174
  31.9 5.6 %collective-permute-done.4.refs_1_ = bf16[64,64,128]{2,1,0:T(8,128)(2,1)} collective-permute-done((bf16[64,64,128]{2,1,0:T(8,128)(2,1)S(1)}, bf16[64,64,128]{2,1,0:T(8,128)(2,1)}, u32[]{:S(2)}, u32[]{:S(2)}) %collective-permute-start.4) | collective-permute-done | bytes 1048608 | tf_op jit(solution)/shard_map/ppermute | solution.py:381
  37.6 4.8 %shard_map.97.ends_ref = bf16[2,64,64,128]{3,2,1,0:T(8,128)(2,1)S(1)} custom-call(bf16[128,256]{1,0:T(8,128)(2,1)S(1)} %bitcast.22, bf16[64,64,128]{2,1,0:T(8,128)(2,1)} %collective-permute-done.5.refs_0_, bf16[64,64,128]{2,1,0:T(8,128)(2,1)} %collective-permute-done.4.refs_1_), custom_call_target="tpu_custom_call" | custom-call | flops 1 | bytes 1 | tf_op jit(solution)/shard_map/pallas_call | solution.py:174
  42.4 1.4 %collective-permute-start.9 = (bf16[2,64,64,128]{3,2,1,0:T(8,128)(2,1)S(1)}, bf16[2,64,64,128]{3,2,1,0:T(8,128)(2,1)S(1)}, u32[]{:S(2)}, u32[]{:S(2)}) collective-permute-start(bf16[2,64,64,128]{3,2,1,0:T(8,128)(2,1)S(1)} %shard_map.97.ends_ref), channel_id=1, source_target_pairs={{1,0},{3,2},{4,5},{6,7},{9,8},{11,10},{12,13},{14,15},{17,16},{19,... | collective-permute-start | bytes 6291464 | tf_op jit(solution)/shard_map/ppermute | solution.py:381
  43.8 1.3 %shard_map.98 = (bf16[64,64,128]{2,1,0:T(8,128)(2,1)S(1)}, bf16[64,64,128]{2,1,0:T(8,128)(2,1)S(1)}) custom-call(bf16[64,64,128]{2,1,0:T(8,128)(2,1)S(1)} %shard_map.93.mine_ref.refs_0_, bf16[64,64,128]{2,1,0:T(8,128)(2,1)S(1)} %shard_map.94.other_ref.refs_1_, bf16[2,64,64,128]{3,2,1,0:T(8,128)(2,1)S(1)} %shard_map.97.ends_ref, ...), custom_call_target="tpu_custom_call" | custom-call | flops 1 | bytes 1 | tf_op jit(solution)/shard_map/pallas_call | solution.py:246
  46.6 4.8 %shard_map.99.refs_2_ = bf16[2,64,64,128]{3,2,1,0:T(8,128)(2,1)S(1)} custom-call(bf16[128,256]{1,0:T(8,128)(2,1)S(1)} %bitcast.19, bf16[64,64,128]{2,1,0:T(8,128)(2,1)} %collective-permute-done.5.refs_0_, bf16[64,64,128]{2,1,0:T(8,128)(2,1)} %collective-permute-done.4.refs_1_), custom_call_target="tpu_custom_call" | custom-call | flops 1 | bytes 1 | tf_op jit(solution)/shard_map/pallas_call | solution.py:174
  51.4 1.8 %shard_map.100.refs_0_ = bf16[64,64,128]{2,1,0:T(8,128)(2,1)S(1)} custom-call(bf16[64,64,128]{2,1,0:T(8,128)(2,1)S(1)} %shard_map.93.mine_ref.refs_0_, bf16[64,64,128]{2,1,0:T(8,128)(2,1)S(1)} %shard_map.94.other_ref.refs_1_, bf16[2,64,64,128]{3,2,1,0:T(8,128)(2,1)S(1)} %shard_map.99.refs_2_, bf16[2,64,64,128]{3,2,1,0:T(8,128)(2,1)S(1)} %shard_map.92.refs_3_), custom_call_target="tpu_custom_call" | custom-call | flops 1 | bytes 1 | tf_op jit(solution)/shard_map/pallas_call | solution.py:211
  53.2 2.2 %collective-permute-start.8 = (bf16[64,64,128]{2,1,0:T(8,128)(2,1)S(1)}, bf16[64,64,128]{2,1,0:T(8,128)(2,1)S(1)}, u32[]{:S(2)}, u32[]{:S(2)}) collective-permute-start(bf16[64,64,128]{2,1,0:T(8,128)(2,1)S(1)} %shard_map.100.refs_0_), channel_id=1, source_target_pairs={{2,0},{3,1},{6,4},{7,5},{8,10},{9,11},{12,14},{13,15},{18,16},{19,... | collective-permute-start | bytes 3145736 | tf_op jit(solution)/shard_map/ppermute | solution.py:381
  55.5 1.3 %collective-permute-start.10 = (bf16[64,64,128]{2,1,0:T(8,128)(2,1)S(1)}, bf16[64,64,128]{2,1,0:T(8,128)(2,1)S(1)}, u32[]{:S(2)}, u32[]{:S(2)}) collective-permute-start(bf16[64,64,128]{2,1,0:T(8,128)(2,1)S(1)} %get-tuple-element.64), channel_id=1, source_target_pairs={{5,7},{7,3},{8,12},{10,8},{21,23},{23,19},{24,28},{26,24}} | collective-permute-start | bytes 3145736 | tf_op jit(solution)/shard_map/ppermute | solution.py:381
  56.8 1.3 %collective-permute-start.11 = (bf16[64,64,128]{2,1,0:T(8,128)(2,1)S(1)}, bf16[64,64,128]{2,1,0:T(8,128)(2,1)S(1)}, u32[]{:S(2)}, u32[]{:S(2)}) collective-permute-start(bf16[64,64,128]{2,1,0:T(8,128)(2,1)S(1)} %get-tuple-element.65.refs_6_), channel_id=1, source_target_pairs={{5,3},{10,12},{21,19},{26,28}} | collective-permute-start | bytes 3145736 | tf_op jit(solution)/shard_map/ppermute | solution.py:381
  58.1 12.5 %collective-permute-done.8.refs_1_ = bf16[64,64,128]{2,1,0:T(8,128)(2,1)S(1)} collective-permute-done((bf16[64,64,128]{2,1,0:T(8,128)(2,1)S(1)}, bf16[64,64,128]{2,1,0:T(8,128)(2,1)S(1)}, u32[]{:S(2)}, u32[]{:S(2)}) %collective-permute-start.8) | collective-permute-done | bytes 1048608 | tf_op jit(solution)/shard_map/ppermute | solution.py:381
  70.7 5.2 %collective-permute-done.10.refs_5_ = bf16[64,64,128]{2,1,0:T(8,128)(2,1)S(1)} collective-permute-done((bf16[64,64,128]{2,1,0:T(8,128)(2,1)S(1)}, bf16[64,64,128]{2,1,0:T(8,128)(2,1)S(1)}, u32[]{:S(2)}, u32[]{:S(2)}) %collective-permute-start.10) | collective-permute-done | bytes 1048608 | tf_op jit(solution)/shard_map/ppermute | solution.py:381
  75.9 2.5 %collective-permute-done.11.refs_7_ = bf16[64,64,128]{2,1,0:T(8,128)(2,1)S(1)} collective-permute-done((bf16[64,64,128]{2,1,0:T(8,128)(2,1)S(1)}, bf16[64,64,128]{2,1,0:T(8,128)(2,1)S(1)}, u32[]{:S(2)}, u32[]{:S(2)}) %collective-permute-start.11) | collective-permute-done | bytes 1048608 | tf_op jit(solution)/shard_map/ppermute | solution.py:381
  78.4 5.5 %shard_map.102 = f32[64,64,128]{2,1,0:T(8,128)} custom-call(bf16[64,64,128]{2,1,0:T(8,128)(2,1)S(1)} %shard_map.100.refs_0_, bf16[64,64,128]{2,1,0:T(8,128)(2,1)S(1)} %collective-permute-done.8.refs_1_, bf16[64,64,128]{2,1,0:T(8,128)(2,1)S(1)} %collective-permute-done.6.refs_2_, bf16[64,64,128]{2,1,0:T(8,128)(2,1)S(1)} %get-tuple-element.59.refs_3_, ...), custom_call_target="tpu_custom_call" | custom-call | flops 1 | bytes 1 | tf_op jit(solution)/shard_map/pallas_call | solution.py:317
  (40 shorter events, 5.4 us)
Async XLA Ops:
  0.0 11.4 %copy-start.2 = (bf16[128,128]{1,0:T(8,128)(2,1)S(1)}, bf16[128,128]{1,0:T(8,128)(2,1)}, u32[]{:S(2)}) copy-start(bf16[128,128]{1,0:T(8,128)(2,1)} %weight_ref.1) | copy-start | bytes 98308
  0.0 13.9 %copy-start.4 = (bf16[128,512]{1,0:T(8,128)(2,1)S(1)}, bf16[128,512]{1,0:T(8,128)(2,1)}, u32[]{:S(2)}) copy-start(bf16[128,512]{1,0:T(8,128)(2,1)} %param.13) | copy-start | bytes 393220
  4.7 5.3 %collective-permute-start.2 = (bf16[64,64,128]{2,1,0:T(8,128)(2,1)}, bf16[64,64,128]{2,1,0:T(8,128)(2,1)S(1)}, u32[]{:S(2)}, u32[]{:S(2)}) collective-permute-start(bf16[64,64,128]{2,1,0:T(8,128)(2,1)} %get-tuple-element.40.refs_0_), channel_id=1, source_target_pairs={{0,1},{1,0},{2,3},{3,2},{4,5},{5,4},{6,7},{7,6},{8,9},{9,8},{10,11... | collective-permute-start | bytes 3145736 | tf_op jit(solution)/shard_map/ppermute | solution.py:381
  5.5 14.3 %collective-permute-start = (bf16[64,64,128]{2,1,0:T(8,128)(2,1)}, bf16[64,64,128]{2,1,0:T(8,128)(2,1)}, u32[]{:S(2)}, u32[]{:S(2)}) collective-permute-start(bf16[64,64,128]{2,1,0:T(8,128)(2,1)} %get-tuple-element.40.refs_0_), channel_id=1, source_target_pairs={{5,9},{7,11},{8,4},{10,6},{21,25},{23,27},{24,20},{26,22}} | collective-permute-start | bytes 3145736 | tf_op jit(solution)/shard_map/ppermute | solution.py:381
  7.1 12.7 %collective-permute-start.1 = (bf16[64,64,128]{2,1,0:T(8,128)(2,1)}, bf16[64,64,128]{2,1,0:T(8,128)(2,1)}, u32[]{:S(2)}, u32[]{:S(2)}) collective-permute-start(bf16[64,64,128]{2,1,0:T(8,128)(2,1)} %get-tuple-element.40.refs_0_), channel_id=1, source_target_pairs={{4,9},{6,11},{9,4},{11,6},{20,25},{22,27},{25,20},{27,22}} | collective-permute-start | bytes 3145736 | tf_op jit(solution)/shard_map/ppermute | solution.py:381
  8.8 17.6 %collective-permute-start.5 = (bf16[64,64,128]{2,1,0:T(8,128)(2,1)}, bf16[64,64,128]{2,1,0:T(8,128)(2,1)}, u32[]{:S(2)}, u32[]{:S(2)}) collective-permute-start(bf16[64,64,128]{2,1,0:T(8,128)(2,1)} %get-tuple-element.40.refs_0_), channel_id=1, source_target_pairs={{0,4},{2,6},{5,1},{7,3},{8,12},{10,14},{13,9},{15,11},{16,20},{18,... | collective-permute-start | bytes 3145736 | tf_op jit(solution)/shard_map/ppermute | solution.py:381
  10.1 27.5 %collective-permute-start.4 = (bf16[64,64,128]{2,1,0:T(8,128)(2,1)S(1)}, bf16[64,64,128]{2,1,0:T(8,128)(2,1)}, u32[]{:S(2)}, u32[]{:S(2)}) collective-permute-start(bf16[64,64,128]{2,1,0:T(8,128)(2,1)S(1)} %collective-permute-done.2.refs_1_.refs_0_), channel_id=1, source_target_pairs={{0,4},{2,6},{5,1},{7,3},{8,12},{10,14},{13,9},{15,11},{16,20},{18,... | collective-permute-start | bytes 3145736 | tf_op jit(solution)/shard_map/ppermute | solution.py:381
  11.4 1.2 %copy-start.1 = (bf16[64,64,128]{2,1,0:T(8,128)(2,1)S(1)}, bf16[64,64,128]{2,1,0:T(8,128)(2,1)}, u32[]{:S(2)}) copy-start(bf16[64,64,128]{2,1,0:T(8,128)(2,1)} %get-tuple-element.42.normed_ref) | copy-start | bytes 3145732
  12.6 1.6 %copy-start.5 = (f32[128]{0:T(128)S(1)}, f32[128]{0:T(128)}, u32[]{:S(2)}) copy-start(f32[128]{0:T(128)} %param.15) | copy-start | bytes 1540
  12.6 2.1 %copy-start.6 = (f32[128]{0:T(128)S(1)}, f32[128]{0:T(128)}, u32[]{:S(2)}) copy-start(f32[128]{0:T(128)} %param.16) | copy-start | bytes 1540
  15.1 1.2 %copy-start = (bf16[64,64,128]{2,1,0:T(8,128)(2,1)S(1)}, bf16[64,64,128]{2,1,0:T(8,128)(2,1)}, u32[]{:S(2)}) copy-start(bf16[64,64,128]{2,1,0:T(8,128)(2,1)} %get-tuple-element.40.refs_0_) | copy-start | bytes 3145732
  26.4 29.1 %collective-permute-start.3 = (bf16[2,64,64,128]{3,2,1,0:T(8,128)(2,1)S(1)}, bf16[2,64,64,128]{3,2,1,0:T(8,128)(2,1)S(1)}, u32[]{:S(2)}, u32[]{:S(2)}) collective-permute-start(bf16[2,64,64,128]{3,2,1,0:T(8,128)(2,1)S(1)} %shard_map.92.refs_3_), channel_id=1, source_target_pairs={{0,8},{2,10},{13,5},{15,7},{16,24},{18,26},{29,21},{31,23}} | collective-permute-start | bytes 6291464 | tf_op jit(solution)/shard_map/ppermute | solution.py:381
  42.4 13.1 %collective-permute-start.9 = (bf16[2,64,64,128]{3,2,1,0:T(8,128)(2,1)S(1)}, bf16[2,64,64,128]{3,2,1,0:T(8,128)(2,1)S(1)}, u32[]{:S(2)}, u32[]{:S(2)}) collective-permute-start(bf16[2,64,64,128]{3,2,1,0:T(8,128)(2,1)S(1)} %shard_map.97.ends_ref), channel_id=1, source_target_pairs={{1,0},{3,2},{4,5},{6,7},{9,8},{11,10},{12,13},{14,15},{17,16},{19,... | collective-permute-start | bytes 6291464 | tf_op jit(solution)/shard_map/ppermute | solution.py:381
  45.1 10.3 %collective-permute-start.6 = (bf16[64,64,128]{2,1,0:T(8,128)(2,1)S(1)}, bf16[64,64,128]{2,1,0:T(8,128)(2,1)S(1)}, u32[]{:S(2)}, u32[]{:S(2)}) collective-permute-start(bf16[64,64,128]{2,1,0:T(8,128)(2,1)S(1)} %get-tuple-element.54), channel_id=1, source_target_pairs={{4,6},{6,2},{9,13},{11,9},{20,22},{22,18},{25,29},{27,25}} | collective-permute-start | bytes 3145736 | tf_op jit(solution)/shard_map/ppermute | solution.py:381
  45.8 9.6 %collective-permute-start.7 = (bf16[64,64,128]{2,1,0:T(8,128)(2,1)S(1)}, bf16[64,64,128]{2,1,0:T(8,128)(2,1)S(1)}, u32[]{:S(2)}, u32[]{:S(2)}) collective-permute-start(bf16[64,64,128]{2,1,0:T(8,128)(2,1)S(1)} %get-tuple-element.59.refs_3_), channel_id=1, source_target_pairs={{4,2},{11,13},{20,18},{27,29}} | collective-permute-start | bytes 3145736 | tf_op jit(solution)/shard_map/ppermute | solution.py:381
  53.2 25.2 %copy-start.3 = (bf16[128,128]{1,0:T(8,128)(2,1)S(1)}, bf16[128,128]{1,0:T(8,128)(2,1)}, u32[]{:S(2)}) copy-start(bf16[128,128]{1,0:T(8,128)(2,1)} %refs_10_.1) | copy-start | bytes 98308
  53.2 17.5 %collective-permute-start.8 = (bf16[64,64,128]{2,1,0:T(8,128)(2,1)S(1)}, bf16[64,64,128]{2,1,0:T(8,128)(2,1)S(1)}, u32[]{:S(2)}, u32[]{:S(2)}) collective-permute-start(bf16[64,64,128]{2,1,0:T(8,128)(2,1)S(1)} %shard_map.100.refs_0_), channel_id=1, source_target_pairs={{2,0},{3,1},{6,4},{7,5},{8,10},{9,11},{12,14},{13,15},{18,16},{19,... | collective-permute-start | bytes 3145736 | tf_op jit(solution)/shard_map/ppermute | solution.py:381
  55.5 20.4 %collective-permute-start.10 = (bf16[64,64,128]{2,1,0:T(8,128)(2,1)S(1)}, bf16[64,64,128]{2,1,0:T(8,128)(2,1)S(1)}, u32[]{:S(2)}, u32[]{:S(2)}) collective-permute-start(bf16[64,64,128]{2,1,0:T(8,128)(2,1)S(1)} %get-tuple-element.64), channel_id=1, source_target_pairs={{5,7},{7,3},{8,12},{10,8},{21,23},{23,19},{24,28},{26,24}} | collective-permute-start | bytes 3145736 | tf_op jit(solution)/shard_map/ppermute | solution.py:381
  56.8 21.6 %collective-permute-start.11 = (bf16[64,64,128]{2,1,0:T(8,128)(2,1)S(1)}, bf16[64,64,128]{2,1,0:T(8,128)(2,1)S(1)}, u32[]{:S(2)}, u32[]{:S(2)}) collective-permute-start(bf16[64,64,128]{2,1,0:T(8,128)(2,1)S(1)} %get-tuple-element.65.refs_6_), channel_id=1, source_target_pairs={{5,3},{10,12},{21,19},{26,28}} | collective-permute-start | bytes 3145736 | tf_op jit(solution)/shard_map/ppermute | solution.py:381

commit v5 on v4

v5 whole, which is shorter than its diff:
```python
import functools

import jax
import jax.numpy as jnp
from jax import lax
from jax.experimental import pallas as pl
from jax.experimental.pallas import tpu as pltpu
from jax.sharding import PartitionSpec as P

EPS = 1e-05
VMEM = pl.BlockSpec(memory_space=pltpu.VMEM)
HBM = pl.BlockSpec(memory_space=pltpu.HBM)
STEP = 16


def place():
    row, col = lax.axis_index("rows"), lax.axis_index("cols")
    whole = col % 2 == row % 2
    early, middle = col // 2 == row // 2, (row == 1) | (row == 2)
    late = jnp.where(whole == middle, 4, jnp.where(middle, 2, 3))
    case = jnp.where(early, jnp.where(whole, 0, 1), late)
    return whole.astype(jnp.int32), ~early, case


def call(body, out_shape, in_specs, out_specs, scratch, limit=12):
    return pl.pallas_call(
        body,
        out_shape=out_shape,
        in_specs=in_specs,
        out_specs=out_specs,
        scratch_shapes=scratch,
        compiler_params=pltpu.CompilerParams(vmem_limit_bytes=limit * 1024 * 1024),
        cost_estimate=pl.CostEstimate(flops=1, bytes_accessed=1, transcendentals=0),
    )


def sigmoid(values):
    return 0.5 * jnp.tanh(0.5 * values) + 0.5


def dot(left, right, dims):
    return lax.dot_general(left, right, (dims, ((), ())), preferred_element_type=jnp.float32)


def split(values):
    high = values.astype(jnp.bfloat16)
    low = (values - high.astype(jnp.float32)).astype(jnp.bfloat16)
    return jnp.concatenate([high, low], axis=1)


def norm_body(pair_ref, mask_ref, gain_ref, shift_ref, out_ref, kept_ref, *scratch):
    held, made, kept, mask, gain_held, shift_held, sems = scratch
    rows, cols, channels = held.shape
    steps = sems.shape[1] - 3
    step = rows // steps
    spans = [pl.ds(at * step, step) for at in range(steps)]
    small = [
        pltpu.make_async_copy(mask_ref, mask, sems.at[0, steps]),
        pltpu.make_async_copy(gain_ref, gain_held, sems.at[0, steps + 1]),
        pltpu.make_async_copy(shift_ref, shift_held, sems.at[0, steps + 2]),
    ]
    loads = [
        pltpu.make_async_copy(pair_ref.at[span], held.at[span], sems.at[0, at])
        for at, span in enumerate(spans)
    ]
    for copy in loads[:1] + small + loads[1:]:
        copy.start()
    ones = jnp.full((2 * channels, channels), 1.0 / channels, jnp.bfloat16)
    for copy in small:
        copy.wait()
    gain, shift = gain_held[...], shift_held[...]
    stores = []
    for at, span in enumerate(spans):
        loads[at].wait()
        values = held[span].reshape(step * cols, channels)
        centered = values - dot(split(values), ones, ((1,), (0,)))
        squares = (centered * centered).astype(jnp.bfloat16)
        spread = dot(squares, ones[:channels], ((1,), (0,)))
        normed = centered * lax.rsqrt(spread + EPS) * gain + shift
        keep = mask[span].astype(jnp.float32).T
        for row in range(step):
            tile = normed[row * cols : (row + 1) * cols] * keep[:, row : row + 1]
            kept[at * step + row] = tile.astype(jnp.bfloat16)
        made[span] = normed.astype(jnp.bfloat16).reshape(step, cols, channels)
        stores += [
            pltpu.make_async_copy(kept.at[span], kept_ref.at[span], sems.at[1, at]),
            pltpu.make_async_copy(made.at[span], out_ref.at[span], sems.at[2, at]),
        ]
        stores[-2].start()
        stores[-1].start()
    for copy in stores:
        copy.wait()


def layer_norm(pair, mask, gain, shift, steps=2):
    half = pltpu.VMEM(pair.shape, jnp.bfloat16)
    return call(
        norm_body,
        [jax.ShapeDtypeStruct(pair.shape, jnp.bfloat16)] * 2,
        [HBM] * 4,
        [HBM] * 2,
        [
            pltpu.VMEM(pair.shape, jnp.float32),
            half,
            half,
            pltpu.VMEM(mask.shape, jnp.int32),
            pltpu.VMEM(gain.shape, jnp.float32),
            pltpu.VMEM(shift.shape, jnp.float32),
            pltpu.SemaphoreType.DMA((3, steps + 3)),
        ],
        limit=58,
    )(pair, mask, gain, shift)


def gate_body(normed_ref, weight_ref, out_ref, held, sems):
    rows, cols, channels = normed_ref.shape
    weight = weight_ref[...]
    copies = []
    for at in range(rows // STEP):
        span = pl.ds(at * STEP, STEP)
        values = dot(normed_ref[span].reshape(STEP * cols, channels), weight, ((1,), (0,)))
        held[span] = sigmoid(values).reshape(STEP, cols, channels)
        copies.append(pltpu.make_async_copy(held.at[span], out_ref.at[span], sems.at[at]))
        copies[-1].start()
    for copy in copies:
        copy.wait()


def output_gate(normed, weight):
    return call(
        gate_body,
        jax.ShapeDtypeStruct(normed.shape, jnp.float32),
        [VMEM, VMEM],
        HBM,
        [
            pltpu.VMEM(normed.shape, jnp.float32),
            pltpu.SemaphoreType.DMA((normed.shape[0] // STEP,)),
        ],
    )(normed, weight)


def side_body(cases, count, weight_ref, *refs):
    tiles, outs, held = refs[:count], refs[count:-1], refs[-1]
    rows, cols, channels = tiles[0].shape
    planes = channels // 2
    steps = rows // STEP
    spans = [pl.ds(at * STEP, STEP) for at in range(steps)]
    zero = jnp.zeros((cols, channels), jnp.bfloat16)

    def project(tile, writes):
        weight = weight_ref[...]
        for at, span in enumerate(spans):
            for row in range(0, STEP, 2):
                parts = []
                for more in range(2):
                    value = tiles[tile][at * STEP + row + more]
                    parts += [jnp.concatenate([value, zero], 1), jnp.concatenate([zero, value], 1)]
                both = dot(weight, jnp.concatenate(parts, axis=0), ((1,), (1,)))
                for more in range(2):
                    values = both[:, 2 * cols * more : 2 * cols * (more + 1)]
                    held[pl.ds(row + more, planes, stride=STEP), :] = (
                        sigmoid(values[planes:]) * values[:planes]
                    )
            for first, out, index in writes:
                out_ref = outs[out] if index is None else outs[out].at[index]
                number = out_ref.shape[0]
                value = held[first * STEP : (first + number) * STEP, :]
                value = value.reshape(number, STEP, 2 * cols)
                out_ref[:, span, :] = value.astype(jnp.bfloat16)

    def work(jobs):
        for tile, writes in jobs:
            project(tile, writes)

    if len(cases) == 1:
        work(cases[0])
    else:
        whole = place()[0]
        for value, jobs in enumerate(cases):
            if jobs:
                pl.when(whole == value)(functools.partial(work, jobs))


def side(cases, shapes, weight, tiles):
    rows, cols, channels = tiles[0].shape
    return call(
        functools.partial(side_body, cases, len(tiles)),
        [jax.ShapeDtypeStruct(shape + (rows, 2 * cols), jnp.bfloat16) for shape in shapes],
        [VMEM] * (1 + len(tiles)),
        [VMEM] * len(shapes),
        [pltpu.VMEM((channels // 2 * STEP, 2 * cols), jnp.float32)],
    )(weight, *tiles)


def paired(tiles):
    low = lax.broadcasted_iota(jnp.int32, tiles[0].shape, 1) < tiles[0].shape[1] // 2
    zero = jnp.zeros(tiles[0].shape, jnp.bfloat16)
    first = jnp.concatenate([jnp.where(low, tile, zero) for tile in tiles], axis=1)
    second = jnp.concatenate([jnp.where(low, zero, tile) for tile in tiles], axis=1)
    return jnp.concatenate([first, second], axis=0)


def triangle_body(cases, *refs):
    left, right, out_ref = refs[:2], refs[2:-1], refs[-1]

    def work(places):
        for plane, place in enumerate(places):
            first = jnp.concatenate([ref[plane] for ref in left], axis=1)
            second = paired([right[at[0]][at[1:]] for at in place])
            value = dot(first, second, ((1,), (1,)))
            out_ref[plane] = value.astype(jnp.bfloat16)

    if len(cases) == 1:
        work(cases[0])
    else:
        whole = place()[0]
        for case, places in enumerate(cases):
            if places:
                pl.when(whole == case)(functools.partial(work, places))


def triangle(cases, left, right):
    planes, rows, lanes = left[0].shape
    return call(
        functools.partial(triangle_body, cases),
        jax.ShapeDtypeStruct((planes, rows, 2 * rows), jnp.bfloat16),
        [VMEM] * (2 + len(right)),
        VMEM,
        [],
    )(*left, *right)


def served_body(start, order, *refs):
    mine, ends, right, outs = refs[:2], refs[2:4], refs[4:-2], refs[-2:]
    right = right if len(right) == 2 else [right[0].at[tile] for tile in order]
    rows = mine[0].shape[1]

    def work(firsts):
        for at in range(outs[0].shape[0]):
            both = [
                jnp.concatenate([ref[start + at] for ref in first], axis=1) for first in firsts
            ]
            second = paired([ref[at] for ref in right])
            value = dot(jnp.concatenate(both, axis=0), second, ((1,), (1,)))
            value = value.astype(jnp.bfloat16)
            outs[0][at] = value[:rows]
            outs[1][at] = value[rows:]

    whole, owner, _ = place()

    @pl.when((whole == 0) & owner)
    def _():
        work([ends, mine])

    @pl.when((whole == 0) & ~owner)
    def _():
        work([mine, ends])


def served(start, order, mine, ends, right):
    count, rows, _ = right[0].shape[-3:]
    return call(
        functools.partial(served_body, start, order),
        [jax.ShapeDtypeStruct((count, rows, 2 * rows), jnp.bfloat16)] * 2,
        [VMEM] * (4 + len(right)),
        [VMEM] * 2,
        [],
    )(*mine, *ends, *right)


def finish_body(cases, *refs):
    parts, (gain_ref, shift_ref, weight_ref, gate_ref, out_ref) = refs[:-10], refs[-10:-5]
    total, held, made, gate, sems = refs[-5:]
    planes, _, lanes = total.shape
    rows = gate.shape[0]
    steps = rows // STEP
    width = lanes // 2
    weight = weight_ref[...]
    spans = [pl.ds(at * STEP, STEP) for at in range(steps)]
    mine = place()[2] if len(cases) > 1 else 0
    loads = [
        pltpu.make_async_copy(gate_ref.at[span], gate.at[span], sems.at[at])
        for at, span in enumerate(spans)
    ]
    for load in loads:
        load.start()

    def mean(values):
        return (values + pltpu.roll(values, width, 1)) * (1.0 / (2 * planes))

    def add(first, second):
        ones = [(index, at) for index in first for at in range(parts[index].shape[0])]
        twos = [(index, at) for index in second for at in range(parts[index].shape[0])]
        for plane in range(planes):
            (one, here), (two, there) = ones[plane], twos[plane]
            value = parts[one][here].astype(jnp.float32)
            total[plane] = value + parts[two][there].astype(jnp.float32)

    for case, terms in enumerate(cases):
        pl.when(mine == case)(functools.partial(add, *terms))

    for at, span in enumerate(spans):
        added = jnp.zeros((STEP, lanes), jnp.float32)
        for plane in range(planes):
            added = added + total[plane, span]
        middle = mean(added)
        added = jnp.zeros((STEP, lanes), jnp.float32)
        for plane in range(planes):
            centered = total[plane, span] - middle
            added = added + centered * centered
        scale = lax.rsqrt(mean(added) + EPS)
        for plane in range(planes):
            normed = (total[plane, span] - middle) * scale * gain_ref[plane] + shift_ref[plane]
            held[pl.ds(plane, STEP, stride=planes), :] = normed
        loads[at].wait()
        for row in range(STEP):
            tile = held[row * planes : (row + 1) * planes, :].T.astype(jnp.bfloat16)
            update = dot(tile[:width], weight[:planes], ((1,), (0,)))
            update += dot(tile[width:], weight[planes:], ((1,), (0,)))
            made[at * STEP + row] = update * gate[at * STEP + row]
        pltpu.make_async_copy(made.at[span], out_ref.at[span], sems.at[steps + at]).start()
    for at, span in enumerate(spans):
        pltpu.make_async_copy(made.at[span], out_ref.at[span], sems.at[steps + at]).wait()


def finish(cases, parts, gain, shift, weight, gate):
    planes, _, lanes = gain.shape
    rows = gate.shape[0]
    return call(
        functools.partial(finish_body, cases),
        jax.ShapeDtypeStruct(gate.shape, jnp.float32),
        [VMEM] * (len(parts) + 3) + [HBM],
        HBM,
        [
            pltpu.VMEM((planes, rows, lanes), jnp.float32),
            pltpu.VMEM((planes * STEP, lanes), jnp.float32),
            pltpu.VMEM(gate.shape, jnp.float32),
            pltpu.VMEM(gate.shape, jnp.float32),
            pltpu.SemaphoreType.DMA((2 * rows // STEP,)),
        ],
    )(*parts, gain, shift, weight, gate)


def planes_of(vector, width):
    return jnp.repeat(vector.reshape(2, -1).T, width, axis=1)[:, None, :]


def arranged(weight):
    channels = weight.shape[0]
    weight = weight.reshape(channels, 2, 2, 2, channels // 2).transpose(1, 2, 4, 3, 0)
    return weight.reshape(2, channels, 2 * channels)


def per_device(
    mesh_rows,
    mesh_cols,
    pair,
    pair_mask,
    in_gain,
    in_bias,
    proj_weight,
    gate_weight,
    out_gain,
    out_bias,
    out_weight,
):
    rows, cols, channels = pair.shape
    planes = channels // 2
    gain, shift = planes_of(out_gain, cols), planes_of(out_bias, cols)

    if mesh_rows == 4 and mesh_cols == 4:
        both = ("rows", "cols")
        at = lambda z, x, h: z * 4 + 2 * x + h
        places = [(z, x, h) for z in range(4) for x in range(2) for h in range(2)]
        flip = [(at(z, x, h), at(z, x, 1 - h)) for z, x, h in places]
        wholes = [place for place in places if place[2] == place[0] % 2]
        others = [place for place in places if place[2] != place[0] % 2]
        middles = lambda some: [place for place in some if place[0] in (1, 2)]
        partners = [(at(z, x, h), at(z ^ 1, x, h)) for z, x, h in wholes]
        across = [(at(z, x, h), at(3 - z, x, 1 - h)) for z, x, h in middles(others)]
        two_hops = [(at(z, x, h), at(2 - z // 3, x, 1 - h)) for z, x, h in wholes if z in (0, 3)]
        owner = lambda z: 1 - z // 2
        early_pairs = lambda some: [
            (at(z, x, h), at(z, 1 - x, h)) for z, x, h in some if x == owner(z)
        ]
        first_pairs = lambda flipped: [
            (at(z, x, h), at(z ^ 1, x, h ^ flipped) if x == owner(z) else at(z, 1 - x, h ^ flipped))
            for z, x, h in middles(others)
        ]
        second_pairs = lambda flipped: [
            (at(z, x, h), at(z ^ 1, 1 - x, h ^ flipped))
            for z, x, h in middles(others)
            if x != owner(z)
        ]
        beside = [(at(z, x, h), at(z, x, 1 - h)) for z, x, h in middles(others) if x == owner(z)]
        move = lambda array, pairs: lax.ppermute(array, both, pairs)
        tie = lax.optimization_barrier
        cut = 3 * planes // 4
        full = [(0, [(0, 0, None)])]
        cut_tiles = [(tile, [(0, 0, tile), (cut, 1, tile)]) for tile in (0, 1)]
        plain = [[(0, plane), (1, plane)] for plane in range(planes)]
        cut_plain = [
            [(plane // cut, tile, plane % cut) for tile in (0, 1)] for plane in range(planes)
        ]
        one_side = lambda column, cases, tile: side(cases, [(planes,)], weights[column], [tile])[0]

        normed, kept = layer_norm(pair, pair_mask, in_gain[None], in_bias[None])
        kept_other = move(kept, flip)
        partner = move(kept, partners)
        near_other = move(kept, across)
        partner_other = move(kept_other, partners)
        near = move(kept_other, across)
        kept, proj_weight = tie((kept, proj_weight))
        weights = arranged(proj_weight)
        b_own = side(
            [[], cut_tiles], [(2, cut), (2, planes - cut)], weights[1], [kept, kept_other]
        )
        kept, b_own = tie((kept, b_own))
        a_own = one_side(0, [full], kept)
        a_other = one_side(0, [full], kept_other)
        mine = [a_own, a_other]
        own = triangle([[], cut_plain], mine, b_own)
        gate = output_gate(normed, gate_weight)
        partner, mine, own, gate, gain, shift = tie((partner, mine, own, gate, gain, shift))
        near_other, partner = tie((near_other, partner))
        a_end = one_side(0, [full, []], partner)
        b_near_other = one_side(1, [full, []], near_other)
        partner_other, a_end, b_near_other = tie((partner_other, a_end, b_near_other))
        near, partner_other, own, b_own = tie((near, partner_other, own, b_own))
        far = [move(part, two_hops) for part in b_own]
        own_other = move(own, early_pairs(wholes))
        a_end_other = one_side(0, [full, []], partner_other)
        b_near = one_side(1, [full, []], near)
        ends = [a_end, a_end_other]
        one, two = served(0, None, mine, ends, [b_near, b_near_other])
        near = [move(one, first_pairs(0)), two, move(two, second_pairs(0))]
        partner, partner_other, one, own_other = tie((partner, partner_other, one, own_other))
        b_partner = one_side(1, [full, []], partner)
        b_partner_other = one_side(1, [full, []], partner_other)
        partner = triangle([plain, []], mine, [b_partner, b_partner_other])
        partner_sent = move(partner, early_pairs(others))
        ends, partner = tie((ends, partner))
        one, two = served(0, (1, 0), mine, ends, far[:1])
        late = [move(one, first_pairs(1)), move(two, second_pairs(1) + beside)]
        ends, one, near = tie((ends, one, near))
        one, two = served(cut, (1, 0), mine, ends, far[1:])
        last = [move(one, first_pairs(1)), move(two, second_pairs(1) + beside)]
        late, partner_sent, gain, shift = tie((late, partner_sent, gain, shift))
        parts = [own, own_other, partner, partner_sent] + near + late + last
        cases = [([0], [1]), ([2], [3]), ([4], [5]), ([4], [6]), ([7, 9], [8, 10])]
    else:
        normed, kept = layer_norm(pair, pair_mask, in_gain[None], in_bias[None])
        quarters = [[(0, [(planes // 4 * at, at, None) for at in range(4)])]]
        shapes = [(planes // 4,)] * 4
        weights = arranged(proj_weight)
        pieces = side(quarters, shapes, weights[1], [kept])
        lefts = side(quarters, shapes, weights[0], [kept])
        gate = output_gate(normed, gate_weight)
        places = [[[(0, plane), (1, plane)] for plane in range(planes // 4)]]
        sums = []
        for piece, left in zip(pieces, lefts):
            gathered = lax.all_gather(piece, "rows")
            zero = jnp.zeros_like(left)
            product = jnp.stack(
                [
                    triangle(places, [left, zero], [gathered[at], zero])
                    for at in range(mesh_rows)
                ]
            )
            gathered = lax.all_to_all(product, "cols", 0, 0, tiled=True)
            sums.append(jnp.sum(gathered.astype(jnp.float32), axis=0))
        total = jnp.concatenate(sums, axis=0)
        parts, cases = [total, jnp.zeros_like(total)], [([0], [1])]
    return finish(cases, parts, gain, shift, out_weight, gate)


def solution(mesh):
    tile = P(("groups", "rows"), "cols", None)
    return jax.shard_map(
        functools.partial(per_device, mesh.shape["rows"], mesh.shape["cols"]),
        mesh=mesh,
        in_specs=(tile, P(("groups", "rows"), "cols")) + (P(),) * 7,
        out_specs=tile,
        check_vma=False,
    )
```

time: 85.5 us -> 80.8 us (0.945)
  waiting for transfers between devices: 32.5 us -> 22.5 us
  Pallas kernels: 32.4 us -> 35.8 us
  starting transfers between devices: 15.1 us -> 17.6 us
    ppermute x12 -> x15, waiting for transfers between devices: 32.5 us -> 22.5 us  [per_device(): move = lambda array, pairs: lax.ppermute(array, both, pairs)]
    pallas_call x8 -> x12, Pallas kernels: 19.1 us -> 24.2 us  [the longest x9 21.3 us: side(): call(functools.partial(side_body, cases, len(tiles)), [jax.ShapeDtypeStru...]
    ppermute x12 -> x15, starting transfers between devices: 15.1 us -> 17.6 us  [per_device(): move = lambda array, pairs: lax.ppermute(array, both, pairs)]
    pallas_call x1 -> x2, Pallas kernels: 1.81 us -> 1.6 us  [triangle(): call(functools.partial(triangle_body, cases), jax.ShapeDtypeStruct((plane...]
  transfers between devices with their start and end apart: 12 -> 15, of which waited for: 5 -> 6; matrix products, arithmetic and copies ran while one was open for 1% -> 1% of each run, Pallas kernels for 26% -> 34%
where the time goes in v5:
time: 80.8 us; the launch traced here: 80.1 us
  Pallas kernels  35.8 us (44%)
  waiting for transfers between devices  22.5 us (28%)
  starting transfers between devices  17.6 us (22%)
  local copies, waits for them, and re-layouts  3.59 us (4%)
    ppermute x15, waiting for transfers between devices, per_device(): move = lambda array, pairs: lax.ppermute(array, both, pairs)  22.5 us
    pallas_call x9, Pallas kernels, side(): call(functools.partial(side_body, cases, len(tiles)), [jax.ShapeDtypeStru...  21.3 us
    ppermute x15, starting transfers between devices, per_device(): move = lambda array, pairs: lax.ppermute(array, both, pairs)  17.6 us
    pallas_call x1, Pallas kernels, finish(): call(functools.partial(finish_body, cases), jax.ShapeDtypeStruct(gate.sha...  4.62 us
    pallas_call x1, Pallas kernels, layer_norm(): call(norm_body, [jax.ShapeDtypeStruct(pair.shape, jnp.bfloat16)] * 2, [HB...  4.02 us
    pallas_call x3, Pallas kernels, served(): call(functools.partial(served_body, start, order), [jax.ShapeDtypeStruct(...  2.98 us
    unnamed x16, local copies, waits for them, and re-layouts  2.49 us
  transfers between devices with their start and end apart: 15, of which 6 were waited for; matrix products, arithmetic and copies ran while one was open for 1% of the time, Pallas kernels for 34%

profile of v5, /device:TPU:7, one launch (start us, length us, event | category | flops | bytes accessed | tf_op | source)
XLA Modules:
  0.0 80.1 jit_solution(12129217909101341878)
XLA Ops:
  0.0 4.0 %shard_map.91 = (bf16[64,64,128]{2,1,0:T(8,128)(2,1)}, bf16[64,64,128]{2,1,0:T(8,128)(2,1)}) custom-call(f32[64,64,128]{2,1,0:T(8,128)} %pair_ref.1, s32[64,64]{1,0:T(8,128)} %mask_ref.1, f32[1,128]{1,0:T(1,128)} %bitcast.31, f32[1,128]{1,0:T(1,128)} %bitcast.32), custom_call_target="tpu_custom_call" | custom-call | flops 1 | bytes 1 | tf_op jit(solution)/shard_map/pallas_call | solution.py:97
  6.1 1.7 %collective-permute-start.3 = (bf16[64,64,128]{2,1,0:T(8,128)(2,1)}, bf16[64,64,128]{2,1,0:T(8,128)(2,1)}, u32[]{:S(2)}, u32[]{:S(2)}) collective-permute-start(bf16[64,64,128]{2,1,0:T(8,128)(2,1)} %get-tuple-element.58.refs_0_), channel_id=1, source_target_pairs={{4,9},{6,11},{9,4},{11,6},{20,25},{22,27},{25,20},{27,22}} | collective-permute-start | bytes 3145736 | tf_op jit(solution)/shard_map/ppermute | solution.py:396
  9.0 1.6 %collective-permute-start.1 = (bf16[64,64,128]{2,1,0:T(8,128)(2,1)}, bf16[64,64,128]{2,1,0:T(8,128)(2,1)}, u32[]{:S(2)}, u32[]{:S(2)}) collective-permute-start(bf16[64,64,128]{2,1,0:T(8,128)(2,1)} %collective-permute-done.refs_1_.refs_0_), channel_id=1, source_target_pairs={{4,9},{6,11},{9,4},{11,6},{20,25},{22,27},{25,20},{27,22}} | collective-permute-start | bytes 3145736 | tf_op jit(solution)/shard_map/ppermute | solution.py:396
  11.9 1.3 %shard_map.96.refs_14_ = f32[64,64,128]{2,1,0:T(8,128)S(1)} custom-call(bf16[64,64,128]{2,1,0:T(8,128)(2,1)S(1)} %copy-done.1, bf16[128,128]{1,0:T(8,128)(2,1)S(1)} %copy-done.2), custom_call_target="tpu_custom_call" | custom-call | flops 1 | bytes 1 | tf_op jit(solution)/shard_map/pallas_call | solution.py:130
  16.9 1.7 %shard_map.93.refs_0_ = bf16[64,64,128]{2,1,0:T(8,128)(2,1)S(1)} custom-call(bf16[128,256]{1,0:T(8,128)(2,1)S(1)} %bitcast.22, bf16[64,64,128]{2,1,0:T(8,128)(2,1)S(1)} %copy-done), custom_call_target="tpu_custom_call" | custom-call | flops 1 | bytes 1 | tf_op jit(solution)/shard_map/pallas_call | solution.py:186
  18.6 2.9 %shard_map.94.refs_1_ = bf16[64,64,128]{2,1,0:T(8,128)(2,1)S(1)} custom-call(bf16[128,256]{1,0:T(8,128)(2,1)S(1)} %bitcast.23, bf16[64,64,128]{2,1,0:T(8,128)(2,1)} %collective-permute-done.refs_1_.refs_0_), custom_call_target="tpu_custom_call" | custom-call | flops 1 | bytes 1 | tf_op jit(solution)/shard_map/pallas_call | solution.py:186
  21.6 2.9 %shard_map.98.refs_5_ = bf16[64,64,128]{2,1,0:T(8,128)(2,1)S(1)} custom-call(bf16[128,256]{1,0:T(8,128)(2,1)S(1)} %bitcast.18, bf16[64,64,128]{2,1,0:T(8,128)(2,1)} %collective-permute-done.3.refs_0_), custom_call_target="tpu_custom_call" | custom-call | flops 1 | bytes 1 | tf_op jit(solution)/shard_map/pallas_call | solution.py:186
  24.5 1.9 %shard_map.97.refs_2_ = bf16[64,64,128]{2,1,0:T(8,128)(2,1)S(1)} custom-call(bf16[128,256]{1,0:T(8,128)(2,1)S(1)} %bitcast.24, bf16[64,64,128]{2,1,0:T(8,128)(2,1)S(1)} %collective-permute-done.4.refs_0_), custom_call_target="tpu_custom_call" | custom-call | flops 1 | bytes 1 | tf_op jit(solution)/shard_map/pallas_call | solution.py:186
  26.4 5.4 %collective-permute-done.2.refs_0_ = bf16[64,64,128]{2,1,0:T(8,128)(2,1)} collective-permute-done((bf16[64,64,128]{2,1,0:T(8,128)(2,1)}, bf16[64,64,128]{2,1,0:T(8,128)(2,1)}, u32[]{:S(2)}, u32[]{:S(2)}) %collective-permute-start.2) | collective-permute-done | bytes 1048608 | tf_op jit(solution)/shard_map/ppermute | solution.py:396
  33.4 2.9 %shard_map.100.refs_4_ = bf16[64,64,128]{2,1,0:T(8,128)(2,1)S(1)} custom-call(bf16[128,256]{1,0:T(8,128)(2,1)S(1)} %bitcast.19, bf16[64,64,128]{2,1,0:T(8,128)(2,1)} %collective-permute-done.1.refs_0_), custom_call_target="tpu_custom_call" | custom-call | flops 1 | bytes 1 | tf_op jit(solution)/shard_map/pallas_call | solution.py:186
  36.3 2.9 %shard_map.99.refs_3_ = bf16[64,64,128]{2,1,0:T(8,128)(2,1)S(1)} custom-call(bf16[128,256]{1,0:T(8,128)(2,1)S(1)} %bitcast.25, bf16[64,64,128]{2,1,0:T(8,128)(2,1)} %collective-permute-done.2.refs_0_), custom_call_target="tpu_custom_call" | custom-call | flops 1 | bytes 1 | tf_op jit(solution)/shard_map/pallas_call | solution.py:186
  39.3 1.3 %shard_map.101 = (bf16[64,64,128]{2,1,0:T(8,128)(2,1)S(1)}, bf16[64,64,128]{2,1,0:T(8,128)(2,1)S(1)}) custom-call(bf16[64,64,128]{2,1,0:T(8,128)(2,1)S(1)} %shard_map.93.refs_0_, bf16[64,64,128]{2,1,0:T(8,128)(2,1)S(1)} %shard_map.94.refs_1_, bf16[64,64,128]{2,1,0:T(8,128)(2,1)S(1)} %shard_map.97.refs_2_, bf16[64,64,128]{2,1,0:T(8,128)(2,1)S(1)} %shard_map.99.refs_3_, ...), custom_call_target="tpu_custom_call" | custom-call | flops 1 | bytes 1 | tf_op jit(solution)/shard_map/pallas_call | solution.py:262
  42.0 2.9 %shard_map.103.refs_3_ = bf16[64,64,128]{2,1,0:T(8,128)(2,1)S(1)} custom-call(bf16[128,256]{1,0:T(8,128)(2,1)S(1)} %bitcast.20, bf16[64,64,128]{2,1,0:T(8,128)(2,1)} %collective-permute-done.2.refs_0_), custom_call_target="tpu_custom_call" | custom-call | flops 1 | bytes 1 | tf_op jit(solution)/shard_map/pallas_call | solution.py:186
  45.0 1.7 %shard_map.102.refs_2_ = bf16[64,64,128]{2,1,0:T(8,128)(2,1)S(1)} custom-call(bf16[128,256]{1,0:T(8,128)(2,1)S(1)} %bitcast.21, bf16[64,64,128]{2,1,0:T(8,128)(2,1)S(1)} %collective-permute-done.4.refs_0_), custom_call_target="tpu_custom_call" | custom-call | flops 1 | bytes 1 | tf_op jit(solution)/shard_map/pallas_call | solution.py:186
  46.7 1.6 %shard_map.104.refs_2_ = bf16[64,64,128]{2,1,0:T(8,128)(2,1)S(1)} custom-call(bf16[64,64,128]{2,1,0:T(8,128)(2,1)S(1)} %shard_map.93.refs_0_, bf16[64,64,128]{2,1,0:T(8,128)(2,1)S(1)} %shard_map.94.refs_1_, bf16[64,64,128]{2,1,0:T(8,128)(2,1)S(1)} %shard_map.102.refs_2_, bf16[64,64,128]{2,1,0:T(8,128)(2,1)S(1)} %shard_map.103.refs_3_), custom_call_target="tpu_custom_call" | custom-call | flops 1 | bytes 1 | tf_op jit(solution)/shard_map/pallas_call | solution.py:224
  48.3 2.2 %collective-permute-start.9 = (bf16[64,64,128]{2,1,0:T(8,128)(2,1)S(1)}, bf16[64,64,128]{2,1,0:T(8,128)(2,1)S(1)}, u32[]{:S(2)}, u32[]{:S(2)}) collective-permute-start(bf16[64,64,128]{2,1,0:T(8,128)(2,1)S(1)} %shard_map.104.refs_2_), channel_id=1, source_target_pairs={{3,1},{6,4},{9,11},{12,14},{19,17},{22,20},{25,27},{28,30}} | collective-permute-start | bytes 3145736 | tf_op jit(solution)/shard_map/ppermute | solution.py:396
  52.5 1.3 %collective-permute-start.7 = (bf16[48,64,128]{2,1,0:T(8,128)(2,1)S(1)}, bf16[48,64,128]{2,1,0:T(8,128)(2,1)S(1)}, u32[]{:S(2)}, u32[]{:S(2)}) collective-permute-start(bf16[48,64,128]{2,1,0:T(8,128)(2,1)S(1)} %get-tuple-element.82), channel_id=1, source_target_pairs={{4,7},{6,3},{9,12},{11,8},{20,23},{22,19},{25,28},{27,24}} | collective-permute-start | bytes 2359304 | tf_op jit(solution)/shard_map/ppermute | solution.py:396
  53.8 1.3 %collective-permute-start.8 = (bf16[48,64,128]{2,1,0:T(8,128)(2,1)S(1)}, bf16[48,64,128]{2,1,0:T(8,128)(2,1)S(1)}, u32[]{:S(2)}, u32[]{:S(2)}) collective-permute-start(bf16[48,64,128]{2,1,0:T(8,128)(2,1)S(1)} %get-tuple-element.83), channel_id=1, source_target_pairs={{4,3},{11,12},{6,7},{9,8},{20,19},{27,28},{22,23},{25,24}} | collective-permute-start | bytes 2359304 | tf_op jit(solution)/shard_map/ppermute | solution.py:396
  55.6 1.3 %collective-permute-start.13 = (bf16[16,64,128]{2,1,0:T(8,128)(2,1)S(1)}, bf16[16,64,128]{2,1,0:T(8,128)(2,1)S(1)}, u32[]{:S(2)}, u32[]{:S(2)}) collective-permute-start(bf16[16,64,128]{2,1,0:T(8,128)(2,1)S(1)} %get-tuple-element.96), channel_id=1, source_target_pairs={{4,7},{6,3},{9,12},{11,8},{20,23},{22,19},{25,28},{27,24}} | collective-permute-start | bytes 786440 | tf_op jit(solution)/shard_map/ppermute | solution.py:396
  56.9 1.3 %collective-permute-start.14 = (bf16[16,64,128]{2,1,0:T(8,128)(2,1)S(1)}, bf16[16,64,128]{2,1,0:T(8,128)(2,1)S(1)}, u32[]{:S(2)}, u32[]{:S(2)}) collective-permute-start(bf16[16,64,128]{2,1,0:T(8,128)(2,1)S(1)} %get-tuple-element.97), channel_id=1, source_target_pairs={{4,3},{11,12},{6,7},{9,8},{20,19},{27,28},{22,23},{25,24}} | collective-permute-start | bytes 786440 | tf_op jit(solution)/shard_map/ppermute | solution.py:396
  58.2 5.8 %collective-permute-done.9.refs_3_ = bf16[64,64,128]{2,1,0:T(8,128)(2,1)S(1)} collective-permute-done((bf16[64,64,128]{2,1,0:T(8,128)(2,1)S(1)}, bf16[64,64,128]{2,1,0:T(8,128)(2,1)S(1)}, u32[]{:S(2)}, u32[]{:S(2)}) %collective-permute-start.9) | collective-permute-done | bytes 1048608 | tf_op jit(solution)/shard_map/ppermute | solution.py:396
  64.0 7.5 %collective-permute-done.7.refs_7_ = bf16[48,64,128]{2,1,0:T(8,128)(2,1)S(1)} collective-permute-done((bf16[48,64,128]{2,1,0:T(8,128)(2,1)S(1)}, bf16[48,64,128]{2,1,0:T(8,128)(2,1)S(1)}, u32[]{:S(2)}, u32[]{:S(2)}) %collective-permute-start.7) | collective-permute-done | bytes 786464 | tf_op jit(solution)/shard_map/ppermute | solution.py:396
  71.7 3.6 %collective-permute-done.13.refs_9_ = bf16[16,64,128]{2,1,0:T(8,128)(2,1)S(1)} collective-permute-done((bf16[16,64,128]{2,1,0:T(8,128)(2,1)S(1)}, bf16[16,64,128]{2,1,0:T(8,128)(2,1)S(1)}, u32[]{:S(2)}, u32[]{:S(2)}) %collective-permute-start.13) | collective-permute-done | bytes 262176 | tf_op jit(solution)/shard_map/ppermute | solution.py:396
  75.3 4.6 %shard_map.107 = f32[64,64,128]{2,1,0:T(8,128)} custom-call(bf16[64,64,128]{2,1,0:T(8,128)(2,1)S(1)} %shard_map.95.refs_0_, bf16[64,64,128]{2,1,0:T(8,128)(2,1)S(1)} %collective-permute-done.5.refs_1_, bf16[64,64,128]{2,1,0:T(8,128)(2,1)S(1)} %shard_map.104.refs_2_, bf16[64,64,128]{2,1,0:T(8,128)(2,1)S(1)} %collective-permute-done.9.refs_3_, ...), custom_call_target="tpu_custom_call" | custom-call | flops 1 | bytes 1 | tf_op jit(solution)/shard_map/pallas_call | solution.py:329
  (51 shorter events, 13.7 us)
Async XLA Ops:
  0.0 10.7 %copy-start.2 = (bf16[128,128]{1,0:T(8,128)(2,1)S(1)}, bf16[128,128]{1,0:T(8,128)(2,1)}, u32[]{:S(2)}) copy-start(bf16[128,128]{1,0:T(8,128)(2,1)} %weight_ref.1) | copy-start | bytes 98308
  0.0 13.2 %copy-start.4 = (bf16[128,512]{1,0:T(8,128)(2,1)S(1)}, bf16[128,512]{1,0:T(8,128)(2,1)}, u32[]{:S(2)}) copy-start(bf16[128,512]{1,0:T(8,128)(2,1)} %param.13) | copy-start | bytes 393220
  4.0 3.7 %collective-permute-start = (bf16[64,64,128]{2,1,0:T(8,128)(2,1)}, bf16[64,64,128]{2,1,0:T(8,128)(2,1)}, u32[]{:S(2)}, u32[]{:S(2)}) collective-permute-start(bf16[64,64,128]{2,1,0:T(8,128)(2,1)} %get-tuple-element.58.refs_0_), channel_id=1, source_target_pairs={{0,1},{1,0},{2,3},{3,2},{4,5},{5,4},{6,7},{7,6},{8,9},{9,8},{10,11... | collective-permute-start | bytes 3145736 | tf_op jit(solution)/shard_map/ppermute | solution.py:396
  4.8 16.8 %collective-permute-start.4 = (bf16[64,64,128]{2,1,0:T(8,128)(2,1)}, bf16[64,64,128]{2,1,0:T(8,128)(2,1)S(1)}, u32[]{:S(2)}, u32[]{:S(2)}) collective-permute-start(bf16[64,64,128]{2,1,0:T(8,128)(2,1)} %get-tuple-element.58.refs_0_), channel_id=1, source_target_pairs={{0,4},{2,6},{5,1},{7,3},{8,12},{10,14},{13,9},{15,11},{16,20},{18,... | collective-permute-start | bytes 3145736 | tf_op jit(solution)/shard_map/ppermute | solution.py:396
  6.1 15.5 %collective-permute-start.3 = (bf16[64,64,128]{2,1,0:T(8,128)(2,1)}, bf16[64,64,128]{2,1,0:T(8,128)(2,1)}, u32[]{:S(2)}, u32[]{:S(2)}) collective-permute-start(bf16[64,64,128]{2,1,0:T(8,128)(2,1)} %get-tuple-element.58.refs_0_), channel_id=1, source_target_pairs={{4,9},{6,11},{9,4},{11,6},{20,25},{22,27},{25,20},{27,22}} | collective-permute-start | bytes 3145736 | tf_op jit(solution)/shard_map/ppermute | solution.py:396
  7.7 24.1 %collective-permute-start.2 = (bf16[64,64,128]{2,1,0:T(8,128)(2,1)}, bf16[64,64,128]{2,1,0:T(8,128)(2,1)}, u32[]{:S(2)}, u32[]{:S(2)}) collective-permute-start(bf16[64,64,128]{2,1,0:T(8,128)(2,1)} %collective-permute-done.refs_1_.refs_0_), channel_id=1, source_target_pairs={{0,4},{2,6},{5,1},{7,3},{8,12},{10,14},{13,9},{15,11},{16,20},{18,... | collective-permute-start | bytes 3145736 | tf_op jit(solution)/shard_map/ppermute | solution.py:396
  9.0 22.8 %collective-permute-start.1 = (bf16[64,64,128]{2,1,0:T(8,128)(2,1)}, bf16[64,64,128]{2,1,0:T(8,128)(2,1)}, u32[]{:S(2)}, u32[]{:S(2)}) collective-permute-start(bf16[64,64,128]{2,1,0:T(8,128)(2,1)} %collective-permute-done.refs_1_.refs_0_), channel_id=1, source_target_pairs={{4,9},{6,11},{9,4},{11,6},{20,25},{22,27},{25,20},{27,22}} | collective-permute-start | bytes 3145736 | tf_op jit(solution)/shard_map/ppermute | solution.py:396
  10.7 1.2 %copy-start.1 = (bf16[64,64,128]{2,1,0:T(8,128)(2,1)S(1)}, bf16[64,64,128]{2,1,0:T(8,128)(2,1)}, u32[]{:S(2)}) copy-start(bf16[64,64,128]{2,1,0:T(8,128)(2,1)} %get-tuple-element.61.normed_ref) | copy-start | bytes 3145732
  11.9 1.6 %copy-start.5 = (f32[128]{0:T(128)S(1)}, f32[128]{0:T(128)}, u32[]{:S(2)}) copy-start(f32[128]{0:T(128)} %param.15) | copy-start | bytes 1540
  11.9 2.1 %copy-start.6 = (f32[128]{0:T(128)S(1)}, f32[128]{0:T(128)}, u32[]{:S(2)}) copy-start(f32[128]{0:T(128)} %param.16) | copy-start | bytes 1540
  14.4 1.2 %copy-start = (bf16[64,64,128]{2,1,0:T(8,128)(2,1)S(1)}, bf16[64,64,128]{2,1,0:T(8,128)(2,1)}, u32[]{:S(2)}) copy-start(bf16[64,64,128]{2,1,0:T(8,128)(2,1)} %get-tuple-element.58.refs_0_) | copy-start | bytes 3145732
  31.9 19.4 %collective-permute-start.6 = (bf16[2,48,64,128]{3,2,1,0:T(8,128)(2,1)S(1)}, bf16[2,48,64,128]{3,2,1,0:T(8,128)(2,1)S(1)}, u32[]{:S(2)}, u32[]{:S(2)}) collective-permute-start(bf16[2,48,64,128]{3,2,1,0:T(8,128)(2,1)S(1)} %get-tuple-element.81.refs_2_), channel_id=1, source_target_pairs={{0,9},{2,11},{13,4},{15,6},{16,25},{18,27},{29,20},{31,22}} | collective-permute-start | bytes 4718600 | tf_op jit(solution)/shard_map/ppermute | solution.py:396
  32.6 9.4 %collective-permute-start.5 = (bf16[64,64,128]{2,1,0:T(8,128)(2,1)S(1)}, bf16[64,64,128]{2,1,0:T(8,128)(2,1)S(1)}, u32[]{:S(2)}, u32[]{:S(2)}) collective-permute-start(bf16[64,64,128]{2,1,0:T(8,128)(2,1)S(1)} %shard_map.95.refs_0_), channel_id=1, source_target_pairs={{2,0},{7,5},{8,10},{13,15},{18,16},{23,21},{24,26},{29,31}} | collective-permute-start | bytes 3145736 | tf_op jit(solution)/shard_map/ppermute | solution.py:396
  40.5 13.3 %collective-permute-start.10 = (bf16[64,64,128]{2,1,0:T(8,128)(2,1)S(1)}, bf16[64,64,128]{2,1,0:T(8,128)(2,1)S(1)}, u32[]{:S(2)}, u32[]{:S(2)}) collective-permute-start(bf16[64,64,128]{2,1,0:T(8,128)(2,1)S(1)} %get-tuple-element.74), channel_id=1, source_target_pairs={{4,6},{6,2},{9,13},{11,9},{20,22},{22,18},{25,29},{27,25}} | collective-permute-start | bytes 3145736 | tf_op jit(solution)/shard_map/ppermute | solution.py:396
  41.3 13.8 %collective-permute-start.11 = (bf16[64,64,128]{2,1,0:T(8,128)(2,1)S(1)}, bf16[64,64,128]{2,1,0:T(8,128)(2,1)S(1)}, u32[]{:S(2)}, u32[]{:S(2)}) collective-permute-start(bf16[64,64,128]{2,1,0:T(8,128)(2,1)S(1)} %get-tuple-element.89.refs_5_), channel_id=1, source_target_pairs={{4,2},{11,13},{20,18},{27,29}} | collective-permute-start | bytes 3145736 | tf_op jit(solution)/shard_map/ppermute | solution.py:396
  48.3 15.7 %collective-permute-start.9 = (bf16[64,64,128]{2,1,0:T(8,128)(2,1)S(1)}, bf16[64,64,128]{2,1,0:T(8,128)(2,1)S(1)}, u32[]{:S(2)}, u32[]{:S(2)}) collective-permute-start(bf16[64,64,128]{2,1,0:T(8,128)(2,1)S(1)} %shard_map.104.refs_2_), channel_id=1, source_target_pairs={{3,1},{6,4},{9,11},{12,14},{19,17},{22,20},{25,27},{28,30}} | collective-permute-start | bytes 3145736 | tf_op jit(solution)/shard_map/ppermute | solution.py:396
  50.5 4.6 %collective-permute-start.12 = (bf16[2,16,64,128]{3,2,1,0:T(8,128)(2,1)S(1)}, bf16[2,16,64,128]{3,2,1,0:T(8,128)(2,1)S(1)}, u32[]{:S(2)}, u32[]{:S(2)}) collective-permute-start(bf16[2,16,64,128]{3,2,1,0:T(8,128)(2,1)S(1)} %get-tuple-element.95.refs_3_), channel_id=1, source_target_pairs={{0,9},{2,11},{13,4},{15,6},{16,25},{18,27},{29,20},{31,22}} | collective-permute-start | bytes 1572872 | tf_op jit(solution)/shard_map/ppermute | solution.py:396
  52.5 19.0 %collective-permute-start.7 = (bf16[48,64,128]{2,1,0:T(8,128)(2,1)S(1)}, bf16[48,64,128]{2,1,0:T(8,128)(2,1)S(1)}, u32[]{:S(2)}, u32[]{:S(2)}) collective-permute-start(bf16[48,64,128]{2,1,0:T(8,128)(2,1)S(1)} %get-tuple-element.82), channel_id=1, source_target_pairs={{4,7},{6,3},{9,12},{11,8},{20,23},{22,19},{25,28},{27,24}} | collective-permute-start | bytes 2359304 | tf_op jit(solution)/shard_map/ppermute | solution.py:396
  53.8 21.5 %copy-start.3 = (bf16[128,128]{1,0:T(8,128)(2,1)S(1)}, bf16[128,128]{1,0:T(8,128)(2,1)}, u32[]{:S(2)}) copy-start(bf16[128,128]{1,0:T(8,128)(2,1)} %refs_13_.1) | copy-start | bytes 98308
  53.8 17.8 %collective-permute-start.8 = (bf16[48,64,128]{2,1,0:T(8,128)(2,1)S(1)}, bf16[48,64,128]{2,1,0:T(8,128)(2,1)S(1)}, u32[]{:S(2)}, u32[]{:S(2)}) collective-permute-start(bf16[48,64,128]{2,1,0:T(8,128)(2,1)S(1)} %get-tuple-element.83), channel_id=1, source_target_pairs={{4,3},{11,12},{6,7},{9,8},{20,19},{27,28},{22,23},{25,24}} | collective-permute-start | bytes 2359304 | tf_op jit(solution)/shard_map/ppermute | solution.py:396
  55.6 19.6 %collective-permute-start.13 = (bf16[16,64,128]{2,1,0:T(8,128)(2,1)S(1)}, bf16[16,64,128]{2,1,0:T(8,128)(2,1)S(1)}, u32[]{:S(2)}, u32[]{:S(2)}) collective-permute-start(bf16[16,64,128]{2,1,0:T(8,128)(2,1)S(1)} %get-tuple-element.96), channel_id=1, source_target_pairs={{4,7},{6,3},{9,12},{11,8},{20,23},{22,19},{25,28},{27,24}} | collective-permute-start | bytes 786440 | tf_op jit(solution)/shard_map/ppermute | solution.py:396
  56.9 18.4 %collective-permute-start.14 = (bf16[16,64,128]{2,1,0:T(8,128)(2,1)S(1)}, bf16[16,64,128]{2,1,0:T(8,128)(2,1)S(1)}, u32[]{:S(2)}, u32[]{:S(2)}) collective-permute-start(bf16[16,64,128]{2,1,0:T(8,128)(2,1)S(1)} %get-tuple-element.97), channel_id=1, source_target_pairs={{4,3},{11,12},{6,7},{9,8},{20,19},{27,28},{22,23},{25,24}} | collective-permute-start | bytes 786440 | tf_op jit(solution)/shard_map/ppermute | solution.py:396
